TPU v7x, 32 devices: a whole 2x2x4 slice. The times are simulated.
32 devices in a mesh: grp: 2 (over y), snap: 4 (over z), clus: 4 (over x, core).
Axes of the slice: x: 2, y: 2, z: 4, core: 2. Of those that a mesh axis runs over, the one named last changes fastest.
Arguments:
- features: bfloat16 [16, 8192, 256], P(('grp', 'snap'), 'clus'), parts along dimension 0, may hold values from -6 to 6
- adj_tiles: bfloat16 [16, 64, 4, 128, 128], P(('grp', 'snap'), 'clus'), parts along dimension 0, may hold values from -0.25 to 0.25
- neighbors: int32 [16, 64, 4], P(('grp', 'snap')), parts along dimension 0, may hold values from 0 to 63, as said below
- w_struct: bfloat16 [256, 256], replicated, may hold values from -0.375 to 0.375
- pos_embed: bfloat16 [8, 256], replicated, may hold values from -3 to 3
- w_query: bfloat16 [256, 256], replicated, may hold values from -9 to 9
- w_key: bfloat16 [256, 256], replicated, may hold values from -9 to 9
- w_value: bfloat16 [256, 256], replicated, may hold values from -0.375 to 0.375
- w_out: bfloat16 [256, 256], replicated, may hold values from -0.375 to 0.375
- w_up: bfloat16 [256, 1024], replicated, may hold values from -0.375 to 0.375
- up_bias: float32 [1024], replicated, may hold values from -3 to 3
- w_down: bfloat16 [1024, 256], replicated, may hold values from -0.1875 to 0.1875
Outputs:
- layer_out: bfloat16 [16, 8192, 256], P(('grp', 'snap'), 'clus'), parts along dimension 0
There are 2 independent parts, one for each index of `grp`. A program takes and returns all parts, laid end to end along the dimension named above; an argument that names none is the same for every part. Nothing has to cross between parts.
Inputs may be any that keep to these rules, and one draw needn't show every extreme that they name: `neighbors`: cluster c holds blocks c * 16 to (c + 1) * 16 - 1. Entry 0 of each block row names the row itself; the other entries name blocks of the row's own cluster, except that the last entry may name a block of another cluster. In each snapshot the rows of one cluster name exactly 4 distinct blocks of each other cluster.
All inputs are finite; a program needn't handle non-finite values.
Results may differ from a plain program's by a relative error of at most 0.0073.
Values may be sent and summed in bfloat16 or wider, within the bound.
No kernel may reach another device: no remote copies, remote signals or barrier semaphores. Data moves between devices by JAX's collectives and lax.ppermute only.
A program may use at most 128 MiB of HBM per device.

v0:
```python
import math

import jax
import jax.numpy as jnp
from jax import lax
from jax.sharding import PartitionSpec as P

HEADS = 8


def project_three(zvals, w_query, w_key, w_value):
    queries = jnp.dot(zvals, w_query, preferred_element_type=jnp.float32).astype(jnp.bfloat16)
    keys_all = jnp.dot(zvals, w_key, preferred_element_type=jnp.float32).astype(jnp.bfloat16)
    values = jnp.dot(zvals, w_value, preferred_element_type=jnp.float32).astype(jnp.bfloat16)
    return (queries, keys_all, values)


def temporal(zvals, queries, keys_all, values, w_out, w_up, up_bias, w_down):
    nsnap, nvert, width = zvals.shape
    head_dim = width // HEADS
    q_heads = queries.reshape(nsnap, nvert, HEADS, head_dim)
    k_heads = keys_all.reshape(nsnap, nvert, HEADS, head_dim)
    v_heads = values.reshape(nsnap, nvert, HEADS, head_dim)
    scores = jnp.einsum("tvhd,svhd->vhts", q_heads, k_heads, preferred_element_type=jnp.float32) * (
        1.0 / math.sqrt(head_dim)
    )
    causal = jnp.arange(nsnap)[:, None] >= jnp.arange(nsnap)[None, :]
    scores = jnp.where(causal, scores, -1e30)
    peak = jnp.max(scores, axis=-1, keepdims=True)
    expo = jnp.exp(scores - peak)
    probs = (expo / jnp.sum(expo, axis=-1, keepdims=True)).astype(jnp.bfloat16)
    attended = jnp.einsum("vhts,svhd->tvhd", probs, v_heads, preferred_element_type=jnp.float32)
    attended = attended.astype(jnp.bfloat16).reshape(nsnap, nvert, width)
    mixed = zvals.astype(jnp.float32) + jnp.dot(attended, w_out, preferred_element_type=jnp.float32)
    mixed_in = mixed.astype(jnp.bfloat16)
    hidden = jax.nn.relu(
        jnp.dot(mixed_in, w_up, preferred_element_type=jnp.float32) + up_bias
    ).astype(jnp.bfloat16)
    return (mixed + jnp.dot(hidden, w_down, preferred_element_type=jnp.float32)).astype(
        jnp.bfloat16
    )


def on_device(
    features,
    adj_tiles,
    neighbors,
    w_struct,
    pos_embed,
    w_query,
    w_key,
    w_value,
    w_out,
    w_up,
    up_bias,
    w_down,
):
    snap_dev, vert_cl, width = features.shape
    blk_cl, nbr_k, block = (adj_tiles.shape[1], adj_tiles.shape[2], adj_tiles.shape[3])
    my_cluster = lax.axis_index("clus")
    projected = jnp.dot(features, w_struct, preferred_element_type=jnp.float32).astype(jnp.bfloat16)
    projected = projected.reshape(snap_dev, blk_cl, block, width)
    my_rows = lax.dynamic_slice_in_dim(neighbors, my_cluster * blk_cl, blk_cl, 1)
    table = lax.all_gather(projected, "clus", axis=1, tiled=True)
    sources = jnp.take_along_axis(
        table, my_rows.reshape(snap_dev, blk_cl * nbr_k)[:, :, None, None], axis=1
    )
    sources = sources.reshape(snap_dev, blk_cl, nbr_k, block, width)
    summed = jnp.einsum("tbkij,tbkjd->tbid", adj_tiles, sources, preferred_element_type=jnp.float32)
    rows_in = features.astype(jnp.float32).reshape(snap_dev, blk_cl, block, width)
    struct_out = (rows_in + jax.nn.relu(summed)).astype(jnp.bfloat16)
    nsnap_dev = lax.axis_size("snap")
    vert_dev = vert_cl // nsnap_dev
    struct_out = struct_out.reshape(snap_dev, nsnap_dev, vert_dev, width)
    inputs = lax.all_to_all(struct_out, "snap", split_axis=1, concat_axis=0, tiled=True)[:, 0]
    zvals = (inputs.astype(jnp.float32) + pos_embed.astype(jnp.float32)[:, None, :]).astype(
        jnp.bfloat16
    )
    queries, keys_all, values = project_three(zvals, w_query, w_key, w_value)
    result = temporal(zvals, queries, keys_all, values, w_out, w_up, up_bias, w_down)[:, None]
    returned = lax.all_to_all(result, "snap", split_axis=0, concat_axis=1, tiled=True)
    return returned.reshape(snap_dev, vert_cl, width)


def solution(mesh):
    placed = (
        P(("grp", "snap"), "clus", None),
        P(("grp", "snap"), "clus", None, None, None),
        P(("grp", "snap"), None, None),
        P(),
        P(),
        P(),
        P(),
        P(),
        P(),
        P(),
        P(),
        P(),
    )
    return jax.shard_map(
        on_device,
        mesh=mesh,
        in_specs=placed,
        out_specs=P(("grp", "snap"), "clus", None),
        check_vma=False,
    )
```

profile of v0, /device:TPU:0, one launch (start us, length us, event | category | flops | bytes accessed | tf_op | source)
XLA Modules:
  0.0 317.0 jit_solution(16713772144260316526)
XLA Ops:
  6.5 0.0 copy-start
  6.5 0.0 copy-start.7
  6.5 0.0 all-gather.2.cloned.1.call-start
  6.5 3.7 %convolution_convert_fusion = bf16[2,2048,256]{2,1,0:T(8,128)(2,1)} fusion(bf16[2,2048,256]{2,1,0:T(8,128)(2,1)} %param.12, bf16[256,256]{1,0:T(8,128)(2,1)} %param.15), kind=kOutput, calls=%fused_computation.15 | convolution fusion | flops 537919488 | bytes 4325376 | tf_op jit(solution)/shard_map/dot_general | solution.py:61
  10.2 0.0 all-gather.2.cloned.1.call-update
  10.3 0.0 copy-done.7
  10.3 0.1 compare_and_fusion
  10.4 0.1 copy.52
  10.4 0.1 broadcast_in_dim_reshape.3
  10.5 0.1 reshape.118
  10.6 0.1 copy.51
  10.7 0.0 copy-start.1
  10.7 60.7 %all-gather.2.cloned.1.call-done = bf16[2,64,128,256]{3,2,1,0:T(8,128)(2,1)} async-done(((bf16[2,16,128,256]{3,2,1,0:T(8,128)(2,1)}), bf16[2,64,128,256]{3,2,1,0:T(8,128)(2,1)}) %all-gather.2.cloned.1.call-update) | async-done | bytes 8388624 | tf_op jit(solution)/shard_map/all_gather | solution.py:64
  71.4 10.6 %gather_fusion = bf16[128,128,256]{2,1,0:T(8,128)(2,1)} fusion(bf16[2,64,128,256]{3,2,1,0:T(8,128)(2,1)} %all-gather.2.cloned.1.call-done, s32[128]{0:T(128)S(1)} %reshape.118), kind=kCustom, calls=%fused_computation | custom fusion | bytes 16778240 | tf_op jit(solution)/shard_map/jit(take_along_axis)/gather | solution.py:65
  82.0 0.0 copy-done.1
  82.0 7.2 %fusion.5 = bf16[2,16,128,256]{3,2,1,0:T(8,128)(2,1)S(1)} fusion(bf16[2,16,128,256]{3,2,1,0:T(8,128)(2,1)S(1)} %bitcast.76, bf16[2,16,4,128,128]{4,3,2,1,0:T(8,128)(2,1)} %param.13, bf16[2,16,4,128,256]{4,3,2,1,0:T(8,128)(2,1)} %bitcast.73, pred[2,16,4]{2,1,0:T(8,128)(4,1)S(1)} %copy.51), kind=kOutput, calls=%fused_computation.10 | convolution fusion | flops 1082130432 | bytes 16777344 | tf_op jit(solution)/shard_map/tbkij,tbkjd->tbid/dot_general | solution.py:69
  89.2 0.0 copy-start.6
  89.2 1.5 copy.53
  90.7 4.6 %all-to-all-start = ((bf16[2,4,512,256]{3,2,0,1:T(8,128)(2,1)}), bf16[2,4,512,256]{3,2,0,1:T(8,128)(2,1)S(1)}, u32[]{:S(2)}, u32[]{:S(2)}) async-start(bf16[2,4,512,256]{3,2,0,1:T(8,128)(2,1)} %copy.53), calls=%async_computation | async-start | bytes 4194304 | tf_op jit(solution)/shard_map/all_to_all | solution.py:75
  95.3 0.0 copy-done.6
  95.3 48.6 %all-to-all-done = bf16[2,4,512,256]{3,2,0,1:T(8,128)(2,1)S(1)} async-done(((bf16[2,4,512,256]{3,2,0,1:T(8,128)(2,1)}), bf16[2,4,512,256]{3,2,0,1:T(8,128)(2,1)S(1)}, u32[]{:S(2)}, u32[]{:S(2)}) %all-to-all-start) | async-done | bytes 2097184 | tf_op jit(solution)/shard_map/all_to_all | solution.py:75
  143.9 0.4 bitcast_convert_fusion
  144.3 0.0 copy-start.2
  144.3 0.6 fusion.4
  145.0 0.2 copy-done.2
  145.2 2.1 convolution_convert_fusion.2
  147.3 0.0 copy-start.3
  147.3 12.6 %copy.57 = bf16[8,512,8,32]{3,0,2,1:T(8,128)(2,1)} copy(bf16[8,512,8,32]{1,3,2,0:T(8,128)(2,1)} %bitcast.70) | data formatting | bytes 4194304 | tf_op jit(solution)/shard_map/reshape | solution.py:21
  159.9 0.0 copy-done.3
  159.9 2.1 convolution_convert_fusion.1
  162.0 12.6 %copy.58 = bf16[8,512,8,32]{3,0,2,1:T(8,128)(2,1)} copy(bf16[8,512,8,32]{1,3,2,0:T(8,128)(2,1)} %bitcast.71) | data formatting | bytes 4194304 | tf_op jit(solution)/shard_map/reshape | solution.py:22
  174.5 11.5 %fusion.37 = f32[512,8,8,8]{2,3,1,0:T(8,128)} fusion(bf16[8,512,8,32]{3,0,2,1:T(8,128)(2,1)} %copy.57, bf16[8,512,8,32]{3,0,2,1:T(8,128)(2,1)} %copy.58), kind=kOutput, calls=%fused_computation.51 | convolution fusion | flops 16777216 | bytes 5242880 | tf_op jit(solution)/shard_map/tvhd,svhd->vhts/dot_general | solution.py:24
  186.1 10.7 %copy.59 = f32[512,8,8,8]{0,3,2,1:T(8,128)} copy(f32[512,8,8,8]{2,3,1,0:T(8,128)} %fusion.37) | data formatting | bytes 2097152 | tf_op jit(solution)/shard_map/tvhd,svhd->vhts/dot_general | solution.py:24
  196.7 1.9 fusion.36
  198.6 0.2 divide_convert_fusion
  198.8 0.0 copy-start.4
  198.9 11.8 %copy.61 = bf16[512,8,8,8]{3,2,1,0:T(8,128)(2,1)} copy(bf16[512,8,8,8]{0,3,2,1:T(8,128)(2,1)S(1)} %divide_convert_fusion) | data formatting | bytes 1048576 | tf_op jit(solution)/shard_map/convert_element_type | solution.py:31
  210.6 0.0 copy-done.4
  210.6 2.1 convolution_convert_fusion.3
  212.7 12.6 %copy.60 = bf16[8,512,8,32]{3,0,2,1:T(8,128)(2,1)} copy(bf16[8,512,8,32]{1,3,2,0:T(8,128)(2,1)} %bitcast.72) | data formatting | bytes 4194304 | tf_op jit(solution)/shard_map/reshape | solution.py:23
  225.3 10.1 %convert_bitcast_fusion = bf16[8,512,8,32]{3,0,2,1:T(8,128)(2,1)} fusion(bf16[8,512,8,32]{3,0,2,1:T(8,128)(2,1)} %copy.60, bf16[512,8,8,8]{3,2,1,0:T(8,128)(2,1)} %copy.61), kind=kOutput, calls=%fused_computation.3 | convolution fusion | flops 17825792 | bytes 4718592 | tf_op jit(solution)/shard_map/vhts,svhd->tvhd/dot_general | solution.py:32
  235.4 0.0 copy-start.5
  235.4 9.4 %copy.62 = bf16[8,512,8,32]{1,3,2,0:T(8,128)(2,1)} copy(bf16[8,512,8,32]{3,0,2,1:T(8,128)(2,1)} %convert_bitcast_fusion) | data formatting | bytes 4194304 | tf_op jit(solution)/shard_map/convert_element_type | solution.py:33
  244.8 0.0 copy-start.8
  244.8 0.0 copy-start.9
  244.8 0.0 copy-done.5
  244.8 4.4 %fusion.23 = f32[8,512,256]{2,1,0:T(8,128)} fusion(bf16[8,512,256]{1,2,0:T(8,128)(2,1)} %bitcast.69, bf16[256,256]{1,0:T(8,128)(2,1)S(1)} %copy-done.5), kind=kOutput, calls=%fused_computation.32 | convolution fusion | flops 536870912 | bytes 6422528 | tf_op jit(solution)/shard_map/dot_general | solution.py:34
  249.2 0.0 copy-done
  249.2 0.0 copy-done.8
  249.2 0.0 copy-done.9
  249.2 8.1 %fusion.9 = bf16[8,1,512,256]{3,2,1,0:T(8,128)(2,1)} fusion(f32[8,512,256]{2,1,0:T(8,128)} %fusion.23, bf16[8,512,256]{2,1,0:T(8,128)(2,1)S(1)} %fusion.4, f32[1024]{0:T(1024)S(1)} %copy-done.9, bf16[1024,256]{1,0:T(8,128)(2,1)S(1)} %copy-done, bf16[256,1024]{1,0:T(8,128)(2,1)S(1)} %copy-done.8), kind=kOutput, calls=%fused_computation.17 | convolution fusion | flops 4314890240 | bytes 9441280 | tf_op jit(solution)/shard_map/dot_general | solution.py:39
  257.3 51.4 %all_to_all.24 = bf16[8,1,512,256]{3,2,1,0:T(8,128)(2,1)S(1)} all-to-all(bf16[8,1,512,256]{3,2,1,0:T(8,128)(2,1)} %fusion.9), channel_id=1, replica_groups=mesh['grp'=2,'snap'=4,'clus'=4] {'snap'}, dimensions={0} | all-to-all | bytes 4194304 | tf_op jit(solution)/shard_map/all_to_all | solution.py:81
  308.7 1.5 copy.65
  (3 shorter events, 0.0 us)
Async XLA Ops:
  6.5 242.6 %copy-start = (bf16[1024,256]{1,0:T(8,128)(2,1)S(1)}, bf16[1024,256]{1,0:T(8,128)(2,1)}, u32[]{:S(2)}) copy-start(bf16[1024,256]{1,0:T(8,128)(2,1)} %param.23) | copy-start | bytes 1572868
  6.5 3.7 %copy-start.7 = (s32[2,64,4]{1,2,0:T(4,128)S(1)}, s32[2,64,4]{1,2,0:T(4,128)}, u32[]{:S(2)}) copy-start(s32[2,64,4]{1,2,0:T(4,128)} %param.14) | copy-start | bytes 6148
  6.5 64.9 %all-gather.2.cloned.1.call-start = ((), (), s32[]{:S(2)}) async-start(), calls=%async_computation.2 | async-start | bytes 10485760 | tf_op jit(solution)/shard_map/all_gather | solution.py:64
  10.7 71.3 %copy-start.1 = (bf16[2,2048,256]{2,1,0:T(8,128)(2,1)S(1)}, bf16[2,2048,256]{2,1,0:T(8,128)(2,1)}, u32[]{:S(2)}) copy-start(bf16[2,2048,256]{2,1,0:T(8,128)(2,1)} %param.12) | copy-start | bytes 6291460
  89.2 6.1 %copy-start.6 = (bf16[8,256]{1,0:T(8,128)(2,1)S(1)}, bf16[8,256]{1,0:T(8,128)(2,1)}, u32[]{:S(2)}) copy-start(bf16[8,256]{1,0:T(8,128)(2,1)} %param.16) | copy-start | bytes 12292
  90.7 53.2 %all-to-all-start = ((bf16[2,4,512,256]{3,2,0,1:T(8,128)(2,1)}), bf16[2,4,512,256]{3,2,0,1:T(8,128)(2,1)S(1)}, u32[]{:S(2)}, u32[]{:S(2)}) async-start(bf16[2,4,512,256]{3,2,0,1:T(8,128)(2,1)} %copy.53), calls=%async_computation | async-start | bytes 4194304 | tf_op jit(solution)/shard_map/all_to_all | solution.py:75
  144.3 0.9 copy-start.2
  147.3 12.6 %copy-start.3 = (bf16[256,256]{1,0:T(8,128)(2,1)S(1)}, bf16[256,256]{1,0:T(8,128)(2,1)}, u32[]{:S(2)}) copy-start(bf16[256,256]{1,0:T(8,128)(2,1)} %param.18) | copy-start | bytes 393220
  198.8 11.8 %copy-start.4 = (bf16[256,256]{1,0:T(8,128)(2,1)S(1)}, bf16[256,256]{1,0:T(8,128)(2,1)}, u32[]{:S(2)}) copy-start(bf16[256,256]{1,0:T(8,128)(2,1)} %param.19) | copy-start | bytes 393220
  235.4 9.4 %copy-start.5 = (bf16[256,256]{1,0:T(8,128)(2,1)S(1)}, bf16[256,256]{1,0:T(8,128)(2,1)}, u32[]{:S(2)}) copy-start(bf16[256,256]{1,0:T(8,128)(2,1)} %param.20) | copy-start | bytes 393220
  244.8 4.4 %copy-start.8 = (bf16[256,1024]{1,0:T(8,128)(2,1)S(1)}, bf16[256,1024]{1,0:T(8,128)(2,1)}, u32[]{:S(2)}) copy-start(bf16[256,1024]{1,0:T(8,128)(2,1)} %param.21) | copy-start | bytes 1572868
  244.8 4.4 %copy-start.9 = (f32[1024]{0:T(1024)S(1)}, f32[1024]{0:T(1024)}, u32[]{:S(2)}) copy-start(f32[1024]{0:T(1024)} %param.22) | copy-start | bytes 12292
Sparse Core Ops, SparseCore 0:
  10.4 60.9 all-gather.1
where the time goes:
time: 318 us; the launch traced here: 317 us
  waiting for transfers between devices  109 us (34%)
  local copies, waits for them, and re-layouts  83.7 us (26%)
  blocking collectives  51.4 us (16%)
  matrix products  51.3 us (16%)
  between operations  13.5 us (4%)
  starting transfers between devices  4.6 us (1%)
  other arithmetic  3.22 us (1%)
    all_gather x1, waiting for transfers between devices, on_device(): table = lax.all_gather(projected, 'clus', axis=1, tiled=True)  60.7 us
    all_to_all x1, blocking collectives, on_device(): lax.all_to_all(result, 'snap', split_axis=0, concat_axis=1, tiled=True)  51.4 us
    all_to_all x1, waiting for transfers between devices, on_device(): lax.all_to_all(struct_out, 'snap', split_axis=1, concat_axis=0, tiled=True)  48.6 us
    reshape x1, local copies, waits for them, and re-layouts, temporal(): q_heads = queries.reshape(nsnap, nvert, HEADS, head_dim)  12.6 us
    reshape x1, local copies, waits for them, and re-layouts, temporal(): v_heads = values.reshape(nsnap, nvert, HEADS, head_dim)  12.6 us
    reshape x1, local copies, waits for them, and re-layouts, temporal(): k_heads = keys_all.reshape(nsnap, nvert, HEADS, head_dim)  12.6 us
    convert_element_type x1, local copies, waits for them, and re-layouts, temporal(): probs = (expo / jnp.sum(expo, axis=-1, keepdims=True)).astype(jnp.bfloat16)  11.8 us
    dot_general x1, matrix products, temporal(): jnp.einsum('tvhd,svhd->vhts', q_heads, k_heads, preferred_element_type=jn...  11.5 us
  transfers between devices with their start and end apart: 2, of which 2 were waited for; matrix products, arithmetic and copies ran while one was open for 0% of the time, Pallas kernels for 0%

commit v1 on v0

v1 whole, which is shorter than its diff:
```python
import functools
import math

import jax
import jax.numpy as jnp
from jax import lax
from jax.experimental import pallas as pl
from jax.experimental.pallas import tpu as pltpu
from jax.sharding import PartitionSpec as P

HEADS = 8
LANES = 128
NEG = -1e30
F32 = jnp.float32
BF16 = jnp.bfloat16


def dot(a, b):
    return jnp.dot(a, b, preferred_element_type=F32)


def partner(me, d, n):
    return me ^ d if n & (n - 1) == 0 else (me + d) % n


def came_from(me, d, n):
    return me ^ d if n & (n - 1) == 0 else (me + n - d) % n


def named_mask(nbr_ref, t, first, cluster, blk_cl):
    last = nbr_ref.shape[1] - 1
    mask = jnp.int32(0)
    for i in range(blk_cl):
        g = nbr_ref[t, last, first + i] - cluster * blk_cl
        mask |= jnp.where((g >= 0) & (g < blk_cl), jnp.left_shift(1, g & 31), 0)
    return mask


def gather_kernel(most, n_clus, nbr_ref, feat_ref, *refs):
    snap_dev, blk_cl = feat_ref.shape[:2]
    outs, sems = refs[:-1], refs[-1]
    me = lax.axis_index("clus")
    copies = []
    for t in range(snap_dev):
        for d in range(1, n_clus):
            where_to = partner(me, d, n_clus)
            mask = named_mask(nbr_ref, t, where_to * blk_cl, me, blk_cl)
            picked = [jnp.int32(0)] * most
            count = jnp.int32(0)
            for b in range(blk_cl):
                bit = jnp.right_shift(mask, b) & 1
                for j in range(most):
                    picked[j] = jnp.where((bit == 1) & (count == j), b, picked[j])
                count += bit
            e = t * (n_clus - 1) + d - 1
            for j in range(most):
                copy = pltpu.make_async_copy(
                    feat_ref.at[t, picked[j]], outs[e].at[j], sems.at[e, j]
                )
                copy.start()
                copies.append(copy)
    for copy in copies:
        copy.wait()


def gather_blocks(nbr, feat, most, n_clus):
    snap_dev, _, block, width = feat.shape
    sets = snap_dev * (n_clus - 1)
    shape = (most, block, width)
    return pl.pallas_call(
        functools.partial(gather_kernel, most, n_clus),
        grid=(1,),
        out_shape=[pltpu.HBM(shape, BF16)] * sets,
        in_specs=[
            pl.BlockSpec(memory_space=pltpu.SMEM),
            pl.BlockSpec(memory_space=pl.ANY),
        ],
        out_specs=[pl.BlockSpec(shape, lambda g: (0, 0, 0))] * sets,
        scratch_shapes=[pltpu.SemaphoreType.DMA((sets, most))],
        cost_estimate=pl.CostEstimate(
            flops=0, bytes_accessed=2 * 2 * sets * most * block * width, transcendentals=0
        ),
        name="gather_blocks",
    )(nbr, feat)


def struct_kernel(dims, t, nbr_ref, feat_ref, *refs):
    n_clus, most, n_snap = dims
    remote = refs[: n_clus - 1]
    adj_ref, w_ref = refs[n_clus - 1 : n_clus + 1]
    outs = refs[n_clus + 1 : n_clus + 1 + n_snap]
    table, slots = refs[n_clus + 1 + n_snap :]
    g = pl.program_id(0)
    my_clus = lax.axis_index("clus")
    my_snap = lax.axis_index("snap") if n_snap > 1 else 0
    blk_cl, block, width = feat_ref.shape[1:]
    nbr_k = adj_ref.shape[2]
    first = my_clus * blk_cl

    @pl.when(g == 0)
    def _():
        for i in range(blk_cl):
            slots[i] = nbr_ref[t, nbr_k - 1, first + i] - first
        for d in range(1, n_clus):
            other = came_from(my_clus, d, n_clus)
            mask = named_mask(nbr_ref, t, first, other, blk_cl)
            for i in range(blk_cl):
                b = nbr_ref[t, nbr_k - 1, first + i] - other * blk_cl
                below = mask & (jnp.left_shift(1, b & 31) - 1)
                rank = jnp.int32(0)
                for _ in range(most):
                    rank += jnp.where(below != 0, 1, 0)
                    below &= below - 1
                slots[i] = jnp.where(
                    (b >= 0) & (b < blk_cl), blk_cl + (d - 1) * most + rank, slots[i]
                )
        w = w_ref[...]
        for b in range(blk_cl):
            table[b] = dot(feat_ref[0, b], w).astype(BF16)
        for d in range(n_clus - 1):
            for j in range(most):
                table[blk_cl + d * most + j] = dot(remote[d][j], w).astype(BF16)

    for d in range(n_snap):
        p = lax.rem(my_snap + d, n_snap) if n_snap > 1 else 0
        row = g * n_snap + p
        where = [nbr_ref[t, k, first + row] - first for k in range(nbr_k - 1)] + [slots[row]]
        tiles = jnp.concatenate([adj_ref[0, p, k] for k in range(nbr_k)], axis=1)
        total = dot(tiles, jnp.concatenate([table[slot] for slot in where], axis=0))
        outs[d][0] = (feat_ref[0, row].astype(F32) + jnp.maximum(total, 0.0)).astype(BF16)


def struct_phase(nbr, feat, remote, adj, w, t, n_snap):
    _, blk_cl, block, width = feat.shape
    nbr_k = adj.shape[2]
    n_clus = len(remote) + 1
    most = remote[0].shape[0] if remote else 0
    chunks = blk_cl // n_snap
    whole = lambda *shape: pl.BlockSpec(shape, lambda g: (0,) * len(shape))
    return pl.pallas_call(
        functools.partial(struct_kernel, (n_clus, most, n_snap), t),
        grid=(chunks,),
        out_shape=[pltpu.HBM((chunks, block, width), BF16)] * n_snap,
        in_specs=[
            pl.BlockSpec(memory_space=pltpu.SMEM),
            pl.BlockSpec((1, blk_cl, block, width), lambda g: (t, 0, 0, 0)),
        ]
        + [whole(most, block, width)] * (n_clus - 1)
        + [
            pl.BlockSpec((1, n_snap, nbr_k, block, block), lambda g: (t, g, 0, 0, 0)),
            whole(width, width),
        ],
        out_specs=[pl.BlockSpec((1, block, width), lambda g: (g, 0, 0))] * n_snap,
        scratch_shapes=[
            pltpu.VMEM((blk_cl + (n_clus - 1) * most, block, width), BF16),
            pltpu.SMEM((blk_cl,), jnp.int32),
        ],
        compiler_params=pltpu.CompilerParams(vmem_limit_bytes=24 << 20),
        cost_estimate=pl.CostEstimate(
            flops=2 * blk_cl * block * width * (2 * width + nbr_k * block),
            bytes_accessed=2 * blk_cl * block * (3 * width + nbr_k * block),
            transcendentals=0,
        ),
        name="struct_phase",
    )(nbr, feat, *remote, adj, w)


def temporal_kernel(n_snap, per, *refs):
    count = n_snap * per
    ins = refs[:count]
    pos_ref, wqkv_ref, wo_ref, wup_ref, bias_ref, wdown_ref = refs[count : count + 6]
    outs = refs[count + 6 : count + 6 + n_snap]
    zs, qkv, att, res = refs[count + 6 + n_snap :]
    me = lax.axis_index("snap")
    nsnap, nvert, width = zs.shape
    head_dim = width // HEADS
    for d in range(n_snap):
        src = lax.rem(me + n_snap - d, n_snap)
        for j in range(per):
            t = src * per + j
            zs[t] = (ins[d * per + j][0].astype(F32) + pos_ref[pl.ds(t, 1), :]).astype(BF16)

    for t in range(nsnap):
        qkv[t] = (
            lax.dot_general(
                wqkv_ref[...], zs[t], (((1,), (1,)), ((), ())), preferred_element_type=F32
            )
            .astype(BF16)
            .astype(F32)
        )

    def part(which, t):
        return qkv[t, which * width : (which + 1) * width, :].reshape(head_dim, HEADS, nvert)

    for t in range(nsnap):
        q = part(0, t)
        scores = [
            jnp.sum(q * part(1, s), axis=0) * (1.0 / math.sqrt(head_dim)) for s in range(t + 1)
        ]
        peak = functools.reduce(jnp.maximum, scores)
        expo = [jnp.exp(x - peak) for x in scores]
        total = functools.reduce(jnp.add, expo)
        acc = None
        for s in range(t + 1):
            prob = (expo[s] / total).astype(BF16).astype(F32)
            term = prob[None] * part(2, s)
            acc = term if acc is None else acc + term
        att[t] = acc.reshape(width, nvert).astype(BF16)

    group = max(1, 256 // nvert)
    for g in range(nsnap // group):
        some = slice(g * group, (g + 1) * group)
        z = zs[some].reshape(group * nvert, width)
        joined = jnp.concatenate([att[g * group + i] for i in range(group)], axis=1)
        mixed = z.astype(F32) + lax.dot_general(
            joined, wo_ref[...], (((0,), (0,)), ((), ())), preferred_element_type=F32
        )
        hidden = jnp.maximum(dot(mixed.astype(BF16), wup_ref[...]) + bias_ref[...], 0.0)
        out = mixed + dot(hidden.astype(BF16), wdown_ref[...])
        res[some] = out.astype(BF16).reshape(group, nvert, width)

    for d in range(n_snap):
        dst = lax.rem(me + d, n_snap)
        for j in range(per):
            outs[d][j] = res[dst * per + j]


def temporal_chunk(ins, chunk, weights, n_snap, per):
    pos, wqkv, wo, wup, bias, wdown = weights
    _, block, width = ins[0].shape
    nsnap = n_snap * per
    ff = wup.shape[1]
    whole = lambda x: pl.BlockSpec(x.shape, lambda g: (0,) * x.ndim)
    tokens = nsnap * block
    return pl.pallas_call(
        functools.partial(temporal_kernel, n_snap, per),
        grid=(1,),
        out_shape=[pltpu.HBM((per, block, width), BF16)] * n_snap,
        in_specs=[pl.BlockSpec((1, block, width), lambda g: (chunk, 0, 0))] * len(ins)
        + [whole(x) for x in weights],
        out_specs=[pl.BlockSpec((per, block, width), lambda g: (0, 0, 0))] * n_snap,
        scratch_shapes=[
            pltpu.VMEM((nsnap, block, width), BF16),
            pltpu.VMEM((nsnap, 3 * width, block), F32),
            pltpu.VMEM((nsnap, width, block), BF16),
            pltpu.VMEM((nsnap, block, width), BF16),
        ],
        compiler_params=pltpu.CompilerParams(vmem_limit_bytes=32 << 20),
        cost_estimate=pl.CostEstimate(
            flops=2 * tokens * width * (4 * width + 2 * ff),
            bytes_accessed=4 * tokens * width + 2 * width * (4 * width + 2 * ff),
            transcendentals=tokens * HEADS * nsnap,
        ),
        name="temporal_chunk",
    )(*ins, *weights)


def head_minor(w):
    width = w.shape[0]
    return w.T.reshape(HEADS, width // HEADS, width).transpose(1, 0, 2).reshape(width, width)


def shift(x, d, n):
    return lax.ppermute(x, "snap", [(i, (i + d) % n) for i in range(n)])


def temporal_fast(sent, weights, n_snap):
    per = len(sent)
    chunks, block, width = sent[0][0].shape
    got = [
        [sent[t][d] if d == 0 else shift(sent[t][d], d, n_snap) for d in range(n_snap)]
        for t in range(per)
    ]
    out = jnp.zeros((per, chunks * n_snap * block, width), BF16)
    me = lax.axis_index("snap")
    for c in range(chunks):
        ins = [got[j][d] for d in range(n_snap) for j in range(per)]
        res = temporal_chunk(ins, c, weights, n_snap, per)
        for d in range(n_snap):
            back = res[d] if d == 0 else shift(res[d], d, n_snap)
            src = (me + n_snap - d) % n_snap
            out = lax.dynamic_update_slice_in_dim(out, back, (c * n_snap + src) * block, 1)
    return out


def temporal_plain(zvals, w_query, w_key, w_value, w_out, w_up, up_bias, w_down):
    nsnap, nvert, width = zvals.shape
    head_dim = width // HEADS
    heads = (nsnap, nvert, HEADS, head_dim)
    q_heads = dot(zvals, w_query).astype(BF16).reshape(heads)
    k_heads = dot(zvals, w_key).astype(BF16).reshape(heads)
    v_heads = dot(zvals, w_value).astype(BF16).reshape(heads)
    scores = jnp.einsum("tvhd,svhd->vhts", q_heads, k_heads, preferred_element_type=F32)
    scores = scores * (1.0 / math.sqrt(head_dim))
    causal = jnp.arange(nsnap)[:, None] >= jnp.arange(nsnap)[None, :]
    scores = jnp.where(causal, scores, NEG)
    peak = jnp.max(scores, axis=-1, keepdims=True)
    expo = jnp.exp(scores - peak)
    probs = (expo / jnp.sum(expo, axis=-1, keepdims=True)).astype(BF16)
    attended = jnp.einsum("vhts,svhd->tvhd", probs, v_heads, preferred_element_type=F32)
    attended = attended.astype(BF16).reshape(nsnap, nvert, width)
    mixed = zvals.astype(F32) + dot(attended, w_out)
    hidden = jax.nn.relu(dot(mixed.astype(BF16), w_up) + up_bias).astype(BF16)
    return (mixed + dot(hidden, w_down)).astype(BF16)


def on_device(
    features,
    adj_tiles,
    neighbors,
    w_struct,
    pos_embed,
    w_query,
    w_key,
    w_value,
    w_out,
    w_up,
    up_bias,
    w_down,
):
    snap_dev, vert_cl, width = features.shape
    blk_cl, nbr_k, block = adj_tiles.shape[1:4]
    n_clus, n_snap = lax.axis_size("clus"), lax.axis_size("snap")
    most = 4
    nbr = neighbors.transpose(0, 2, 1)
    feat = features.reshape(snap_dev, blk_cl, block, width)
    sets = gather_blocks(nbr, feat, most, n_clus)
    remote = []
    for t in range(snap_dev):
        remote.append(
            [
                lax.ppermute(
                    sets[t * (n_clus - 1) + d - 1],
                    "clus",
                    [(i, partner(i, d, n_clus)) for i in range(n_clus)],
                )
                for d in range(1, n_clus)
            ]
        )
    fast = snap_dev * n_snap <= 8 and blk_cl % n_snap == 0 and block % LANES == 0
    groups = n_snap if fast else 1
    sent = [
        struct_phase(nbr, feat, remote[t], adj_tiles, w_struct, t, groups)
        for t in range(snap_dev)
    ]
    if fast:
        weights = (
            pos_embed.astype(F32),
            jnp.concatenate([head_minor(w_query), head_minor(w_key), head_minor(w_value)], 0),
            w_out.reshape(HEADS, width // HEADS, width)
            .transpose(1, 0, 2)
            .reshape(width, width),
            w_up,
            up_bias.reshape(1, -1),
            w_down,
        )
        return temporal_fast(sent, weights, n_snap)
    vert_dev = vert_cl // n_snap
    struct_out = jnp.stack([s[0].reshape(n_snap, vert_dev, width) for s in sent])
    inputs = lax.all_to_all(struct_out, "snap", split_axis=1, concat_axis=0, tiled=True)[:, 0]
    zvals = (inputs.astype(F32) + pos_embed.astype(F32)[:, None, :]).astype(BF16)
    result = temporal_plain(zvals, w_query, w_key, w_value, w_out, w_up, up_bias, w_down)
    returned = lax.all_to_all(
        result[:, None], "snap", split_axis=0, concat_axis=1, tiled=True
    )
    return returned.reshape(snap_dev, vert_cl, width)


def solution(mesh):
    placed = (
        P(("grp", "snap"), "clus", None),
        P(("grp", "snap"), "clus", None, None, None),
        P(("grp", "snap"), None, None),
        P(),
        P(),
        P(),
        P(),
        P(),
        P(),
        P(),
        P(),
        P(),
    )
    return jax.shard_map(
        on_device,
        mesh=mesh,
        in_specs=placed,
        out_specs=P(("grp", "snap"), "clus", None),
        check_vma=False,
    )
```

time: 318 us -> 131 us (0.41)
  local copies, waits for them, and re-layouts: 83.7 us -> 13.1 us
  waiting for transfers between devices: 109 us -> 56.1 us
  blocking collectives: 51.4 us -> 0 us
  matrix products: 51.3 us -> 0 us
  starting transfers between devices: 4.6 us -> 34.6 us
  Pallas kernels: 0 us -> 26.5 us
  between operations: 13.5 us -> 0.54 us
  other arithmetic: 3.22 us -> 0.03 us
    all_gather x1 -> x0, waiting for transfers between devices: 60.7 us -> none  [on_device(): table = lax.all_gather(projected, 'clus', axis=1, tiled=True)]
    ppermute x0 -> x24, waiting for transfers between devices: none -> 56.1 us  [the longest x18 45.6 us: shift(): return lax.ppermute(x, 'snap', [(i, (i + d) % n) for i in range(n)])]
    all_to_all x1 -> x0, blocking collectives: 51.4 us -> none  [on_device(): lax.all_to_all(result, 'snap', split_axis=0, concat_axis=1, tiled=True)]
    dot_general x9 -> x0, matrix products: 51.3 us -> none  [the longest x1 11.5 us: temporal(): jnp.einsum('tvhd,svhd->vhts', q_heads, k_heads, preferred_element_type=jn...]
    all_to_all x1 -> x0, waiting for transfers between devices: 48.6 us -> none  [on_device(): lax.all_to_all(struct_out, 'snap', split_axis=1, concat_axis=0, tiled=True)]
    reshape x4 -> x2, local copies, waits for them, and re-layouts: 39.2 us -> 1.13 us  [the longest x1 0.98 us: on_device(): w_out.reshape(HEADS, width // HEADS, width).transpose(1, 0, 2)]
    ppermute x0 -> x24, starting transfers between devices: none -> 34.6 us  [the longest x18 29.4 us: shift(): return lax.ppermute(x, 'snap', [(i, (i + d) % n) for i in range(n)])]
    pallas_call x0 -> x7, Pallas kernels: none -> 26.5 us  [the longest x4 15 us: temporal_chunk(): pl.pallas_call(functools.partial(temporal_kernel, n_snap, per), grid=(1,)...]
  transfers between devices with their start and end apart: 2 -> 24, of which waited for: 2 -> 8; matrix products, arithmetic and copies ran while one was open for 0% -> 3% of each run, Pallas kernels for 0% -> 14%
where the time goes in v1:
time: 131 us
  waiting for transfers between devices  56.1 us (43%)
  starting transfers between devices  34.6 us (26%)
  Pallas kernels  26.5 us (20%)
  local copies, waits for them, and re-layouts  13.1 us (10%)
    ppermute x18, waiting for transfers between devices, shift(): return lax.ppermute(x, 'snap', [(i, (i + d) % n) for i in range(n)])  45.6 us
    ppermute x18, starting transfers between devices, shift(): return lax.ppermute(x, 'snap', [(i, (i + d) % n) for i in range(n)])  29.4 us
    pallas_call x4, Pallas kernels, temporal_chunk(): pl.pallas_call(functools.partial(temporal_kernel, n_snap, per), grid=(1,)...  15 us
    unnamed x59, local copies, waits for them, and re-layouts  10.8 us
    ppermute x6, waiting for transfers between devices, on_device(): lax.ppermute(sets[t * (n_clus - 1) + d - 1], 'clus', [(i, partner(i, d, n...  10.4 us
    pallas_call x2, Pallas kernels, struct_phase(): pl.pallas_call(functools.partial(struct_kernel, (n_clus, most, n_snap), t...  7.32 us
    ppermute x6, starting transfers between devices, on_device(): lax.ppermute(sets[t * (n_clus - 1) + d - 1], 'clus', [(i, partner(i, d, n...  5.23 us
    pallas_call x1, Pallas kernels, gather_blocks(): pl.pallas_call(functools.partial(gather_kernel, most, n_clus), grid=(1,),...  4.11 us
  transfers between devices with their start and end apart: 24, of which 8 were waited for; matrix products, arithmetic and copies ran while one was open for 3% of the time, Pallas kernels for 14%

profile of v1, /device:TPU:0, one launch (start us, length us, event | category | flops | bytes accessed | tf_op | source)
XLA Modules:
  0.0 130.8 jit_solution(690227145732495507)
XLA Ops:
  0.0 4.1 %gather_blocks.1 = (bf16[4,128,256]{2,1,0:T(8,128)(2,1)}, bf16[4,128,256]{2,1,0:T(8,128)(2,1)}, bf16[4,128,256]{2,1,0:T(8,128)(2,1)}, bf16[4,128,256]{2,1,0:T(8,...) custom-call(s32[2,4,64]{2,1,0:T(4,128)} %bitcast.38, bf16[2,16,128,256]{3,2,1,0:T(8,128)(2,1)} %bitcast.31), custom_call_target="tpu_custom_call" | custom-call | bytes 3145728 | tf_op jit(solution)/shard_map/gather_blocks/pallas_call | solution.py:70
  4.1 0.5 collective-permute-start.3
  4.6 2.6 %collective-permute-start.4 = (bf16[4,128,256]{2,1,0:T(8,128)(2,1)}, bf16[4,128,256]{2,1,0:T(8,128)(2,1)S(1)}, u32[]{:S(2)}, u32[]{:S(2)}) collective-permute-start(bf16[4,128,256]{2,1,0:T(8,128)(2,1)} %get-tuple-element.40), channel_id=1, source_target_pairs={{0,2},{1,3},{2,0},{3,1},{4,6},{5,7},{6,4},{7,5},{8,10},{9,11},{10,... | collective-permute-start | bytes 786440 | tf_op jit(solution)/shard_map/ppermute | solution.py:332
  7.2 0.1 collective-permute-start.5
  7.3 0.1 collective-permute-start
  7.4 1.9 %collective-permute-start.1 = (bf16[4,128,256]{2,1,0:T(8,128)(2,1)}, bf16[4,128,256]{2,1,0:T(8,128)(2,1)S(1)}, u32[]{:S(2)}, u32[]{:S(2)}) collective-permute-start(bf16[4,128,256]{2,1,0:T(8,128)(2,1)} %get-tuple-element.36), channel_id=1, source_target_pairs={{0,2},{1,3},{2,0},{3,1},{4,6},{5,7},{6,4},{7,5},{8,10},{9,11},{10,... | collective-permute-start | bytes 786440 | tf_op jit(solution)/shard_map/ppermute | solution.py:332
  9.3 0.0 collective-permute-done.3.refs_0_
  9.3 0.0 collective-permute-start.2
  9.4 5.2 %collective-permute-done.4.refs_1_ = bf16[4,128,256]{2,1,0:T(8,128)(2,1)S(1)} collective-permute-done((bf16[4,128,256]{2,1,0:T(8,128)(2,1)}, bf16[4,128,256]{2,1,0:T(8,128)(2,1)S(1)}, u32[]{:S(2)}, u32[]{:S(2)}) %collective-permute-start.4) | collective-permute-done | bytes 262176 | tf_op jit(solution)/shard_map/ppermute | solution.py:332
  14.6 5.2 %collective-permute-done.5.refs_2_ = bf16[4,128,256]{2,1,0:T(8,128)(2,1)S(1)} collective-permute-done((bf16[4,128,256]{2,1,0:T(8,128)(2,1)}, bf16[4,128,256]{2,1,0:T(8,128)(2,1)S(1)}, u32[]{:S(2)}, u32[]{:S(2)}) %collective-permute-start.5) | collective-permute-done | bytes 262176 | tf_op jit(solution)/shard_map/ppermute | solution.py:332
  19.8 2.2 %copy-done.1 = bf16[2,16,4,128,128]{4,3,2,1,0:T(8,128)(2,1)S(1)} copy-done((bf16[2,16,4,128,128]{4,3,2,1,0:T(8,128)(2,1)S(1)}, bf16[2,16,4,128,128]{4,3,2,1,0:T(8,128)(2,1)}, u32[]{:S(2)}) %copy-start.1) | copy-done | bytes 4194328
  22.0 0.9 copy-done.3
  22.9 3.7 %struct_phase.3 = (bf16[4,128,256]{2,1,0:T(8,128)(2,1)}, bf16[4,128,256]{2,1,0:T(8,128)(2,1)}, bf16[4,128,256]{2,1,0:T(8,128)(2,1)}, bf16[4,128,256]{2,1,0:T(8,128)(2,1)}) custom-call(s32[2,4,64]{2,1,0:T(4,128)S(1)} %bitcast.39, bf16[2,16,128,256]{3,2,1,0:T(8,128)(2,1)S(1)} %bitcast.32, bf16[4,128,256]{2,1,0:T(8,128)(2,1)S(1)} %collective-permute-done.3.refs_0_, ...), custom_call_target="tpu_custom_call" | custom-call | flops 1073741824 | bytes 5242880 | tf_op jit(solution)/shard_map/struct_phase/pallas_call | solution.py:140
  26.5 3.6 %collective-permute-start.11 = (bf16[4,128,256]{2,1,0:T(8,128)(2,1)}, bf16[4,128,256]{2,1,0:T(8,128)(2,1)S(1)}, u32[]{:S(2)}, u32[]{:S(2)}) collective-permute-start(bf16[4,128,256]{2,1,0:T(8,128)(2,1)} %get-tuple-element.48), channel_id=1, source_target_pairs={{0,12},{4,0},{8,4},{12,8},{1,13},{5,1},{9,5},{13,9},{2,14},{6,2},{... | collective-permute-start | bytes 786440 | tf_op jit(solution)/shard_map/ppermute | solution.py:264
  30.1 0.8 copy.21
  30.9 0.8 copy.19
  31.7 1.0 copy.17
  32.7 0.1 copy.29
  32.8 1.0 copy.28
  33.9 0.1 collective-permute-start.7
  33.9 1.0 collective-permute-start.9
  34.9 0.0 copy-start.2
  35.0 2.2 %copy-done.2 = bf16[2,16,4,128,128]{4,3,2,1,0:T(8,128)(2,1)S(1)} copy-done((bf16[2,16,4,128,128]{4,3,2,1,0:T(8,128)(2,1)S(1)}, bf16[2,16,4,128,128]{4,3,2,1,0:T(8,128)(2,1)}, u32[]{:S(2)}) %copy-start.2) | copy-done | bytes 4194328
  37.2 0.0 copy-start.10
  37.2 3.7 %struct_phase.2 = (bf16[4,128,256]{2,1,0:T(8,128)(2,1)}, bf16[4,128,256]{2,1,0:T(8,128)(2,1)}, bf16[4,128,256]{2,1,0:T(8,128)(2,1)}, bf16[4,128,256]{2,1,0:T(8,128)(2,1)}) custom-call(s32[2,4,64]{2,1,0:T(4,128)S(1)} %bitcast.40, bf16[2,16,128,256]{3,2,1,0:T(8,128)(2,1)S(1)} %bitcast.33, bf16[4,128,256]{2,1,0:T(8,128)(2,1)S(1)} %collective-permute-done.refs_0_, ...), custom_call_target="tpu_custom_call" | custom-call | flops 1073741824 | bytes 5242880 | tf_op jit(solution)/shard_map/struct_phase/pallas_call | solution.py:140
  40.8 2.8 %collective-permute-start.10 = (bf16[4,128,256]{2,1,0:T(8,128)(2,1)}, bf16[4,128,256]{2,1,0:T(8,128)(2,1)S(1)}, u32[]{:S(2)}, u32[]{:S(2)}) collective-permute-start(bf16[4,128,256]{2,1,0:T(8,128)(2,1)} %get-tuple-element.47), channel_id=1, source_target_pairs={{0,12},{4,0},{8,4},{12,8},{1,13},{5,1},{9,5},{13,9},{2,14},{6,2},{... | collective-permute-start | bytes 786440 | tf_op jit(solution)/shard_map/ppermute | solution.py:264
  43.6 0.6 collective-permute-start.6
  44.2 0.0 collective-permute-done.11.refs_7_
  44.2 1.4 %collective-permute-start.8 = (bf16[4,128,256]{2,1,0:T(8,128)(2,1)}, bf16[4,128,256]{2,1,0:T(8,128)(2,1)S(1)}, u32[]{:S(2)}, u32[]{:S(2)}) collective-permute-start(bf16[4,128,256]{2,1,0:T(8,128)(2,1)} %get-tuple-element.45), channel_id=1, source_target_pairs={{0,8},{4,12},{8,0},{12,4},{1,9},{5,13},{9,1},{13,5},{2,10},{6,14},... | collective-permute-start | bytes 786440 | tf_op jit(solution)/shard_map/ppermute | solution.py:264
  45.7 0.1 copy_bitcast_fusion.1
  45.9 9.7 %collective-permute-done.9.refs_5_ = bf16[4,128,256]{2,1,0:T(8,128)(2,1)S(1)} collective-permute-done((bf16[4,128,256]{2,1,0:T(8,128)(2,1)}, bf16[4,128,256]{2,1,0:T(8,128)(2,1)S(1)}, u32[]{:S(2)}, u32[]{:S(2)}) %collective-permute-start.9) | collective-permute-done | bytes 262176 | tf_op jit(solution)/shard_map/ppermute | solution.py:264
  55.6 6.4 %collective-permute-done.6.refs_2_ = bf16[4,128,256]{2,1,0:T(8,128)(2,1)S(1)} collective-permute-done((bf16[4,128,256]{2,1,0:T(8,128)(2,1)}, bf16[4,128,256]{2,1,0:T(8,128)(2,1)S(1)}, u32[]{:S(2)}, u32[]{:S(2)}) %collective-permute-start.6) | collective-permute-done | bytes 262176 | tf_op jit(solution)/shard_map/ppermute | solution.py:264
  62.0 15.5 %collective-permute-done.8.refs_4_ = bf16[4,128,256]{2,1,0:T(8,128)(2,1)S(1)} collective-permute-done((bf16[4,128,256]{2,1,0:T(8,128)(2,1)}, bf16[4,128,256]{2,1,0:T(8,128)(2,1)S(1)}, u32[]{:S(2)}, u32[]{:S(2)}) %collective-permute-start.8) | collective-permute-done | bytes 262176 | tf_op jit(solution)/shard_map/ppermute | solution.py:264
  77.5 0.0 copy-start.9
  77.5 0.9 copy-done.9
  78.5 3.7 %temporal_chunk.4 = (bf16[2,128,256]{2,1,0:T(8,128)(2,1)}, bf16[2,128,256]{2,1,0:T(8,128)(2,1)}, bf16[2,128,256]{2,1,0:T(8,128)(2,1)}, bf16[2,128,256]{2,1,0:T(8,128)(2,1)}) custom-call(bf16[4,128,256]{2,1,0:T(8,128)(2,1)S(1)} %copy-done.9, bf16[4,128,256]{2,1,0:T(8,128)(2,1)S(1)} %copy-done.8, bf16[4,128,256]{2,1,0:T(8,128)(2,1)S(1)} %collective-permute-done.6.refs_2_, ...), custom_call_target="tpu_custom_call" | custom-call | flops 1610612736 | bytes 2621440 | tf_op jit(solution)/shard_map/temporal_chunk/pallas_call | solution.py:235
  82.2 0.2 collective-permute-start.12
  82.4 3.3 %collective-permute-start.13 = (bf16[2,128,256]{2,1,0:T(8,128)(2,1)}, bf16[2,128,256]{2,1,0:T(8,128)(2,1)S(1)}, u32[]{:S(2)}, u32[]{:S(2)}) collective-permute-start(bf16[2,128,256]{2,1,0:T(8,128)(2,1)} %get-tuple-element.51), channel_id=1, source_target_pairs={{0,8},{4,12},{8,0},{12,4},{1,9},{5,13},{9,1},{13,5},{2,10},{6,14},... | collective-permute-start | bytes 393224 | tf_op jit(solution)/shard_map/ppermute | solution.py:264
  85.8 0.3 collective-permute-start.14
  86.1 3.8 %temporal_chunk.5 = (bf16[2,128,256]{2,1,0:T(8,128)(2,1)}, bf16[2,128,256]{2,1,0:T(8,128)(2,1)}, bf16[2,128,256]{2,1,0:T(8,128)(2,1)}, bf16[2,128,256]{2,1,0:T(8,128)(2,1)}) custom-call(bf16[4,128,256]{2,1,0:T(8,128)(2,1)S(1)} %copy-done.9, bf16[4,128,256]{2,1,0:T(8,128)(2,1)S(1)} %copy-done.8, bf16[4,128,256]{2,1,0:T(8,128)(2,1)S(1)} %collective-permute-done.6.refs_2_, ...), custom_call_target="tpu_custom_call" | custom-call | flops 1610612736 | bytes 2621440 | tf_op jit(solution)/shard_map/temporal_chunk/pallas_call | solution.py:235
  89.8 1.7 %collective-permute-start.15 = (bf16[2,128,256]{2,1,0:T(8,128)(2,1)}, bf16[2,128,256]{2,1,0:T(8,128)(2,1)S(1)}, u32[]{:S(2)}, u32[]{:S(2)}) collective-permute-start(bf16[2,128,256]{2,1,0:T(8,128)(2,1)} %get-tuple-element.54), channel_id=1, source_target_pairs={{0,4},{4,8},{8,12},{12,0},{1,5},{5,9},{9,13},{13,1},{2,6},{6,10},{... | collective-permute-start | bytes 393224 | tf_op jit(solution)/shard_map/ppermute | solution.py:264
  91.5 0.3 collective-permute-start.16
  91.9 3.8 %temporal_chunk.7 = (bf16[2,128,256]{2,1,0:T(8,128)(2,1)}, bf16[2,128,256]{2,1,0:T(8,128)(2,1)}, bf16[2,128,256]{2,1,0:T(8,128)(2,1)}, bf16[2,128,256]{2,1,0:T(8,128)(2,1)}) custom-call(bf16[4,128,256]{2,1,0:T(8,128)(2,1)S(1)} %copy-done.9, bf16[4,128,256]{2,1,0:T(8,128)(2,1)S(1)} %copy-done.8, bf16[4,128,256]{2,1,0:T(8,128)(2,1)S(1)} %collective-permute-done.6.refs_2_, ...), custom_call_target="tpu_custom_call" | custom-call | flops 1610612736 | bytes 2621440 | tf_op jit(solution)/shard_map/temporal_chunk/pallas_call | solution.py:235
  95.6 3.8 %temporal_chunk.6 = (bf16[2,128,256]{2,1,0:T(8,128)(2,1)}, bf16[2,128,256]{2,1,0:T(8,128)(2,1)}, bf16[2,128,256]{2,1,0:T(8,128)(2,1)}, bf16[2,128,256]{2,1,0:T(8,128)(2,1)}) custom-call(bf16[4,128,256]{2,1,0:T(8,128)(2,1)S(1)} %copy-done.9, bf16[4,128,256]{2,1,0:T(8,128)(2,1)S(1)} %copy-done.8, bf16[4,128,256]{2,1,0:T(8,128)(2,1)S(1)} %collective-permute-done.6.refs_2_, ...), custom_call_target="tpu_custom_call" | custom-call | flops 1610612736 | bytes 2621440 | tf_op jit(solution)/shard_map/temporal_chunk/pallas_call | solution.py:235
  99.5 0.1 broadcast_in_dim.3
  99.6 0.7 copy-done.19
  100.3 0.0 copy-done.27
  100.4 3.0 %collective-permute-start.17 = (bf16[2,128,256]{2,1,0:T(8,128)(2,1)S(1)}, bf16[2,128,256]{2,1,0:T(8,128)(2,1)S(1)}, u32[]{:S(2)}, u32[]{:S(2)}) collective-permute-start(bf16[2,128,256]{2,1,0:T(8,128)(2,1)S(1)} %copy-done.27), channel_id=1, source_target_pairs={{0,12},{4,0},{8,4},{12,8},{1,13},{5,1},{9,5},{13,9},{2,14},{6,2},{... | collective-permute-start | bytes 393224 | tf_op jit(solution)/shard_map/ppermute | solution.py:264
  103.4 0.0 collective-permute-done.13
  103.4 0.1 collective-permute-start.18
  103.5 1.7 %collective-permute-start.19 = (bf16[2,128,256]{2,1,0:T(8,128)(2,1)S(1)}, bf16[2,128,256]{2,1,0:T(8,128)(2,1)S(1)}, u32[]{:S(2)}, u32[]{:S(2)}) collective-permute-start(bf16[2,128,256]{2,1,0:T(8,128)(2,1)S(1)} %copy-done.25), channel_id=1, source_target_pairs={{0,8},{4,12},{8,0},{12,4},{1,9},{5,13},{9,1},{13,5},{2,10},{6,14},... | collective-permute-start | bytes 393224 | tf_op jit(solution)/shard_map/ppermute | solution.py:264
  105.3 2.2 %collective-permute-start.20 = (bf16[2,128,256]{2,1,0:T(8,128)(2,1)S(1)}, bf16[2,128,256]{2,1,0:T(8,128)(2,1)S(1)}, u32[]{:S(2)}, u32[]{:S(2)}) collective-permute-start(bf16[2,128,256]{2,1,0:T(8,128)(2,1)S(1)} %copy-done.24), channel_id=1, source_target_pairs={{0,12},{4,0},{8,4},{12,8},{1,13},{5,1},{9,5},{13,9},{2,14},{6,2},{... | collective-permute-start | bytes 393224 | tf_op jit(solution)/shard_map/ppermute | solution.py:264
  107.6 0.6 collective-permute-start.21
  108.2 3.7 %collective-permute-done.17 = bf16[2,128,256]{2,1,0:T(8,128)(2,1)S(1)} collective-permute-done((bf16[2,128,256]{2,1,0:T(8,128)(2,1)S(1)}, bf16[2,128,256]{2,1,0:T(8,128)(2,1)S(1)}, u32[]{:S(2)}, u32[]{:S(2)}) %collective-permute-start.17) | collective-permute-done | bytes 131104 | tf_op jit(solution)/shard_map/ppermute | solution.py:264
  111.9 2.7 %collective-permute-start.22 = (bf16[2,128,256]{2,1,0:T(8,128)(2,1)S(1)}, bf16[2,128,256]{2,1,0:T(8,128)(2,1)S(1)}, u32[]{:S(2)}, u32[]{:S(2)}) collective-permute-start(bf16[2,128,256]{2,1,0:T(8,128)(2,1)S(1)} %copy-done.22), channel_id=1, source_target_pairs={{0,8},{4,12},{8,0},{12,4},{1,9},{5,13},{9,1},{13,5},{2,10},{6,14},... | collective-permute-start | bytes 393224 | tf_op jit(solution)/shard_map/ppermute | solution.py:264
  114.7 0.0 collective-permute-done.18
  114.7 3.7 %collective-permute-start.23 = (bf16[2,128,256]{2,1,0:T(8,128)(2,1)S(1)}, bf16[2,128,256]{2,1,0:T(8,128)(2,1)S(1)}, u32[]{:S(2)}, u32[]{:S(2)}) collective-permute-start(bf16[2,128,256]{2,1,0:T(8,128)(2,1)S(1)} %copy-done.21), channel_id=1, source_target_pairs={{0,12},{4,0},{8,4},{12,8},{1,13},{5,1},{9,5},{13,9},{2,14},{6,2},{... | collective-permute-start | bytes 393224 | tf_op jit(solution)/shard_map/ppermute | solution.py:264
  118.4 4.7 %collective-permute-done.19 = bf16[2,128,256]{2,1,0:T(8,128)(2,1)S(1)} collective-permute-done((bf16[2,128,256]{2,1,0:T(8,128)(2,1)S(1)}, bf16[2,128,256]{2,1,0:T(8,128)(2,1)S(1)}, u32[]{:S(2)}, u32[]{:S(2)}) %collective-permute-start.19) | collective-permute-done | bytes 131104 | tf_op jit(solution)/shard_map/ppermute | solution.py:264
  123.2 0.0 collective-permute-done.20
  123.3 5.5 %collective-permute-done.22 = bf16[2,128,256]{2,1,0:T(8,128)(2,1)S(1)} collective-permute-done((bf16[2,128,256]{2,1,0:T(8,128)(2,1)S(1)}, bf16[2,128,256]{2,1,0:T(8,128)(2,1)S(1)}, u32[]{:S(2)}, u32[]{:S(2)}) %collective-permute-start.22) | collective-permute-done | bytes 131104 | tf_op jit(solution)/shard_map/ppermute | solution.py:264
  128.8 0.0 copy-start.11
  128.8 0.0 collective-permute-done.23
  128.8 1.3 copy-done.11
  130.1 0.7 constant_dynamic-update-slice_fusion
  (72 shorter events, 0.4 us)
Async XLA Ops:
  0.0 19.8 %copy-start.5 = (s32[2,64,4]{1,2,0:T(4,128)S(1)}, s32[2,64,4]{1,2,0:T(4,128)}, u32[]{:S(2)}) copy-start(s32[2,64,4]{1,2,0:T(4,128)} %param.14) | copy-start | bytes 6148
  0.0 19.8 %copy-start = (bf16[2,2048,256]{2,1,0:T(8,128)(2,1)S(1)}, bf16[2,2048,256]{2,1,0:T(8,128)(2,1)}, u32[]{:S(2)}) copy-start(bf16[2,2048,256]{2,1,0:T(8,128)(2,1)} %param.12) | copy-start | bytes 6291460
  4.1 5.2 %collective-permute-start.3 = (bf16[4,128,256]{2,1,0:T(8,128)(2,1)}, bf16[4,128,256]{2,1,0:T(8,128)(2,1)S(1)}, u32[]{:S(2)}, u32[]{:S(2)}) collective-permute-start(bf16[4,128,256]{2,1,0:T(8,128)(2,1)} %get-tuple-element.39), channel_id=1, source_target_pairs={{0,1},{1,0},{2,3},{3,2},{4,5},{5,4},{6,7},{7,6},{8,9},{9,8},{10,11... | collective-permute-start | bytes 786440 | tf_op jit(solution)/shard_map/ppermute | solution.py:332
  4.6 9.9 %collective-permute-start.4 = (bf16[4,128,256]{2,1,0:T(8,128)(2,1)}, bf16[4,128,256]{2,1,0:T(8,128)(2,1)S(1)}, u32[]{:S(2)}, u32[]{:S(2)}) collective-permute-start(bf16[4,128,256]{2,1,0:T(8,128)(2,1)} %get-tuple-element.40), channel_id=1, source_target_pairs={{0,2},{1,3},{2,0},{3,1},{4,6},{5,7},{6,4},{7,5},{8,10},{9,11},{10,... | collective-permute-start | bytes 786440 | tf_op jit(solution)/shard_map/ppermute | solution.py:332
  7.2 12.6 %collective-permute-start.5 = (bf16[4,128,256]{2,1,0:T(8,128)(2,1)}, bf16[4,128,256]{2,1,0:T(8,128)(2,1)S(1)}, u32[]{:S(2)}, u32[]{:S(2)}) collective-permute-start(bf16[4,128,256]{2,1,0:T(8,128)(2,1)} %get-tuple-element.41), channel_id=1, source_target_pairs={{0,3},{1,2},{2,1},{3,0},{4,7},{5,6},{6,5},{7,4},{8,11},{9,10},{10,... | collective-permute-start | bytes 786440 | tf_op jit(solution)/shard_map/ppermute | solution.py:332
  7.3 26.7 %collective-permute-start = (bf16[4,128,256]{2,1,0:T(8,128)(2,1)}, bf16[4,128,256]{2,1,0:T(8,128)(2,1)S(1)}, u32[]{:S(2)}, u32[]{:S(2)}) collective-permute-start(bf16[4,128,256]{2,1,0:T(8,128)(2,1)} %get-tuple-element.35), channel_id=1, source_target_pairs={{0,1},{1,0},{2,3},{3,2},{4,5},{5,4},{6,7},{7,6},{8,9},{9,8},{10,11... | collective-permute-start | bytes 786440 | tf_op jit(solution)/shard_map/ppermute | solution.py:332
  7.4 27.5 %collective-permute-start.1 = (bf16[4,128,256]{2,1,0:T(8,128)(2,1)}, bf16[4,128,256]{2,1,0:T(8,128)(2,1)S(1)}, u32[]{:S(2)}, u32[]{:S(2)}) collective-permute-start(bf16[4,128,256]{2,1,0:T(8,128)(2,1)} %get-tuple-element.36), channel_id=1, source_target_pairs={{0,2},{1,3},{2,0},{3,1},{4,6},{5,7},{6,4},{7,5},{8,10},{9,11},{10,... | collective-permute-start | bytes 786440 | tf_op jit(solution)/shard_map/ppermute | solution.py:332
  9.3 25.6 %collective-permute-start.2 = (bf16[4,128,256]{2,1,0:T(8,128)(2,1)}, bf16[4,128,256]{2,1,0:T(8,128)(2,1)S(1)}, u32[]{:S(2)}, u32[]{:S(2)}) collective-permute-start(bf16[4,128,256]{2,1,0:T(8,128)(2,1)} %get-tuple-element.37), channel_id=1, source_target_pairs={{0,3},{1,2},{2,1},{3,0},{4,7},{5,6},{6,5},{7,4},{8,11},{9,10},{10,... | collective-permute-start | bytes 786440 | tf_op jit(solution)/shard_map/ppermute | solution.py:332
  19.8 2.2 %copy-start.1 = (bf16[2,16,4,128,128]{4,3,2,1,0:T(8,128)(2,1)S(1)}, bf16[2,16,4,128,128]{4,3,2,1,0:T(8,128)(2,1)}, u32[]{:S(2)}) copy-start(bf16[2,16,4,128,128]{4,3,2,1,0:T(8,128)(2,1)} %refs_3_.3) | copy-start | bytes 12582916
  22.0 0.9 copy-start.3
  22.9 7.3 %copy-start.14 = (bf16[256,256]{1,0:T(8,128)(2,1)S(1)}, bf16[256,256]{1,0:T(8,128)(2,1)}, u32[]{:S(2)}) copy-start(bf16[256,256]{1,0:T(8,128)(2,1)} %param.19) | copy-start | bytes 393220
  22.9 8.0 %copy-start.15 = (bf16[256,256]{1,0:T(8,128)(2,1)S(1)}, bf16[256,256]{1,0:T(8,128)(2,1)}, u32[]{:S(2)}) copy-start(bf16[256,256]{1,0:T(8,128)(2,1)} %param.18) | copy-start | bytes 393220
  22.9 10.9 %copy-start.20 = (bf16[8,256]{1,0:T(8,128)(2,1)S(1)}, bf16[8,256]{1,0:T(8,128)(2,1)}, u32[]{:S(2)}) copy-start(bf16[8,256]{1,0:T(8,128)(2,1)} %param.16) | copy-start | bytes 12292
  22.9 12.1 %copy-start.4 = (bf16[256,256]{1,0:T(8,128)(2,1)S(1)}, bf16[256,256]{1,0:T(8,128)(2,1)}, u32[]{:S(2)}) copy-start(bf16[256,256]{1,0:T(8,128)(2,1)} %refs_4_.3) | copy-start | bytes 393220
  26.5 17.7 %collective-permute-start.11 = (bf16[4,128,256]{2,1,0:T(8,128)(2,1)}, bf16[4,128,256]{2,1,0:T(8,128)(2,1)S(1)}, u32[]{:S(2)}, u32[]{:S(2)}) collective-permute-start(bf16[4,128,256]{2,1,0:T(8,128)(2,1)} %get-tuple-element.48), channel_id=1, source_target_pairs={{0,12},{4,0},{8,4},{12,8},{1,13},{5,1},{9,5},{13,9},{2,14},{6,2},{... | collective-permute-start | bytes 786440 | tf_op jit(solution)/shard_map/ppermute | solution.py:264
  33.9 12.0 %collective-permute-start.7 = (bf16[4,128,256]{2,1,0:T(8,128)(2,1)}, bf16[4,128,256]{2,1,0:T(8,128)(2,1)S(1)}, u32[]{:S(2)}, u32[]{:S(2)}) collective-permute-start(bf16[4,128,256]{2,1,0:T(8,128)(2,1)} %get-tuple-element.44), channel_id=1, source_target_pairs={{0,4},{4,8},{8,12},{12,0},{1,5},{5,9},{9,13},{13,1},{2,6},{6,10},{... | collective-permute-start | bytes 786440 | tf_op jit(solution)/shard_map/ppermute | solution.py:264
  33.9 21.7 %collective-permute-start.9 = (bf16[4,128,256]{2,1,0:T(8,128)(2,1)}, bf16[4,128,256]{2,1,0:T(8,128)(2,1)S(1)}, u32[]{:S(2)}, u32[]{:S(2)}) collective-permute-start(bf16[4,128,256]{2,1,0:T(8,128)(2,1)} %get-tuple-element.46), channel_id=1, source_target_pairs={{0,8},{4,12},{8,0},{12,4},{1,9},{5,13},{9,1},{13,5},{2,10},{6,14},... | collective-permute-start | bytes 786440 | tf_op jit(solution)/shard_map/ppermute | solution.py:264
  34.9 2.2 %copy-start.2 = (bf16[2,16,4,128,128]{4,3,2,1,0:T(8,128)(2,1)S(1)}, bf16[2,16,4,128,128]{4,3,2,1,0:T(8,128)(2,1)}, u32[]{:S(2)}) copy-start(bf16[2,16,4,128,128]{4,3,2,1,0:T(8,128)(2,1)} %refs_3_.3) | copy-start | bytes 12582916
  37.1 8.5 %copy-start.12 = (bf16[256,256]{0,1:T(8,128)(2,1)S(1)}, bf16[256,256]{0,1:T(8,128)(2,1)}, u32[]{:S(2)}) copy-start(bf16[256,256]{0,1:T(8,128)(2,1)} %copy.21) | copy-start | bytes 393220
  37.1 8.5 %copy-start.13 = (bf16[256,256]{0,1:T(8,128)(2,1)S(1)}, bf16[256,256]{0,1:T(8,128)(2,1)}, u32[]{:S(2)}) copy-start(bf16[256,256]{0,1:T(8,128)(2,1)} %copy.19) | copy-start | bytes 393220
  37.1 40.4 %copy-start.6 = (bf16[256,1024]{1,0:T(8,128)(2,1)S(1)}, bf16[256,1024]{1,0:T(8,128)(2,1)}, u32[]{:S(2)}) copy-start(bf16[256,1024]{1,0:T(8,128)(2,1)} %refs_11_.7) | copy-start | bytes 1572868
  37.1 40.4 %copy-start.7 = (bf16[1024,256]{1,0:T(8,128)(2,1)S(1)}, bf16[1024,256]{1,0:T(8,128)(2,1)}, u32[]{:S(2)}) copy-start(bf16[1024,256]{1,0:T(8,128)(2,1)} %refs_13_.7) | copy-start | bytes 1572868
  37.1 40.4 %copy-start.8 = (bf16[4,128,256]{2,1,0:T(8,128)(2,1)S(1)}, bf16[4,128,256]{2,1,0:T(8,128)(2,1)}, u32[]{:S(2)}) copy-start(bf16[4,128,256]{2,1,0:T(8,128)(2,1)} %get-tuple-element.42.refs_1_) | copy-start | bytes 786436
  37.2 40.4 %copy-start.10 = (f32[1024]{0:T(1024)S(1)}, f32[1024]{0:T(1024)}, u32[]{:S(2)}) copy-start(f32[1024]{0:T(1024)} %param.22) | copy-start | bytes 12292
  40.8 14.8 %collective-permute-start.10 = (bf16[4,128,256]{2,1,0:T(8,128)(2,1)}, bf16[4,128,256]{2,1,0:T(8,128)(2,1)S(1)}, u32[]{:S(2)}, u32[]{:S(2)}) collective-permute-start(bf16[4,128,256]{2,1,0:T(8,128)(2,1)} %get-tuple-element.47), channel_id=1, source_target_pairs={{0,12},{4,0},{8,4},{12,8},{1,13},{5,1},{9,5},{13,9},{2,14},{6,2},{... | collective-permute-start | bytes 786440 | tf_op jit(solution)/shard_map/ppermute | solution.py:264
  43.6 18.4 %collective-permute-start.6 = (bf16[4,128,256]{2,1,0:T(8,128)(2,1)}, bf16[4,128,256]{2,1,0:T(8,128)(2,1)S(1)}, u32[]{:S(2)}, u32[]{:S(2)}) collective-permute-start(bf16[4,128,256]{2,1,0:T(8,128)(2,1)} %get-tuple-element.43), channel_id=1, source_target_pairs={{0,4},{4,8},{8,12},{12,0},{1,5},{5,9},{9,13},{13,1},{2,6},{6,10},{... | collective-permute-start | bytes 786440 | tf_op jit(solution)/shard_map/ppermute | solution.py:264
  44.2 33.3 %collective-permute-start.8 = (bf16[4,128,256]{2,1,0:T(8,128)(2,1)}, bf16[4,128,256]{2,1,0:T(8,128)(2,1)S(1)}, u32[]{:S(2)}, u32[]{:S(2)}) collective-permute-start(bf16[4,128,256]{2,1,0:T(8,128)(2,1)} %get-tuple-element.45), channel_id=1, source_target_pairs={{0,8},{4,12},{8,0},{12,4},{1,9},{5,13},{9,1},{13,5},{2,10},{6,14},... | collective-permute-start | bytes 786440 | tf_op jit(solution)/shard_map/ppermute | solution.py:264
  77.5 1.0 copy-start.9
  82.2 18.1 %collective-permute-start.12 = (bf16[2,128,256]{2,1,0:T(8,128)(2,1)}, bf16[2,128,256]{2,1,0:T(8,128)(2,1)S(1)}, u32[]{:S(2)}, u32[]{:S(2)}) collective-permute-start(bf16[2,128,256]{2,1,0:T(8,128)(2,1)} %get-tuple-element.50), channel_id=1, source_target_pairs={{0,4},{4,8},{8,12},{12,0},{1,5},{5,9},{9,13},{13,1},{2,6},{6,10},{... | collective-permute-start | bytes 393224 | tf_op jit(solution)/shard_map/ppermute | solution.py:264
  82.4 20.9 %collective-permute-start.13 = (bf16[2,128,256]{2,1,0:T(8,128)(2,1)}, bf16[2,128,256]{2,1,0:T(8,128)(2,1)S(1)}, u32[]{:S(2)}, u32[]{:S(2)}) collective-permute-start(bf16[2,128,256]{2,1,0:T(8,128)(2,1)} %get-tuple-element.51), channel_id=1, source_target_pairs={{0,8},{4,12},{8,0},{12,4},{1,9},{5,13},{9,1},{13,5},{2,10},{6,14},... | collective-permute-start | bytes 393224 | tf_op jit(solution)/shard_map/ppermute | solution.py:264
  85.8 17.7 %collective-permute-start.14 = (bf16[2,128,256]{2,1,0:T(8,128)(2,1)}, bf16[2,128,256]{2,1,0:T(8,128)(2,1)S(1)}, u32[]{:S(2)}, u32[]{:S(2)}) collective-permute-start(bf16[2,128,256]{2,1,0:T(8,128)(2,1)} %get-tuple-element.52), channel_id=1, source_target_pairs={{0,12},{4,0},{8,4},{12,8},{1,13},{5,1},{9,5},{13,9},{2,14},{6,2},{... | collective-permute-start | bytes 393224 | tf_op jit(solution)/shard_map/ppermute | solution.py:264
  89.8 15.5 %collective-permute-start.15 = (bf16[2,128,256]{2,1,0:T(8,128)(2,1)}, bf16[2,128,256]{2,1,0:T(8,128)(2,1)S(1)}, u32[]{:S(2)}, u32[]{:S(2)}) collective-permute-start(bf16[2,128,256]{2,1,0:T(8,128)(2,1)} %get-tuple-element.54), channel_id=1, source_target_pairs={{0,4},{4,8},{8,12},{12,0},{1,5},{5,9},{9,13},{13,1},{2,6},{6,10},{... | collective-permute-start | bytes 393224 | tf_op jit(solution)/shard_map/ppermute | solution.py:264
  91.5 16.0 %collective-permute-start.16 = (bf16[2,128,256]{2,1,0:T(8,128)(2,1)}, bf16[2,128,256]{2,1,0:T(8,128)(2,1)S(1)}, u32[]{:S(2)}, u32[]{:S(2)}) collective-permute-start(bf16[2,128,256]{2,1,0:T(8,128)(2,1)} %get-tuple-element.55), channel_id=1, source_target_pairs={{0,8},{4,12},{8,0},{12,4},{1,9},{5,13},{9,1},{13,5},{2,10},{6,14},... | collective-permute-start | bytes 393224 | tf_op jit(solution)/shard_map/ppermute | solution.py:264
  99.4 0.9 copy-start.19
  99.4 1.0 copy-start.27
  99.4 4.0 %copy-start.26 = (bf16[2,128,256]{2,1,0:T(8,128)(2,1)S(1)}, bf16[2,128,256]{2,1,0:T(8,128)(2,1)}, u32[]{:S(2)}) copy-start(bf16[2,128,256]{2,1,0:T(8,128)(2,1)} %get-tuple-element.58) | copy-start | bytes 393220
  99.4 4.1 %copy-start.25 = (bf16[2,128,256]{2,1,0:T(8,128)(2,1)S(1)}, bf16[2,128,256]{2,1,0:T(8,128)(2,1)}, u32[]{:S(2)}) copy-start(bf16[2,128,256]{2,1,0:T(8,128)(2,1)} %get-tuple-element.59) | copy-start | bytes 393220
  99.4 5.8 %copy-start.18 = (bf16[2,128,256]{2,1,0:T(8,128)(2,1)S(1)}, bf16[2,128,256]{2,1,0:T(8,128)(2,1)}, u32[]{:S(2)}) copy-start(bf16[2,128,256]{2,1,0:T(8,128)(2,1)} %get-tuple-element.53) | copy-start | bytes 393220
  99.4 5.9 %copy-start.24 = (bf16[2,128,256]{2,1,0:T(8,128)(2,1)S(1)}, bf16[2,128,256]{2,1,0:T(8,128)(2,1)}, u32[]{:S(2)}) copy-start(bf16[2,128,256]{2,1,0:T(8,128)(2,1)} %get-tuple-element.60) | copy-start | bytes 393220
  99.4 8.1 %copy-start.23 = (bf16[2,128,256]{2,1,0:T(8,128)(2,1)S(1)}, bf16[2,128,256]{2,1,0:T(8,128)(2,1)}, u32[]{:S(2)}) copy-start(bf16[2,128,256]{2,1,0:T(8,128)(2,1)} %get-tuple-element.62) | copy-start | bytes 393220
  99.4 12.5 %copy-start.22 = (bf16[2,128,256]{2,1,0:T(8,128)(2,1)S(1)}, bf16[2,128,256]{2,1,0:T(8,128)(2,1)}, u32[]{:S(2)}) copy-start(bf16[2,128,256]{2,1,0:T(8,128)(2,1)} %get-tuple-element.63) | copy-start | bytes 393220
  99.4 15.2 %copy-start.17 = (bf16[2,128,256]{2,1,0:T(8,128)(2,1)S(1)}, bf16[2,128,256]{2,1,0:T(8,128)(2,1)}, u32[]{:S(2)}) copy-start(bf16[2,128,256]{2,1,0:T(8,128)(2,1)} %get-tuple-element.57) | copy-start | bytes 393220
  99.5 15.2 %copy-start.21 = (bf16[2,128,256]{2,1,0:T(8,128)(2,1)S(1)}, bf16[2,128,256]{2,1,0:T(8,128)(2,1)}, u32[]{:S(2)}) copy-start(bf16[2,128,256]{2,1,0:T(8,128)(2,1)} %get-tuple-element.64) | copy-start | bytes 393220
  100.3 22.9 %copy-start.16 = (bf16[2,128,256]{2,1,0:T(8,128)(2,1)S(1)}, bf16[2,128,256]{2,1,0:T(8,128)(2,1)}, u32[]{:S(2)}) copy-start(bf16[2,128,256]{2,1,0:T(8,128)(2,1)} %get-tuple-element.61) | copy-start | bytes 393220
  100.4 11.6 %collective-permute-start.17 = (bf16[2,128,256]{2,1,0:T(8,128)(2,1)S(1)}, bf16[2,128,256]{2,1,0:T(8,128)(2,1)S(1)}, u32[]{:S(2)}, u32[]{:S(2)}) collective-permute-start(bf16[2,128,256]{2,1,0:T(8,128)(2,1)S(1)} %copy-done.27), channel_id=1, source_target_pairs={{0,12},{4,0},{8,4},{12,8},{1,13},{5,1},{9,5},{13,9},{2,14},{6,2},{... | collective-permute-start | bytes 393224 | tf_op jit(solution)/shard_map/ppermute | solution.py:264
  103.4 11.3 %collective-permute-start.18 = (bf16[2,128,256]{2,1,0:T(8,128)(2,1)S(1)}, bf16[2,128,256]{2,1,0:T(8,128)(2,1)S(1)}, u32[]{:S(2)}, u32[]{:S(2)}) collective-permute-start(bf16[2,128,256]{2,1,0:T(8,128)(2,1)S(1)} %copy-done.26), channel_id=1, source_target_pairs={{0,4},{4,8},{8,12},{12,0},{1,5},{5,9},{9,13},{13,1},{2,6},{6,10},{... | collective-permute-start | bytes 393224 | tf_op jit(solution)/shard_map/ppermute | solution.py:264
  103.5 19.7 %collective-permute-start.19 = (bf16[2,128,256]{2,1,0:T(8,128)(2,1)S(1)}, bf16[2,128,256]{2,1,0:T(8,128)(2,1)S(1)}, u32[]{:S(2)}, u32[]{:S(2)}) collective-permute-start(bf16[2,128,256]{2,1,0:T(8,128)(2,1)S(1)} %copy-done.25), channel_id=1, source_target_pairs={{0,8},{4,12},{8,0},{12,4},{1,9},{5,13},{9,1},{13,5},{2,10},{6,14},... | collective-permute-start | bytes 393224 | tf_op jit(solution)/shard_map/ppermute | solution.py:264
  105.3 17.9 %collective-permute-start.20 = (bf16[2,128,256]{2,1,0:T(8,128)(2,1)S(1)}, bf16[2,128,256]{2,1,0:T(8,128)(2,1)S(1)}, u32[]{:S(2)}, u32[]{:S(2)}) collective-permute-start(bf16[2,128,256]{2,1,0:T(8,128)(2,1)S(1)} %copy-done.24), channel_id=1, source_target_pairs={{0,12},{4,0},{8,4},{12,8},{1,13},{5,1},{9,5},{13,9},{2,14},{6,2},{... | collective-permute-start | bytes 393224 | tf_op jit(solution)/shard_map/ppermute | solution.py:264
  107.6 15.7 %collective-permute-start.21 = (bf16[2,128,256]{2,1,0:T(8,128)(2,1)S(1)}, bf16[2,128,256]{2,1,0:T(8,128)(2,1)S(1)}, u32[]{:S(2)}, u32[]{:S(2)}) collective-permute-start(bf16[2,128,256]{2,1,0:T(8,128)(2,1)S(1)} %copy-done.23), channel_id=1, source_target_pairs={{0,4},{4,8},{8,12},{12,0},{1,5},{5,9},{9,13},{13,1},{2,6},{6,10},{... | collective-permute-start | bytes 393224 | tf_op jit(solution)/shard_map/ppermute | solution.py:264
  111.9 16.9 %collective-permute-start.22 = (bf16[2,128,256]{2,1,0:T(8,128)(2,1)S(1)}, bf16[2,128,256]{2,1,0:T(8,128)(2,1)S(1)}, u32[]{:S(2)}, u32[]{:S(2)}) collective-permute-start(bf16[2,128,256]{2,1,0:T(8,128)(2,1)S(1)} %copy-done.22), channel_id=1, source_target_pairs={{0,8},{4,12},{8,0},{12,4},{1,9},{5,13},{9,1},{13,5},{2,10},{6,14},... | collective-permute-start | bytes 393224 | tf_op jit(solution)/shard_map/ppermute | solution.py:264
  114.7 14.1 %collective-permute-start.23 = (bf16[2,128,256]{2,1,0:T(8,128)(2,1)S(1)}, bf16[2,128,256]{2,1,0:T(8,128)(2,1)S(1)}, u32[]{:S(2)}, u32[]{:S(2)}) collective-permute-start(bf16[2,128,256]{2,1,0:T(8,128)(2,1)S(1)} %copy-done.21), channel_id=1, source_target_pairs={{0,12},{4,0},{8,4},{12,8},{1,13},{5,1},{9,5},{13,9},{2,14},{6,2},{... | collective-permute-start | bytes 393224 | tf_op jit(solution)/shard_map/ppermute | solution.py:264
  128.8 1.3 %copy-start.11 = (bf16[2,2048,256]{2,1,0:T(8,128)(2,1)}, bf16[2,2048,256]{2,1,0:T(8,128)(2,1)S(1)}, u32[]{:S(2)}) copy-start(bf16[2,2048,256]{2,1,0:T(8,128)(2,1)S(1)} %constant_dynamic-update-slice_fusion.1) | copy-start | bytes 6291460

commit v2 on v0

v2 whole, which is shorter than its diff:
```python
import functools
import math

import jax
import jax.numpy as jnp
from jax import lax
from jax.experimental import pallas as pl
from jax.experimental.pallas import tpu as pltpu
from jax.sharding import PartitionSpec as P

HEADS = 8
LANES = 128
ALONE, ROOM = 60, (57, 46)
GATHER_US, GATE_US, NEAR_US, FAR_US, TEMPORAL_US, PLACE_US = 3, 0.5, 3, 2, 3, 1
NEG = -1e30
F32 = jnp.float32
BF16 = jnp.bfloat16


def cost(us):
    return pl.CostEstimate(flops=0, bytes_accessed=int(us * 3.0e4), transcendentals=0)


def dot(a, b):
    return jnp.dot(a, b, preferred_element_type=F32)


def partner(me, d, n):
    return me ^ d if n & (n - 1) == 0 else (me + d) % n


def came_from(me, d, n):
    return me ^ d if n & (n - 1) == 0 else (me + n - d) % n


def named_mask(nbr_ref, t, first, cluster, blk_cl):
    last = nbr_ref.shape[1] - 1
    mask = jnp.int32(0)
    for i in range(blk_cl):
        g = nbr_ref[t, last, first + i] - cluster * blk_cl
        mask |= jnp.where((g >= 0) & (g < blk_cl), jnp.left_shift(1, g & 31), 0)
    return mask


def gather_kernel(t, most, n_clus, after_ref, nbr_ref, feat_ref, *refs):
    blk_cl = feat_ref.shape[1]
    outs, done_ref, sems = refs[:-2], refs[-2], refs[-1]
    done_ref[0] = jnp.int32(0)
    me = lax.axis_index("clus")
    copies = []
    for d in range(1, n_clus):
        mask = named_mask(nbr_ref, t, partner(me, d, n_clus) * blk_cl, me, blk_cl)
        picked = [jnp.int32(0)] * most
        count = jnp.int32(0)
        for b in range(blk_cl):
            bit = jnp.right_shift(mask, b) & 1
            for j in range(most):
                picked[j] = jnp.where((bit == 1) & (count == j), b, picked[j])
            count += bit
        for j in range(most):
            copy = pltpu.make_async_copy(
                feat_ref.at[t, picked[j]], outs[d - 1].at[j], sems.at[d - 1, j]
            )
            copy.start()
            copies.append(copy)
    for copy in copies:
        copy.wait()


def gather_blocks(after, nbr, feat, t, most, n_clus):
    _, _, block, width = feat.shape
    shape = (most, block, width)
    *out, done = pl.pallas_call(
        functools.partial(gather_kernel, t, most, n_clus),
        grid=(1,),
        out_shape=[pltpu.HBM(shape, BF16)] * (n_clus - 1)
        + [jax.ShapeDtypeStruct((1,), jnp.int32)],
        in_specs=[
            pl.BlockSpec(memory_space=pltpu.SMEM),
            pl.BlockSpec(memory_space=pltpu.SMEM),
            pl.BlockSpec(memory_space=pltpu.HBM),
        ],
        out_specs=[pl.BlockSpec(shape, lambda g: (0, 0, 0))] * (n_clus - 1)
        + [pl.BlockSpec(memory_space=pltpu.SMEM)],
        scratch_shapes=[pltpu.SemaphoreType.DMA((n_clus - 1, most))],
        compiler_params=pltpu.CompilerParams(vmem_limit_bytes=ALONE << 20),
        cost_estimate=cost(GATHER_US),
        name="gather_blocks",
    )(after, nbr, feat)
    return out, done


def gate_kernel(*refs):
    pass


def gate(after, xs):
    hbm = pl.BlockSpec(memory_space=pltpu.HBM)
    return pl.pallas_call(
        gate_kernel,
        out_shape=[pltpu.HBM(x.shape, x.dtype) for x in xs],
        in_specs=[pl.BlockSpec(memory_space=pl.ANY)] * len(after) + [hbm] * len(xs),
        out_specs=[hbm] * len(xs),
        input_output_aliases={i + len(after): i for i in range(len(xs))},
        compiler_params=pltpu.CompilerParams(vmem_limit_bytes=1 << 20),
        cost_estimate=cost(GATE_US),
        name="gate",
    )(*after, *xs)


def near_kernel(
    t, n_clus, most, after_ref, nbr_ref, feat_ref, adj_ref, w_ref, acc_ref, own, tiles, slots, table, sems
):
    my_clus = lax.axis_index("clus")
    blk_cl, block, width = own.shape
    nbr_k = tiles.shape[1]
    pieces = sems.shape[1]
    rows = blk_cl // pieces
    first = my_clus * blk_cl
    copies = []
    for source, target in ((feat_ref, own), (adj_ref, tiles)):
        for i in range(pieces):
            some = pl.ds(i * rows, rows)
            copies.append(
                pltpu.make_async_copy(
                    source.at[t, some], target.at[some], sems.at[len(copies) // pieces, i]
                )
            )
            copies[-1].start()
    for i in range(blk_cl):
        slots[i] = (n_clus - 1) * most
    for d in range(1, n_clus):
        other = came_from(my_clus, d, n_clus)
        mask = named_mask(nbr_ref, t, first, other, blk_cl)
        for i in range(blk_cl):
            b = nbr_ref[t, nbr_k - 1, first + i] - other * blk_cl
            below = mask & (jnp.left_shift(1, b & 31) - 1)
            rank = jnp.int32(0)
            for _ in range(most):
                rank += jnp.where(below != 0, 1, 0)
                below &= below - 1
            slots[i] = jnp.where((b >= 0) & (b < blk_cl), (d - 1) * most + rank, slots[i])
    w = w_ref[...]
    for i in range(pieces):
        copies[i].wait()
        some = own[i * rows : (i + 1) * rows].reshape(rows * block, width)
        table[i * rows : (i + 1) * rows] = dot(some, w).astype(BF16).reshape(rows, block, width)
    table[blk_cl] = jnp.zeros((block, width), BF16)
    for row in range(blk_cl):
        if row % rows == 0:
            copies[pieces + row // rows].wait()
        where = [nbr_ref[t, k, first + row] - first for k in range(nbr_k)]
        where[-1] = jnp.where((where[-1] >= 0) & (where[-1] < blk_cl), where[-1], blk_cl)
        wide = jnp.concatenate([tiles[row, k] for k in range(nbr_k)], axis=1)
        acc_ref[row] = dot(wide, jnp.concatenate([table[slot] for slot in where], axis=0))


def near_sum(after, nbr, feat, adj, w, t, n_clus, most, room):
    _, blk_cl, block, width = feat.shape
    nbr_k = adj.shape[2]
    pieces = 4 if blk_cl % 4 == 0 else 1
    vmem = pl.BlockSpec(memory_space=pltpu.VMEM)
    smem = pl.BlockSpec(memory_space=pltpu.SMEM)
    hbm = pl.BlockSpec(memory_space=pltpu.HBM)
    return pl.pallas_call(
        functools.partial(near_kernel, t, n_clus, most),
        out_shape=[
            pltpu.VMEM((blk_cl, block, width), F32),
            pltpu.VMEM((blk_cl, block, width), BF16),
            pltpu.VMEM((blk_cl, nbr_k, block, block), BF16),
            jax.ShapeDtypeStruct((blk_cl,), jnp.int32),
        ],
        in_specs=[smem, smem, hbm, hbm, vmem],
        out_specs=[vmem, vmem, vmem, smem],
        scratch_shapes=[
            pltpu.VMEM((blk_cl + 1, block, width), BF16),
            pltpu.SemaphoreType.DMA((2, pieces)),
        ],
        compiler_params=pltpu.CompilerParams(vmem_limit_bytes=room << 20),
        cost_estimate=cost(NEAR_US),
        name="near_sum",
    )(after, nbr, feat, adj, w)


def far_kernel(n_snap, parts, slots, acc_ref, own, tiles, w_ref, *refs):
    n_out = n_snap * len(parts)
    remote, outs = refs[: -n_out - 4], refs[-n_out - 4 : -4]
    done_ref, table, held, sems = refs[-4:]
    done_ref[0] = jnp.int32(0)
    my_snap = lax.axis_index("snap") if n_snap > 1 else jnp.int32(0)
    most, block, width = remote[0].shape
    w = w_ref[...]
    for d, ref in enumerate(remote):
        some = dot(ref[...].reshape(most * block, width), w).astype(BF16)
        table[d * most : (d + 1) * most] = some.reshape(most, block, width)
    table[len(remote) * most] = jnp.zeros((block, width), BF16)
    copies = []
    for e, (lo, hi) in enumerate(parts):
        for d in list(range(1, n_snap)) + [0]:
            p = partner(my_snap, d, n_snap)
            for g in range(lo, hi):
                row = g * n_snap + p
                total = acc_ref[row] + dot(tiles[row, tiles.shape[1] - 1], table[slots[row]])
                total = (own[row].astype(F32) + jnp.maximum(total, 0.0)).astype(BF16)
                if d == 0:
                    outs[e * n_snap][g - lo] = total
                else:
                    held[d - 1, g] = total
            if d > 0:
                copies.append(
                    pltpu.make_async_copy(
                        held.at[d - 1, lo:hi], outs[e * n_snap + d], sems.at[e, d - 1]
                    )
                )
                copies[-1].start()
    for copy in copies:
        copy.wait()


def far_sum(near, remote, w, n_snap, parts):
    acc, own, tiles, slots = near
    most, block, width = remote[0].shape
    vmem = pl.BlockSpec(memory_space=pltpu.VMEM)
    hbm = pl.BlockSpec(memory_space=pltpu.HBM)
    shapes = [(hi - lo, block, width) for lo, hi in parts]
    *out, done = pl.pallas_call(
        functools.partial(far_kernel, n_snap, parts),
        out_shape=[
            (pltpu.HBM if d else pltpu.VMEM)(shape, BF16) for shape in shapes for d in range(n_snap)
        ]
        + [jax.ShapeDtypeStruct((1,), jnp.int32)],
        in_specs=[pl.BlockSpec(memory_space=pltpu.SMEM)] + [vmem] * (4 + len(remote)),
        out_specs=[hbm if d else vmem for _ in shapes for d in range(n_snap)]
        + [pl.BlockSpec(memory_space=pltpu.SMEM)],
        scratch_shapes=[
            pltpu.VMEM((len(remote) * most + 1, block, width), BF16),
            pltpu.VMEM((max(n_snap - 1, 1), parts[-1][1], block, width), BF16),
            pltpu.SemaphoreType.DMA((len(parts), max(n_snap - 1, 1))),
        ],
        compiler_params=pltpu.CompilerParams(vmem_limit_bytes=8 << 20),
        cost_estimate=cost(FAR_US),
        name="far_sum",
    )(slots, acc, own, tiles, w, *remote)
    return [out[e * n_snap : (e + 1) * n_snap] for e in range(len(parts))], done


def prepare_kernel(after_ref, pos_ref, wq_ref, wk_ref, wv_ref, wo_ref, pos, wqkv, wo):
    width = wo.shape[0]
    head_dim = width // HEADS
    to = lax.broadcasted_iota(jnp.int32, (width, width), 0)
    source = lax.broadcasted_iota(jnp.int32, (width, width), 1)
    named = (to & (HEADS - 1)) * head_dim + jnp.right_shift(to, HEADS.bit_length() - 1)
    order = jnp.where(source == named, 1.0, 0.0).astype(BF16)
    for i, ref in enumerate((wq_ref, wk_ref, wv_ref)):
        turned = lax.dot_general(
            order, ref[...], (((1,), (1,)), ((), ())), preferred_element_type=F32
        )
        wqkv[i * width : (i + 1) * width] = turned.astype(BF16)
    wo[...] = dot(order, wo_ref[...]).astype(BF16)
    pos[...] = pos_ref[...].astype(F32)


def prepare(after, pos, wq, wk, wv, wo):
    width = wo.shape[0]
    vmem = pl.BlockSpec(memory_space=pltpu.VMEM)
    return pl.pallas_call(
        prepare_kernel,
        out_shape=[
            pltpu.VMEM(pos.shape, F32),
            pltpu.VMEM((3 * width, width), BF16),
            pltpu.VMEM((width, width), BF16),
        ],
        in_specs=[pl.BlockSpec(memory_space=pltpu.SMEM)] + [vmem] * 5,
        out_specs=[vmem] * 3,
        compiler_params=pltpu.CompilerParams(vmem_limit_bytes=4 << 20),
        cost_estimate=cost(1),
        name="prepare",
    )(after, pos, wq, wk, wv, wo)


def temporal_kernel(n_snap, per, blocks, chunk, *refs):
    count = n_snap * per
    ins = refs[:count]
    pos_ref, wqkv_ref, wo_ref, wup_ref, bias_ref, wdown_ref = refs[count : count + 6]
    outs = refs[-5 - n_snap : -5]
    raw, zs, qkv, att, out_sems = refs[-5:]
    me = lax.axis_index("snap")
    nsnap, nvert, width = zs.shape
    head_dim = width // HEADS
    for d in range(n_snap):
        for j in range(per):
            i = d * per + j
            raw[came_from(me, d, n_snap) * per + j] = ins[i][blocks[i]]

    for t in range(nsnap):
        zs[t] = (raw[t].astype(F32) + pos_ref[t : t + 1, :]).astype(BF16)
        qkv[t] = (
            lax.dot_general(
                wqkv_ref[...], zs[t], (((1,), (1,)), ((), ())), preferred_element_type=F32
            )
            .astype(BF16)
            .astype(F32)
        )

    def part(which, t):
        return qkv[t, which * width : (which + 1) * width, :].reshape(head_dim, HEADS, nvert)

    for t in range(nsnap):
        q = part(0, t)
        scores = [
            jnp.sum(q * part(1, s), axis=0) * (1.0 / math.sqrt(head_dim)) for s in range(t + 1)
        ]
        peak = functools.reduce(jnp.maximum, scores)
        expo = [jnp.exp(x - peak) for x in scores]
        total = functools.reduce(jnp.add, expo)
        acc = None
        for s in range(t + 1):
            prob = (expo[s] / total).astype(BF16).astype(F32)
            term = prob[None] * part(2, s)
            acc = term if acc is None else acc + term
        att[t] = acc.reshape(width, nvert).astype(BF16)

    def send(d, first):
        target = outs[d]
        if d == 0:
            target = target.at[:, pl.ds((chunk * n_snap + me) * nvert, nvert)]
        return pltpu.make_async_copy(raw.at[pl.ds(first, per)], target, out_sems.at[d])

    for g in range(n_snap):
        some = slice(g * per, (g + 1) * per)
        z = zs[some].reshape(per * nvert, width)
        joined = jnp.concatenate([att[g * per + j] for j in range(per)], axis=1)
        mixed = z.astype(F32) + lax.dot_general(
            joined, wo_ref[...], (((0,), (0,)), ((), ())), preferred_element_type=F32
        )
        hidden = jnp.maximum(dot(mixed.astype(BF16), wup_ref[...]) + bias_ref[...], 0.0)
        out = mixed + dot(hidden.astype(BF16), wdown_ref[...])
        raw[some] = out.astype(BF16).reshape(per, nvert, width)
        for d in range(n_snap):

            @pl.when(partner(me, d, n_snap) == g)
            def _():
                send(d, g * per).start()

    for d in range(n_snap):
        send(d, partner(me, d, n_snap) * per).wait()


def temporal_chunk(ins, blocks, weights, n_snap, per, chunk, chunks, result, waits):
    _, block, width = ins[0].shape
    nsnap = n_snap * per
    vmem = pl.BlockSpec(memory_space=pltpu.VMEM)
    hbm = pl.BlockSpec(memory_space=pltpu.HBM)
    before = [] if result is None else [result]
    n_in = len(ins) + len(weights)
    return pl.pallas_call(
        functools.partial(temporal_kernel, n_snap, per, blocks, chunk),
        out_shape=[pltpu.HBM((per, chunks * n_snap * block, width), BF16)]
        + [pltpu.HBM((per, block, width), BF16)] * (n_snap - 1),
        in_specs=[vmem] * (len(ins) + len(weights)) + [hbm] * len(before + waits),
        out_specs=[hbm] * n_snap,
        input_output_aliases={n_in: 0} if before else {},
        scratch_shapes=[
            pltpu.VMEM((nsnap, block, width), BF16),
            pltpu.VMEM((nsnap, block, width), BF16),
            pltpu.VMEM((nsnap, 3 * width, block), F32),
            pltpu.VMEM((nsnap, width, block), BF16),
            pltpu.SemaphoreType.DMA((n_snap,)),
        ],
        compiler_params=pltpu.CompilerParams(vmem_limit_bytes=14 << 20),
        cost_estimate=cost(TEMPORAL_US),
        name="temporal_chunk",
    )(*ins, *weights, *before, *waits)


def place_kernel(n_snap, chunk, *refs):
    blocks, (_, out_ref, sems) = refs[: n_snap - 1], refs[n_snap - 1 :]
    block = blocks[0].shape[1]
    me = lax.axis_index("snap")
    copies = []
    for d in range(1, n_snap):
        row = (chunk * n_snap + came_from(me, d, n_snap)) * block
        copies.append(
            pltpu.make_async_copy(blocks[d - 1], out_ref.at[:, pl.ds(row, block)], sems.at[d - 1])
        )
        copies[-1].start()
    for copy in copies:
        copy.wait()


def place(result, blocks, n_snap, chunk):
    hbm = pl.BlockSpec(memory_space=pltpu.HBM)
    return pl.pallas_call(
        functools.partial(place_kernel, n_snap, chunk),
        out_shape=pltpu.HBM(result.shape, result.dtype),
        in_specs=[pl.BlockSpec(memory_space=pltpu.VMEM)] * len(blocks) + [hbm],
        out_specs=hbm,
        input_output_aliases={len(blocks): 0},
        scratch_shapes=[pltpu.SemaphoreType.DMA((n_snap - 1,))],
        compiler_params=pltpu.CompilerParams(vmem_limit_bytes=1 << 20),
        cost_estimate=cost(PLACE_US),
        name="place",
    )(*blocks, result)


def shift(x, d, n):
    return lax.ppermute(x, "snap", [(i, partner(i, d, n)) for i in range(n)])


def temporal_fast(got, parts, weights, n_snap, first):
    per = len(got)
    chunks = parts[0][-1][1]
    result, backs = None, []
    for c in range(chunks):
        ins, blocks = [], []
        for d in range(n_snap):
            for j in range(per):
                e = [lo <= c < hi for lo, hi in parts[j]].index(True)
                ins.append(got[j][e][d])
                blocks.append(c - parts[j][e][0])
        result, *sent = temporal_chunk(
            ins, blocks, weights, n_snap, per, c, chunks, result, first if c == 0 else []
        )
        backs.append([shift(x, d + 1, n_snap) for d, x in enumerate(sent)])
        if c > 0:
            result = place(result, backs[c - 1], n_snap, c - 1)
    return place(result, backs[-1], n_snap, chunks - 1)


def temporal_plain(zvals, w_query, w_key, w_value, w_out, w_up, up_bias, w_down):
    nsnap, nvert, width = zvals.shape
    head_dim = width // HEADS
    heads = (nsnap, nvert, HEADS, head_dim)
    q_heads = dot(zvals, w_query).astype(BF16).reshape(heads)
    k_heads = dot(zvals, w_key).astype(BF16).reshape(heads)
    v_heads = dot(zvals, w_value).astype(BF16).reshape(heads)
    scores = jnp.einsum("tvhd,svhd->vhts", q_heads, k_heads, preferred_element_type=F32)
    scores = scores * (1.0 / math.sqrt(head_dim))
    causal = jnp.arange(nsnap)[:, None] >= jnp.arange(nsnap)[None, :]
    scores = jnp.where(causal, scores, NEG)
    peak = jnp.max(scores, axis=-1, keepdims=True)
    expo = jnp.exp(scores - peak)
    probs = (expo / jnp.sum(expo, axis=-1, keepdims=True)).astype(BF16)
    attended = jnp.einsum("vhts,svhd->tvhd", probs, v_heads, preferred_element_type=F32)
    attended = attended.astype(BF16).reshape(nsnap, nvert, width)
    mixed = zvals.astype(F32) + dot(attended, w_out)
    hidden = jax.nn.relu(dot(mixed.astype(BF16), w_up) + up_bias).astype(BF16)
    return (mixed + dot(hidden, w_down)).astype(BF16)


def on_device(
    features,
    adj_tiles,
    neighbors,
    w_struct,
    pos_embed,
    w_query,
    w_key,
    w_value,
    w_out,
    w_up,
    up_bias,
    w_down,
):
    snap_dev, vert_cl, width = features.shape
    blk_cl, nbr_k, block = adj_tiles.shape[1:4]
    n_clus, n_snap = lax.axis_size("clus"), lax.axis_size("snap")
    most = 4
    nbr = neighbors.transpose(0, 2, 1)
    feat = features.reshape(snap_dev, blk_cl, block, width)
    fast = snap_dev * n_snap <= 8 and blk_cl % n_snap == 0 and block % LANES == 0
    groups = n_snap if fast else 1
    chunks = blk_cl // groups
    done = jnp.zeros((1,), jnp.int32)
    sets = []
    for t in range(snap_dev):
        some, done = gather_blocks(done, nbr, feat, t, most, n_clus)
        sets.append(some)
    got, parts, prepared = [], [], None
    for t in range(snap_dev):
        near = near_sum(done, nbr, feat, adj_tiles, w_struct, t, n_clus, most, ROOM[min(t, 1)])
        if t == 0:
            for later in range(1, snap_dev):
                sets[later] = gate(near[-1:], sets[later])
        remote = [
            lax.ppermute(x, "clus", [(i, partner(i, d + 1, n_clus)) for i in range(n_clus)])
            for d, x in enumerate(sets[t])
        ]
        last = t == snap_dev - 1 and fast and chunks > 1
        parts.append([(0, 1), (1, chunks)] if last else [(0, chunks)])
        sent, done = far_sum(near, remote, w_struct, groups, parts[-1])
        got.append([])
        for e, part in enumerate(sent):
            if t > 0 and n_snap > 2:
                waits = got[-2][-1][1:3] if e == 0 else got[-2][-1][3:] + got[-1][-1][1:2]
                part[1:] = gate(waits, part[1:])
            got[-1].append([x if d == 0 else shift(x, d, n_snap) for d, x in enumerate(part)])
        if t == 0 and fast:
            prepared = prepare(done, pos_embed, w_query, w_key, w_value, w_out)
    if fast:
        weights = (*prepared, w_up, up_bias.reshape(1, -1), w_down)
        return temporal_fast(got, parts, weights, n_snap, sent[-1][1:2])
    vert_dev = vert_cl // n_snap
    struct_out = jnp.stack([g[0][0].reshape(n_snap, vert_dev, width) for g in got])
    inputs = lax.all_to_all(struct_out, "snap", split_axis=1, concat_axis=0, tiled=True)[:, 0]
    zvals = (inputs.astype(F32) + pos_embed.astype(F32)[:, None, :]).astype(BF16)
    result = temporal_plain(zvals, w_query, w_key, w_value, w_out, w_up, up_bias, w_down)
    returned = lax.all_to_all(
        result[:, None], "snap", split_axis=0, concat_axis=1, tiled=True
    )
    return returned.reshape(snap_dev, vert_cl, width)


def solution(mesh):
    placed = (
        P(("grp", "snap"), "clus", None),
        P(("grp", "snap"), "clus", None, None, None),
        P(("grp", "snap"), None, None),
        P(),
        P(),
        P(),
        P(),
        P(),
        P(),
        P(),
        P(),
        P(),
    )
    return jax.shard_map(
        on_device,
        mesh=mesh,
        in_specs=placed,
        out_specs=P(("grp", "snap"), "clus", None),
        check_vma=False,
    )
```

time: 318 us -> 121 us (0.38)
  waiting for transfers between devices: 109 us -> 27.4 us
  local copies, waits for them, and re-layouts: 83.7 us -> 2.3 us
  blocking collectives: 51.4 us -> 0 us
  matrix products: 51.3 us -> 0 us
  starting transfers between devices: 4.6 us -> 48.7 us
  Pallas kernels: 0 us -> 41.6 us
  between operations: 13.5 us -> 0.45 us
  other arithmetic: 3.22 us -> 0 us
    all_gather x1 -> x0, waiting for transfers between devices: 60.7 us -> none  [on_device(): table = lax.all_gather(projected, 'clus', axis=1, tiled=True)]
    all_to_all x1 -> x0, blocking collectives: 51.4 us -> none  [on_device(): lax.all_to_all(result, 'snap', split_axis=0, concat_axis=1, tiled=True)]
    dot_general x9 -> x0, matrix products: 51.3 us -> none  [the longest x1 11.5 us: temporal(): jnp.einsum('tvhd,svhd->vhts', q_heads, k_heads, preferred_element_type=jn...]
    ppermute x0 -> x27, starting transfers between devices: none -> 48.7 us  [the longest x21 43.4 us: shift(): return lax.ppermute(x, 'snap', [(i, partner(i, d, n)) for i in range(n)])]
    all_to_all x1 -> x0, waiting for transfers between devices: 48.6 us -> none  [on_device(): lax.all_to_all(struct_out, 'snap', split_axis=1, concat_axis=0, tiled=True)]
    pallas_call x0 -> x18, Pallas kernels: none -> 41.6 us  [the longest x4 14.6 us: temporal_chunk(): pl.pallas_call(functools.partial(temporal_kernel, n_snap, per, blocks, ch...]
    reshape x4 -> x0, local copies, waits for them, and re-layouts: 39.2 us -> none  [the longest x1 12.6 us: temporal(): q_heads = queries.reshape(nsnap, nvert, HEADS, head_dim)]
    ppermute x0 -> x27, waiting for transfers between devices: none -> 27.4 us  [the longest x21 27 us: shift(): return lax.ppermute(x, 'snap', [(i, partner(i, d, n)) for i in range(n)])]
  transfers between devices with their start and end apart: 2 -> 27, of which waited for: 2 -> 8; matrix products, arithmetic and copies ran while one was open for 0% -> 0% of each run, Pallas kernels for 0% -> 31%
where the time goes in v2:
time: 121 us; the launch traced here: 120 us
  starting transfers between devices  48.7 us (40%)
  Pallas kernels  41.6 us (34%)
  waiting for transfers between devices  27.4 us (23%)
  local copies, waits for them, and re-layouts  2.3 us (2%)
    ppermute x21, starting transfers between devices, shift(): return lax.ppermute(x, 'snap', [(i, partner(i, d, n)) for i in range(n)])  43.4 us
    ppermute x21, waiting for transfers between devices, shift(): return lax.ppermute(x, 'snap', [(i, partner(i, d, n)) for i in range(n)])  27 us
    pallas_call x4, Pallas kernels, temporal_chunk(): pl.pallas_call(functools.partial(temporal_kernel, n_snap, per, blocks, ch...  14.6 us
    pallas_call x2, Pallas kernels, near_sum(): pl.pallas_call(functools.partial(near_kernel, t, n_clus, most), out_shape...  10.4 us
    pallas_call x2, Pallas kernels, gather_blocks(): pl.pallas_call(functools.partial(gather_kernel, t, most, n_clus), grid=(1...  6.95 us
    pallas_call x2, Pallas kernels, far_sum(): pl.pallas_call(functools.partial(far_kernel, n_snap, parts), out_shape=[(...  5.47 us
    ppermute x6, starting transfers between devices, on_device(): lax.ppermute(x, 'clus', [(i, partner(i, d + 1, n_clus)) for i in range(n_...  5.22 us
    pallas_call x4, Pallas kernels, place(): pl.pallas_call(functools.partial(place_kernel, n_snap, chunk), out_shape=...  3.07 us
  transfers between devices with their start and end apart: 27, of which 8 were waited for; matrix products, arithmetic and copies ran while one was open for 0% of the time, Pallas kernels for 31%

profile of v2, /device:TPU:0, one launch (start us, length us, event | category | flops | bytes accessed | tf_op | source)
XLA Modules:
  0.0 120.4 jit_solution(6370223217415969518)
XLA Ops:
  0.0 3.1 %gather_blocks.2 = (bf16[4,128,256]{2,1,0:T(8,128)(2,1)}, bf16[4,128,256]{2,1,0:T(8,128)(2,1)}, bf16[4,128,256]{2,1,0:T(8,128)(2,1)}, s32[1]{0:T(128)}) custom-call(s32[1]{0:T(128)} %constant.0.clone.1.after_ref, s32[2,4,64]{2,1,0:T(4,128)} %bitcast.11, bf16[2,16,128,256]{3,2,1,0:T(8,128)(2,1)} %bitcast.3), custom_call_target="tpu_custom_call" | custom-call | bytes 90000 | tf_op jit(solution)/shard_map/gather_blocks/pallas_call | solution.py:73
  3.1 0.5 collective-permute-start
  3.6 2.6 %collective-permute-start.1 = (bf16[4,128,256]{2,1,0:T(8,128)(2,1)}, bf16[4,128,256]{2,1,0:T(8,128)(2,1)S(1)}, u32[]{:S(2)}, u32[]{:S(2)}) collective-permute-start(bf16[4,128,256]{2,1,0:T(8,128)(2,1)} %get-tuple-element.69), channel_id=1, source_target_pairs={{0,2},{1,3},{2,0},{3,1},{4,6},{5,7},{6,4},{7,5},{8,10},{9,11},{10,... | collective-permute-start | bytes 786440 | tf_op jit(solution)/shard_map/ppermute | solution.py:486
  6.2 0.1 collective-permute-start.2
  6.3 3.8 %gather_blocks.3 = (bf16[4,128,256]{2,1,0:T(8,128)(2,1)}, bf16[4,128,256]{2,1,0:T(8,128)(2,1)}, bf16[4,128,256]{2,1,0:T(8,128)(2,1)}, s32[1]{0:T(128)}) custom-call(s32[1]{0:T(128)} %get-tuple-element.62.after_ref, s32[2,4,64]{2,1,0:T(4,128)} %bitcast.12, bf16[2,16,128,256]{3,2,1,0:T(8,128)(2,1)} %bitcast.4), custom_call_target="tpu_custom_call" | custom-call | bytes 90000 | tf_op jit(solution)/shard_map/gather_blocks/pallas_call | solution.py:73
  10.1 0.0 copy-start.3
  10.1 5.4 %near_sum.2 = (f32[16,128,256]{2,1,0:T(8,128)S(1)}, bf16[16,128,256]{2,1,0:T(8,128)(2,1)S(1)}, bf16[16,4,128,128]{3,2,1,0:T(8,128)(2,1)S(1)}, s32[16]{0:T(128)}) custom-call(s32[1]{0:T(128)} %get-tuple-element.63.after_ref, s32[2,4,64]{2,1,0:T(4,128)} %bitcast.13, bf16[2,16,128,256]{3,2,1,0:T(8,128)(2,1)} %bitcast.5, bf16[2,16,4,128,128]{4,3,2,1,0:T(8,128)(2,1)} %adj_ref.3, ...), custom_call_target="tpu_custom_call" | custom-call | bytes 90000 | tf_op jit(solution)/shard_map/near_sum/pallas_call | solution.py:165
  15.5 0.7 copy-done.12
  16.2 0.1 collective-permute-start.3
  16.3 1.9 %collective-permute-start.4 = (bf16[4,128,256]{2,1,0:T(8,128)(2,1)}, bf16[4,128,256]{2,1,0:T(8,128)(2,1)S(1)}, u32[]{:S(2)}, u32[]{:S(2)}) collective-permute-start(bf16[4,128,256]{2,1,0:T(8,128)(2,1)} %get-tuple-element.81), channel_id=1, source_target_pairs={{0,2},{1,3},{2,0},{3,1},{4,6},{5,7},{6,4},{7,5},{8,10},{9,11},{10,... | collective-permute-start | bytes 786440 | tf_op jit(solution)/shard_map/ppermute | solution.py:486
  18.3 0.0 collective-permute-start.5
  18.3 0.0 collective-permute-done.1.refs_1_
  18.3 0.4 collective-permute-done.2.refs_2_
  18.7 0.7 copy-done.13
  19.3 2.7 %far_sum.2 = (bf16[4,128,256]{2,1,0:T(8,128)(2,1)S(1)}, bf16[4,128,256]{2,1,0:T(8,128)(2,1)}, bf16[4,128,256]{2,1,0:T(8,128)(2,1)}, bf16[4,128,256]{2,1,0:T(8,128)(2,1)}, s32[1]{0:T(128)}) custom-call(s32[16]{0:T(128)S(1)} %copy-done.13, f32[16,128,256]{2,1,0:T(8,128)S(1)} %get-tuple-element.65.acc_ref, bf16[16,128,256]{2,1,0:T(8,128)(2,1)S(1)} %get-tuple-element.66.own, ...), custom_call_target="tpu_custom_call" | custom-call | bytes 60000 | tf_op jit(solution)/shard_map/far_sum/pallas_call | solution.py:226
  22.0 1.7 %collective-permute-start.6 = (bf16[4,128,256]{2,1,0:T(8,128)(2,1)}, bf16[4,128,256]{2,1,0:T(8,128)(2,1)S(1)}, u32[]{:S(2)}, u32[]{:S(2)}) collective-permute-start(bf16[4,128,256]{2,1,0:T(8,128)(2,1)} %get-tuple-element.84), channel_id=1, source_target_pairs={{0,4},{4,0},{8,12},{12,8},{1,5},{5,1},{9,13},{13,9},{2,6},{6,2},{1... | collective-permute-start | bytes 786440 | tf_op jit(solution)/shard_map/ppermute | solution.py:407
  23.7 2.6 %collective-permute-start.8 = (bf16[4,128,256]{2,1,0:T(8,128)(2,1)}, bf16[4,128,256]{2,1,0:T(8,128)(2,1)S(1)}, u32[]{:S(2)}, u32[]{:S(2)}) collective-permute-start(bf16[4,128,256]{2,1,0:T(8,128)(2,1)} %get-tuple-element.86), channel_id=1, source_target_pairs={{0,8},{4,12},{8,0},{12,4},{1,9},{5,13},{9,1},{13,5},{2,10},{6,14},... | collective-permute-start | bytes 786440 | tf_op jit(solution)/shard_map/ppermute | solution.py:407
  26.3 0.0 collective-permute-done.3.refs_0_
  26.3 0.1 collective-permute-start.7
  26.5 5.1 %near_sum.3 = (f32[16,128,256]{2,1,0:T(8,128)S(1)}, bf16[16,128,256]{2,1,0:T(8,128)(2,1)S(1)}, bf16[16,4,128,128]{3,2,1,0:T(8,128)(2,1)S(1)}, s32[16]{0:T(128)S(1)}) custom-call(s32[1]{0:T(128)} %get-tuple-element.72.after_ref, s32[2,4,64]{2,1,0:T(4,128)S(1)} %bitcast.14, bf16[2,16,128,256]{3,2,1,0:T(8,128)(2,1)S(1)} %bitcast.6, ...), custom_call_target="tpu_custom_call" | custom-call | bytes 90000 | tf_op jit(solution)/shard_map/near_sum/pallas_call | solution.py:165
  31.6 0.0 collective-permute-done.4.refs_1_
  31.6 0.0 copy-start.5
  31.6 0.0 copy-start.6
  31.6 0.0 copy-start.7
  31.6 0.0 copy-start.8
  31.6 0.0 copy-start.11
  31.6 2.8 %far_sum.3 = (bf16[1,128,256]{2,1,0:T(8,128)(2,1)S(1)}, bf16[1,128,256]{2,1,0:T(8,128)(2,1)}, bf16[1,128,256]{2,1,0:T(8,128)(2,1)}, bf16[1,128,256]{2,1,0:T(8,12...) custom-call(s32[16]{0:T(128)S(1)} %get-tuple-element.73.slots, ...), custom_call_target="tpu_custom_call" | custom-call | bytes 60000 | tf_op jit(solution)/shard_map/far_sum/pallas_call | solution.py:226
  34.4 0.0 copy-start.1
  34.4 0.0 copy-start.2
  34.5 0.0 copy-start.9
  34.5 1.3 %collective-permute-done.6.refs_0_.refs_2_ = bf16[4,128,256]{2,1,0:T(8,128)(2,1)S(1)} collective-permute-done((bf16[4,128,256]{2,1,0:T(8,128)(2,1)}, bf16[4,128,256]{2,1,0:T(8,128)(2,1)S(1)}, u32[]{:S(2)}, u32[]{:S(2)}) %collective-permute-start.6) | collective-permute-done | bytes 262176 | tf_op jit(solution)/shard_map/ppermute | solution.py:407
  35.8 9.6 %collective-permute-done.8.refs_1_.refs_4_ = bf16[4,128,256]{2,1,0:T(8,128)(2,1)S(1)} collective-permute-done((bf16[4,128,256]{2,1,0:T(8,128)(2,1)}, bf16[4,128,256]{2,1,0:T(8,128)(2,1)S(1)}, u32[]{:S(2)}, u32[]{:S(2)}) %collective-permute-start.8) | collective-permute-done | bytes 262176 | tf_op jit(solution)/shard_map/ppermute | solution.py:407
  45.4 4.5 %collective-permute-done.9.refs_1_.refs_3_ = bf16[1,128,256]{2,1,0:T(8,128)(2,1)S(1)} collective-permute-done((bf16[1,128,256]{2,1,0:T(8,128)(2,1)}, bf16[1,128,256]{2,1,0:T(8,128)(2,1)S(1)}, u32[]{:S(2)}, u32[]{:S(2)}) %collective-permute-start.9) | collective-permute-done | bytes 65568 | tf_op jit(solution)/shard_map/ppermute | solution.py:407
  49.8 0.8 collective-permute-start.10
  50.6 2.2 %collective-permute-start.13 = (bf16[1,128,256]{2,1,0:T(8,128)(2,1)}, bf16[1,128,256]{2,1,0:T(8,128)(2,1)S(1)}, u32[]{:S(2)}, u32[]{:S(2)}) collective-permute-start(bf16[1,128,256]{2,1,0:T(8,128)(2,1)} %get-tuple-element.101), channel_id=1, source_target_pairs={{0,8},{4,12},{8,0},{12,4},{1,9},{5,13},{9,1},{13,5},{2,10},{6,14},... | collective-permute-start | bytes 196616 | tf_op jit(solution)/shard_map/ppermute | solution.py:407
  52.8 1.4 %collective-permute-start.14 = (bf16[1,128,256]{2,1,0:T(8,128)(2,1)}, bf16[1,128,256]{2,1,0:T(8,128)(2,1)S(1)}, u32[]{:S(2)}, u32[]{:S(2)}) collective-permute-start(bf16[1,128,256]{2,1,0:T(8,128)(2,1)} %get-tuple-element.102), channel_id=1, source_target_pairs={{0,12},{4,8},{8,4},{12,0},{1,13},{5,9},{9,5},{13,1},{2,14},{6,10},... | collective-permute-start | bytes 196616 | tf_op jit(solution)/shard_map/ppermute | solution.py:407
  54.2 0.8 collective-permute-start.11
  55.0 1.6 %collective-permute-start.12 = (bf16[3,128,256]{2,1,0:T(8,128)(2,1)}, bf16[3,128,256]{2,1,0:T(8,128)(2,1)S(1)}, u32[]{:S(2)}, u32[]{:S(2)}) collective-permute-start(bf16[3,128,256]{2,1,0:T(8,128)(2,1)} %get-tuple-element.96), channel_id=1, source_target_pairs={{0,12},{4,8},{8,4},{12,0},{1,13},{5,9},{9,5},{13,1},{2,14},{6,10},... | collective-permute-start | bytes 589832 | tf_op jit(solution)/shard_map/ppermute | solution.py:407
  56.7 1.0 prepare.1
  57.7 0.2 collective-permute-done.13.refs_5_
  57.9 4.0 %collective-permute-done.14.refs_7_ = bf16[1,128,256]{2,1,0:T(8,128)(2,1)S(1)} collective-permute-done((bf16[1,128,256]{2,1,0:T(8,128)(2,1)}, bf16[1,128,256]{2,1,0:T(8,128)(2,1)S(1)}, u32[]{:S(2)}, u32[]{:S(2)}) %collective-permute-start.14) | collective-permute-done | bytes 65568 | tf_op jit(solution)/shard_map/ppermute | solution.py:407
  62.0 0.9 copy-done.4
  62.9 3.6 %temporal_chunk.4 = (bf16[2,2048,256]{2,1,0:T(8,128)(2,1)}, bf16[2,128,256]{2,1,0:T(8,128)(2,1)}, bf16[2,128,256]{2,1,0:T(8,128)(2,1)}, bf16[2,128,256]{2,1,0:T(8,128)(2,1)}) custom-call(bf16[4,128,256]{2,1,0:T(8,128)(2,1)S(1)} %get-tuple-element.71.refs_0_, bf16[1,128,256]{2,1,0:T(8,128)(2,1)S(1)} %get-tuple-element.100.refs_1_, ...), custom_call_target="tpu_custom_call" | custom-call | bytes 90000 | tf_op jit(solution)/shard_map/temporal_chunk/pallas_call | solution.py:356
  66.5 6.9 %collective-permute-start.18 = (bf16[2,128,256]{2,1,0:T(8,128)(2,1)}, bf16[2,128,256]{2,1,0:T(8,128)(2,1)S(1)}, u32[]{:S(2)}, u32[]{:S(2)}) collective-permute-start(bf16[2,128,256]{2,1,0:T(8,128)(2,1)} %get-tuple-element.107), channel_id=1, source_target_pairs={{0,4},{4,0},{8,12},{12,8},{1,5},{5,1},{9,13},{13,9},{2,6},{6,2},{1... | collective-permute-start | bytes 393224 | tf_op jit(solution)/shard_map/ppermute | solution.py:407
  73.3 4.5 %collective-permute-start.19 = (bf16[2,128,256]{2,1,0:T(8,128)(2,1)}, bf16[2,128,256]{2,1,0:T(8,128)(2,1)S(1)}, u32[]{:S(2)}, u32[]{:S(2)}) collective-permute-start(bf16[2,128,256]{2,1,0:T(8,128)(2,1)} %get-tuple-element.108), channel_id=1, source_target_pairs={{0,8},{4,12},{8,0},{12,4},{1,9},{5,13},{9,1},{13,5},{2,10},{6,14},... | collective-permute-start | bytes 393224 | tf_op jit(solution)/shard_map/ppermute | solution.py:407
  77.8 1.4 %collective-permute-start.20 = (bf16[2,128,256]{2,1,0:T(8,128)(2,1)}, bf16[2,128,256]{2,1,0:T(8,128)(2,1)S(1)}, u32[]{:S(2)}, u32[]{:S(2)}) collective-permute-start(bf16[2,128,256]{2,1,0:T(8,128)(2,1)} %get-tuple-element.109), channel_id=1, source_target_pairs={{0,12},{4,8},{8,4},{12,0},{1,13},{5,9},{9,5},{13,1},{2,14},{6,10},... | collective-permute-start | bytes 393224 | tf_op jit(solution)/shard_map/ppermute | solution.py:407
  79.2 3.6 %temporal_chunk.5 = (bf16[2,2048,256]{2,1,0:T(8,128)(2,1)}, bf16[2,128,256]{2,1,0:T(8,128)(2,1)}, bf16[2,128,256]{2,1,0:T(8,128)(2,1)}, bf16[2,128,256]{2,1,0:T(8,128)(2,1)}) custom-call(bf16[4,128,256]{2,1,0:T(8,128)(2,1)S(1)} %get-tuple-element.71.refs_0_, bf16[3,128,256]{2,1,0:T(8,128)(2,1)S(1)} %get-tuple-element.83.refs_1_, ...), custom_call_target="tpu_custom_call", output_to_operand_aliasing={{0}: (14, {})} | custom-call | bytes 90000 | tf_op jit(solution)/shard_map/temporal_chunk/pallas_call | solution.py:356
  82.8 1.9 %collective-permute-start.15 = (bf16[2,128,256]{2,1,0:T(8,128)(2,1)}, bf16[2,128,256]{2,1,0:T(8,128)(2,1)S(1)}, u32[]{:S(2)}, u32[]{:S(2)}) collective-permute-start(bf16[2,128,256]{2,1,0:T(8,128)(2,1)} %get-tuple-element.104), channel_id=1, source_target_pairs={{0,4},{4,0},{8,12},{12,8},{1,5},{5,1},{9,13},{13,9},{2,6},{6,2},{1... | collective-permute-start | bytes 393224 | tf_op jit(solution)/shard_map/ppermute | solution.py:407
  84.7 1.2 collective-permute-start.16
  85.9 1.4 %collective-permute-start.17 = (bf16[2,128,256]{2,1,0:T(8,128)(2,1)}, bf16[2,128,256]{2,1,0:T(8,128)(2,1)S(1)}, u32[]{:S(2)}, u32[]{:S(2)}) collective-permute-start(bf16[2,128,256]{2,1,0:T(8,128)(2,1)} %get-tuple-element.106), channel_id=1, source_target_pairs={{0,12},{4,8},{8,4},{12,0},{1,13},{5,9},{9,5},{13,1},{2,14},{6,10},... | collective-permute-start | bytes 393224 | tf_op jit(solution)/shard_map/ppermute | solution.py:407
  87.3 0.8 place.4.refs_14_
  88.1 3.8 %temporal_chunk.6 = (bf16[2,2048,256]{2,1,0:T(8,128)(2,1)}, bf16[2,128,256]{2,1,0:T(8,128)(2,1)}, bf16[2,128,256]{2,1,0:T(8,128)(2,1)}, bf16[2,128,256]{2,1,0:T(8,128)(2,1)}) custom-call(bf16[4,128,256]{2,1,0:T(8,128)(2,1)S(1)} %get-tuple-element.71.refs_0_, bf16[3,128,256]{2,1,0:T(8,128)(2,1)S(1)} %get-tuple-element.83.refs_1_, ...), custom_call_target="tpu_custom_call", output_to_operand_aliasing={{0}: (14, {})} | custom-call | bytes 90000 | tf_op jit(solution)/shard_map/temporal_chunk/pallas_call | solution.py:356
  91.9 7.9 %collective-permute-start.24 = (bf16[2,128,256]{2,1,0:T(8,128)(2,1)}, bf16[2,128,256]{2,1,0:T(8,128)(2,1)S(1)}, u32[]{:S(2)}, u32[]{:S(2)}) collective-permute-start(bf16[2,128,256]{2,1,0:T(8,128)(2,1)} %get-tuple-element.115), channel_id=1, source_target_pairs={{0,4},{4,0},{8,12},{12,8},{1,5},{5,1},{9,13},{13,9},{2,6},{6,2},{1... | collective-permute-start | bytes 393224 | tf_op jit(solution)/shard_map/ppermute | solution.py:407
  99.8 1.2 %collective-permute-start.25 = (bf16[2,128,256]{2,1,0:T(8,128)(2,1)}, bf16[2,128,256]{2,1,0:T(8,128)(2,1)S(1)}, u32[]{:S(2)}, u32[]{:S(2)}) collective-permute-start(bf16[2,128,256]{2,1,0:T(8,128)(2,1)} %get-tuple-element.116), channel_id=1, source_target_pairs={{0,8},{4,12},{8,0},{12,4},{1,9},{5,13},{9,1},{13,5},{2,10},{6,14},... | collective-permute-start | bytes 393224 | tf_op jit(solution)/shard_map/ppermute | solution.py:407
  101.1 1.4 %collective-permute-start.26 = (bf16[2,128,256]{2,1,0:T(8,128)(2,1)}, bf16[2,128,256]{2,1,0:T(8,128)(2,1)S(1)}, u32[]{:S(2)}, u32[]{:S(2)}) collective-permute-start(bf16[2,128,256]{2,1,0:T(8,128)(2,1)} %get-tuple-element.117), channel_id=1, source_target_pairs={{0,12},{4,8},{8,4},{12,0},{1,13},{5,9},{9,5},{13,1},{2,14},{6,10},... | collective-permute-start | bytes 393224 | tf_op jit(solution)/shard_map/ppermute | solution.py:407
  102.5 0.8 place.5.refs_14_
  103.2 3.6 %temporal_chunk.7 = (bf16[2,2048,256]{2,1,0:T(8,128)(2,1)}, bf16[2,128,256]{2,1,0:T(8,128)(2,1)}, bf16[2,128,256]{2,1,0:T(8,128)(2,1)}, bf16[2,128,256]{2,1,0:T(8,128)(2,1)}) custom-call(bf16[4,128,256]{2,1,0:T(8,128)(2,1)S(1)} %get-tuple-element.71.refs_0_, bf16[3,128,256]{2,1,0:T(8,128)(2,1)S(1)} %get-tuple-element.83.refs_1_, ...), custom_call_target="tpu_custom_call", output_to_operand_aliasing={{0}: (14, {})} | custom-call | bytes 90000 | tf_op jit(solution)/shard_map/temporal_chunk/pallas_call | solution.py:356
  106.9 1.2 collective-permute-start.21
  108.0 1.9 %collective-permute-start.22 = (bf16[2,128,256]{2,1,0:T(8,128)(2,1)}, bf16[2,128,256]{2,1,0:T(8,128)(2,1)S(1)}, u32[]{:S(2)}, u32[]{:S(2)}) collective-permute-start(bf16[2,128,256]{2,1,0:T(8,128)(2,1)} %get-tuple-element.113), channel_id=1, source_target_pairs={{0,8},{4,12},{8,0},{12,4},{1,9},{5,13},{9,1},{13,5},{2,10},{6,14},... | collective-permute-start | bytes 393224 | tf_op jit(solution)/shard_map/ppermute | solution.py:407
  109.9 1.4 %collective-permute-start.23 = (bf16[2,128,256]{2,1,0:T(8,128)(2,1)}, bf16[2,128,256]{2,1,0:T(8,128)(2,1)S(1)}, u32[]{:S(2)}, u32[]{:S(2)}) collective-permute-start(bf16[2,128,256]{2,1,0:T(8,128)(2,1)} %get-tuple-element.114), channel_id=1, source_target_pairs={{0,12},{4,8},{8,4},{12,0},{1,13},{5,9},{9,5},{13,1},{2,14},{6,10},... | collective-permute-start | bytes 393224 | tf_op jit(solution)/shard_map/ppermute | solution.py:407
  111.3 0.8 place.6.refs_3_
  112.1 2.3 %collective-permute-done.21.refs_0_ = bf16[2,128,256]{2,1,0:T(8,128)(2,1)S(1)} collective-permute-done((bf16[2,128,256]{2,1,0:T(8,128)(2,1)}, bf16[2,128,256]{2,1,0:T(8,128)(2,1)S(1)}, u32[]{:S(2)}, u32[]{:S(2)}) %collective-permute-start.21) | collective-permute-done | bytes 131104 | tf_op jit(solution)/shard_map/ppermute | solution.py:407
  114.4 5.0 %collective-permute-done.22.refs_1_ = bf16[2,128,256]{2,1,0:T(8,128)(2,1)S(1)} collective-permute-done((bf16[2,128,256]{2,1,0:T(8,128)(2,1)}, bf16[2,128,256]{2,1,0:T(8,128)(2,1)S(1)}, u32[]{:S(2)}, u32[]{:S(2)}) %collective-permute-start.22) | collective-permute-done | bytes 131104 | tf_op jit(solution)/shard_map/ppermute | solution.py:407
  119.4 0.8 place.7
  (36 shorter events, 0.1 us)
Async XLA Ops:
  3.1 15.1 %collective-permute-start = (bf16[4,128,256]{2,1,0:T(8,128)(2,1)}, bf16[4,128,256]{2,1,0:T(8,128)(2,1)S(1)}, u32[]{:S(2)}, u32[]{:S(2)}) collective-permute-start(bf16[4,128,256]{2,1,0:T(8,128)(2,1)} %get-tuple-element.68), channel_id=1, source_target_pairs={{0,1},{1,0},{2,3},{3,2},{4,5},{5,4},{6,7},{7,6},{8,9},{9,8},{10,11... | collective-permute-start | bytes 786440 | tf_op jit(solution)/shard_map/ppermute | solution.py:486
  3.6 14.6 %collective-permute-start.1 = (bf16[4,128,256]{2,1,0:T(8,128)(2,1)}, bf16[4,128,256]{2,1,0:T(8,128)(2,1)S(1)}, u32[]{:S(2)}, u32[]{:S(2)}) collective-permute-start(bf16[4,128,256]{2,1,0:T(8,128)(2,1)} %get-tuple-element.69), channel_id=1, source_target_pairs={{0,2},{1,3},{2,0},{3,1},{4,6},{5,7},{6,4},{7,5},{8,10},{9,11},{10,... | collective-permute-start | bytes 786440 | tf_op jit(solution)/shard_map/ppermute | solution.py:486
  6.2 12.5 %collective-permute-start.2 = (bf16[4,128,256]{2,1,0:T(8,128)(2,1)}, bf16[4,128,256]{2,1,0:T(8,128)(2,1)S(1)}, u32[]{:S(2)}, u32[]{:S(2)}) collective-permute-start(bf16[4,128,256]{2,1,0:T(8,128)(2,1)} %get-tuple-element.70), channel_id=1, source_target_pairs={{0,3},{1,2},{2,1},{3,0},{4,7},{5,6},{6,5},{7,4},{8,11},{9,10},{10,... | collective-permute-start | bytes 786440 | tf_op jit(solution)/shard_map/ppermute | solution.py:486
  10.1 8.6 %copy-start.3 = (bf16[256,256]{1,0:T(8,128)(2,1)S(1)}, bf16[256,256]{1,0:T(8,128)(2,1)}, u32[]{:S(2)}) copy-start(bf16[256,256]{1,0:T(8,128)(2,1)} %w_ref.7) | copy-start | bytes 393220
  15.5 0.7 copy-start.12
  16.2 10.1 %collective-permute-start.3 = (bf16[4,128,256]{2,1,0:T(8,128)(2,1)}, bf16[4,128,256]{2,1,0:T(8,128)(2,1)S(1)}, u32[]{:S(2)}, u32[]{:S(2)}) collective-permute-start(bf16[4,128,256]{2,1,0:T(8,128)(2,1)} %get-tuple-element.80), channel_id=1, source_target_pairs={{0,1},{1,0},{2,3},{3,2},{4,5},{5,4},{6,7},{7,6},{8,9},{9,8},{10,11... | collective-permute-start | bytes 786440 | tf_op jit(solution)/shard_map/ppermute | solution.py:486
  16.3 15.2 %collective-permute-start.4 = (bf16[4,128,256]{2,1,0:T(8,128)(2,1)}, bf16[4,128,256]{2,1,0:T(8,128)(2,1)S(1)}, u32[]{:S(2)}, u32[]{:S(2)}) collective-permute-start(bf16[4,128,256]{2,1,0:T(8,128)(2,1)} %get-tuple-element.81), channel_id=1, source_target_pairs={{0,2},{1,3},{2,0},{3,1},{4,6},{5,7},{6,4},{7,5},{8,10},{9,11},{10,... | collective-permute-start | bytes 786440 | tf_op jit(solution)/shard_map/ppermute | solution.py:486
  18.3 13.3 %collective-permute-start.5 = (bf16[4,128,256]{2,1,0:T(8,128)(2,1)}, bf16[4,128,256]{2,1,0:T(8,128)(2,1)S(1)}, u32[]{:S(2)}, u32[]{:S(2)}) collective-permute-start(bf16[4,128,256]{2,1,0:T(8,128)(2,1)} %get-tuple-element.82), channel_id=1, source_target_pairs={{0,3},{1,2},{2,1},{3,0},{4,7},{5,6},{6,5},{7,4},{8,11},{9,10},{10,... | collective-permute-start | bytes 786440 | tf_op jit(solution)/shard_map/ppermute | solution.py:486
  18.7 0.7 copy-start.13
  19.3 7.2 %copy-start = (bf16[2,2048,256]{2,1,0:T(8,128)(2,1)S(1)}, bf16[2,2048,256]{2,1,0:T(8,128)(2,1)}, u32[]{:S(2)}) copy-start(bf16[2,2048,256]{2,1,0:T(8,128)(2,1)} %param.12) | copy-start | bytes 6291460
  19.3 7.2 %copy-start.10 = (s32[2,64,4]{1,2,0:T(4,128)S(1)}, s32[2,64,4]{1,2,0:T(4,128)}, u32[]{:S(2)}) copy-start(s32[2,64,4]{1,2,0:T(4,128)} %param.14) | copy-start | bytes 6148
  22.0 13.8 %collective-permute-start.6 = (bf16[4,128,256]{2,1,0:T(8,128)(2,1)}, bf16[4,128,256]{2,1,0:T(8,128)(2,1)S(1)}, u32[]{:S(2)}, u32[]{:S(2)}) collective-permute-start(bf16[4,128,256]{2,1,0:T(8,128)(2,1)} %get-tuple-element.84), channel_id=1, source_target_pairs={{0,4},{4,0},{8,12},{12,8},{1,5},{5,1},{9,13},{13,9},{2,6},{6,2},{1... | collective-permute-start | bytes 786440 | tf_op jit(solution)/shard_map/ppermute | solution.py:407
  23.7 21.6 %collective-permute-start.8 = (bf16[4,128,256]{2,1,0:T(8,128)(2,1)}, bf16[4,128,256]{2,1,0:T(8,128)(2,1)S(1)}, u32[]{:S(2)}, u32[]{:S(2)}) collective-permute-start(bf16[4,128,256]{2,1,0:T(8,128)(2,1)} %get-tuple-element.86), channel_id=1, source_target_pairs={{0,8},{4,12},{8,0},{12,4},{1,9},{5,13},{9,1},{13,5},{2,10},{6,14},... | collective-permute-start | bytes 786440 | tf_op jit(solution)/shard_map/ppermute | solution.py:407
  26.3 19.0 %collective-permute-start.7 = (bf16[4,128,256]{2,1,0:T(8,128)(2,1)}, bf16[4,128,256]{2,1,0:T(8,128)(2,1)S(1)}, u32[]{:S(2)}, u32[]{:S(2)}) collective-permute-start(bf16[4,128,256]{2,1,0:T(8,128)(2,1)} %get-tuple-element.85), channel_id=1, source_target_pairs={{0,12},{4,8},{8,4},{12,0},{1,13},{5,9},{9,5},{13,1},{2,14},{6,10},... | collective-permute-start | bytes 786440 | tf_op jit(solution)/shard_map/ppermute | solution.py:407
  31.6 25.1 %copy-start.5 = (bf16[256,256]{1,0:T(8,128)(2,1)S(1)}, bf16[256,256]{1,0:T(8,128)(2,1)}, u32[]{:S(2)}) copy-start(bf16[256,256]{1,0:T(8,128)(2,1)} %wq_ref.1) | copy-start | bytes 393220
  31.6 25.1 %copy-start.6 = (bf16[256,256]{1,0:T(8,128)(2,1)S(1)}, bf16[256,256]{1,0:T(8,128)(2,1)}, u32[]{:S(2)}) copy-start(bf16[256,256]{1,0:T(8,128)(2,1)} %wk_ref.1) | copy-start | bytes 393220
  31.6 25.1 %copy-start.7 = (bf16[256,256]{1,0:T(8,128)(2,1)S(1)}, bf16[256,256]{1,0:T(8,128)(2,1)}, u32[]{:S(2)}) copy-start(bf16[256,256]{1,0:T(8,128)(2,1)} %wv_ref.1) | copy-start | bytes 393220
  31.6 25.0 %copy-start.8 = (bf16[256,256]{1,0:T(8,128)(2,1)S(1)}, bf16[256,256]{1,0:T(8,128)(2,1)}, u32[]{:S(2)}) copy-start(bf16[256,256]{1,0:T(8,128)(2,1)} %wo_ref.1) | copy-start | bytes 393220
  31.6 25.0 %copy-start.11 = (bf16[8,256]{1,0:T(8,128)(2,1)S(1)}, bf16[8,256]{1,0:T(8,128)(2,1)}, u32[]{:S(2)}) copy-start(bf16[8,256]{1,0:T(8,128)(2,1)} %pos_ref.1) | copy-start | bytes 12292
  34.4 27.5 %copy-start.1 = (bf16[256,1024]{1,0:T(8,128)(2,1)S(1)}, bf16[256,1024]{1,0:T(8,128)(2,1)}, u32[]{:S(2)}) copy-start(bf16[256,1024]{1,0:T(8,128)(2,1)} %refs_11_.7) | copy-start | bytes 1572868
  34.4 27.5 %copy-start.2 = (bf16[1024,256]{1,0:T(8,128)(2,1)S(1)}, bf16[1024,256]{1,0:T(8,128)(2,1)}, u32[]{:S(2)}) copy-start(bf16[1024,256]{1,0:T(8,128)(2,1)} %refs_13_.7) | copy-start | bytes 1572868
  34.5 27.5 %copy-start.9 = (f32[1024]{0:T(1024)S(1)}, f32[1024]{0:T(1024)}, u32[]{:S(2)}) copy-start(f32[1024]{0:T(1024)} %param.22) | copy-start | bytes 12292
  45.3 4.5 %collective-permute-start.9 = (bf16[1,128,256]{2,1,0:T(8,128)(2,1)}, bf16[1,128,256]{2,1,0:T(8,128)(2,1)S(1)}, u32[]{:S(2)}, u32[]{:S(2)}) collective-permute-start(bf16[1,128,256]{2,1,0:T(8,128)(2,1)} %get-tuple-element.90), channel_id=1, source_target_pairs={{0,4},{4,0},{8,12},{12,8},{1,5},{5,1},{9,13},{13,9},{2,6},{6,2},{1... | collective-permute-start | bytes 196616 | tf_op jit(solution)/shard_map/ppermute | solution.py:407
  49.8 28.0 %collective-permute-start.10 = (bf16[3,128,256]{2,1,0:T(8,128)(2,1)}, bf16[3,128,256]{2,1,0:T(8,128)(2,1)S(1)}, u32[]{:S(2)}, u32[]{:S(2)}) collective-permute-start(bf16[3,128,256]{2,1,0:T(8,128)(2,1)} %get-tuple-element.94.refs_14_), channel_id=1, source_target_pairs={{0,4},{4,0},{8,12},{12,8},{1,5},{5,1},{9,13},{13,9},{2,6},{6,2},{1... | collective-permute-start | bytes 589832 | tf_op jit(solution)/shard_map/ppermute | solution.py:407
  50.6 7.4 %collective-permute-start.13 = (bf16[1,128,256]{2,1,0:T(8,128)(2,1)}, bf16[1,128,256]{2,1,0:T(8,128)(2,1)S(1)}, u32[]{:S(2)}, u32[]{:S(2)}) collective-permute-start(bf16[1,128,256]{2,1,0:T(8,128)(2,1)} %get-tuple-element.101), channel_id=1, source_target_pairs={{0,8},{4,12},{8,0},{12,4},{1,9},{5,13},{9,1},{13,5},{2,10},{6,14},... | collective-permute-start | bytes 196616 | tf_op jit(solution)/shard_map/ppermute | solution.py:407
  52.8 9.1 %collective-permute-start.14 = (bf16[1,128,256]{2,1,0:T(8,128)(2,1)}, bf16[1,128,256]{2,1,0:T(8,128)(2,1)S(1)}, u32[]{:S(2)}, u32[]{:S(2)}) collective-permute-start(bf16[1,128,256]{2,1,0:T(8,128)(2,1)} %get-tuple-element.102), channel_id=1, source_target_pairs={{0,12},{4,8},{8,4},{12,0},{1,13},{5,9},{9,5},{13,1},{2,14},{6,10},... | collective-permute-start | bytes 196616 | tf_op jit(solution)/shard_map/ppermute | solution.py:407
  54.2 25.0 %collective-permute-start.11 = (bf16[3,128,256]{2,1,0:T(8,128)(2,1)}, bf16[3,128,256]{2,1,0:T(8,128)(2,1)S(1)}, u32[]{:S(2)}, u32[]{:S(2)}) collective-permute-start(bf16[3,128,256]{2,1,0:T(8,128)(2,1)} %get-tuple-element.95), channel_id=1, source_target_pairs={{0,8},{4,12},{8,0},{12,4},{1,9},{5,13},{9,1},{13,5},{2,10},{6,14},... | collective-permute-start | bytes 589832 | tf_op jit(solution)/shard_map/ppermute | solution.py:407
  55.0 24.2 %collective-permute-start.12 = (bf16[3,128,256]{2,1,0:T(8,128)(2,1)}, bf16[3,128,256]{2,1,0:T(8,128)(2,1)S(1)}, u32[]{:S(2)}, u32[]{:S(2)}) collective-permute-start(bf16[3,128,256]{2,1,0:T(8,128)(2,1)} %get-tuple-element.96), channel_id=1, source_target_pairs={{0,12},{4,8},{8,4},{12,0},{1,13},{5,9},{9,5},{13,1},{2,14},{6,10},... | collective-permute-start | bytes 589832 | tf_op jit(solution)/shard_map/ppermute | solution.py:407
  62.0 0.9 copy-start.4
  66.5 19.4 %collective-permute-start.18 = (bf16[2,128,256]{2,1,0:T(8,128)(2,1)}, bf16[2,128,256]{2,1,0:T(8,128)(2,1)S(1)}, u32[]{:S(2)}, u32[]{:S(2)}) collective-permute-start(bf16[2,128,256]{2,1,0:T(8,128)(2,1)} %get-tuple-element.107), channel_id=1, source_target_pairs={{0,4},{4,0},{8,12},{12,8},{1,5},{5,1},{9,13},{13,9},{2,6},{6,2},{1... | collective-permute-start | bytes 393224 | tf_op jit(solution)/shard_map/ppermute | solution.py:407
  73.3 14.0 %collective-permute-start.19 = (bf16[2,128,256]{2,1,0:T(8,128)(2,1)}, bf16[2,128,256]{2,1,0:T(8,128)(2,1)S(1)}, u32[]{:S(2)}, u32[]{:S(2)}) collective-permute-start(bf16[2,128,256]{2,1,0:T(8,128)(2,1)} %get-tuple-element.108), channel_id=1, source_target_pairs={{0,8},{4,12},{8,0},{12,4},{1,9},{5,13},{9,1},{13,5},{2,10},{6,14},... | collective-permute-start | bytes 393224 | tf_op jit(solution)/shard_map/ppermute | solution.py:407
  77.8 9.5 %collective-permute-start.20 = (bf16[2,128,256]{2,1,0:T(8,128)(2,1)}, bf16[2,128,256]{2,1,0:T(8,128)(2,1)S(1)}, u32[]{:S(2)}, u32[]{:S(2)}) collective-permute-start(bf16[2,128,256]{2,1,0:T(8,128)(2,1)} %get-tuple-element.109), channel_id=1, source_target_pairs={{0,12},{4,8},{8,4},{12,0},{1,13},{5,9},{9,5},{13,1},{2,14},{6,10},... | collective-permute-start | bytes 393224 | tf_op jit(solution)/shard_map/ppermute | solution.py:407
  82.8 18.2 %collective-permute-start.15 = (bf16[2,128,256]{2,1,0:T(8,128)(2,1)}, bf16[2,128,256]{2,1,0:T(8,128)(2,1)S(1)}, u32[]{:S(2)}, u32[]{:S(2)}) collective-permute-start(bf16[2,128,256]{2,1,0:T(8,128)(2,1)} %get-tuple-element.104), channel_id=1, source_target_pairs={{0,4},{4,0},{8,12},{12,8},{1,5},{5,1},{9,13},{13,9},{2,6},{6,2},{1... | collective-permute-start | bytes 393224 | tf_op jit(solution)/shard_map/ppermute | solution.py:407
  84.7 17.7 %collective-permute-start.16 = (bf16[2,128,256]{2,1,0:T(8,128)(2,1)}, bf16[2,128,256]{2,1,0:T(8,128)(2,1)S(1)}, u32[]{:S(2)}, u32[]{:S(2)}) collective-permute-start(bf16[2,128,256]{2,1,0:T(8,128)(2,1)} %get-tuple-element.105), channel_id=1, source_target_pairs={{0,8},{4,12},{8,0},{12,4},{1,9},{5,13},{9,1},{13,5},{2,10},{6,14},... | collective-permute-start | bytes 393224 | tf_op jit(solution)/shard_map/ppermute | solution.py:407
  85.9 16.6 %collective-permute-start.17 = (bf16[2,128,256]{2,1,0:T(8,128)(2,1)}, bf16[2,128,256]{2,1,0:T(8,128)(2,1)S(1)}, u32[]{:S(2)}, u32[]{:S(2)}) collective-permute-start(bf16[2,128,256]{2,1,0:T(8,128)(2,1)} %get-tuple-element.106), channel_id=1, source_target_pairs={{0,12},{4,8},{8,4},{12,0},{1,13},{5,9},{9,5},{13,1},{2,14},{6,10},... | collective-permute-start | bytes 393224 | tf_op jit(solution)/shard_map/ppermute | solution.py:407
  91.9 18.0 %collective-permute-start.24 = (bf16[2,128,256]{2,1,0:T(8,128)(2,1)}, bf16[2,128,256]{2,1,0:T(8,128)(2,1)S(1)}, u32[]{:S(2)}, u32[]{:S(2)}) collective-permute-start(bf16[2,128,256]{2,1,0:T(8,128)(2,1)} %get-tuple-element.115), channel_id=1, source_target_pairs={{0,4},{4,0},{8,12},{12,8},{1,5},{5,1},{9,13},{13,9},{2,6},{6,2},{1... | collective-permute-start | bytes 393224 | tf_op jit(solution)/shard_map/ppermute | solution.py:407
  99.8 11.5 %collective-permute-start.25 = (bf16[2,128,256]{2,1,0:T(8,128)(2,1)}, bf16[2,128,256]{2,1,0:T(8,128)(2,1)S(1)}, u32[]{:S(2)}, u32[]{:S(2)}) collective-permute-start(bf16[2,128,256]{2,1,0:T(8,128)(2,1)} %get-tuple-element.116), channel_id=1, source_target_pairs={{0,8},{4,12},{8,0},{12,4},{1,9},{5,13},{9,1},{13,5},{2,10},{6,14},... | collective-permute-start | bytes 393224 | tf_op jit(solution)/shard_map/ppermute | solution.py:407
  101.1 10.2 %collective-permute-start.26 = (bf16[2,128,256]{2,1,0:T(8,128)(2,1)}, bf16[2,128,256]{2,1,0:T(8,128)(2,1)S(1)}, u32[]{:S(2)}, u32[]{:S(2)}) collective-permute-start(bf16[2,128,256]{2,1,0:T(8,128)(2,1)} %get-tuple-element.117), channel_id=1, source_target_pairs={{0,12},{4,8},{8,4},{12,0},{1,13},{5,9},{9,5},{13,1},{2,14},{6,10},... | collective-permute-start | bytes 393224 | tf_op jit(solution)/shard_map/ppermute | solution.py:407
  106.9 7.6 %collective-permute-start.21 = (bf16[2,128,256]{2,1,0:T(8,128)(2,1)}, bf16[2,128,256]{2,1,0:T(8,128)(2,1)S(1)}, u32[]{:S(2)}, u32[]{:S(2)}) collective-permute-start(bf16[2,128,256]{2,1,0:T(8,128)(2,1)} %get-tuple-element.112), channel_id=1, source_target_pairs={{0,4},{4,0},{8,12},{12,8},{1,5},{5,1},{9,13},{13,9},{2,6},{6,2},{1... | collective-permute-start | bytes 393224 | tf_op jit(solution)/shard_map/ppermute | solution.py:407
  108.0 11.4 %collective-permute-start.22 = (bf16[2,128,256]{2,1,0:T(8,128)(2,1)}, bf16[2,128,256]{2,1,0:T(8,128)(2,1)S(1)}, u32[]{:S(2)}, u32[]{:S(2)}) collective-permute-start(bf16[2,128,256]{2,1,0:T(8,128)(2,1)} %get-tuple-element.113), channel_id=1, source_target_pairs={{0,8},{4,12},{8,0},{12,4},{1,9},{5,13},{9,1},{13,5},{2,10},{6,14},... | collective-permute-start | bytes 393224 | tf_op jit(solution)/shard_map/ppermute | solution.py:407
  109.9 9.5 %collective-permute-start.23 = (bf16[2,128,256]{2,1,0:T(8,128)(2,1)}, bf16[2,128,256]{2,1,0:T(8,128)(2,1)S(1)}, u32[]{:S(2)}, u32[]{:S(2)}) collective-permute-start(bf16[2,128,256]{2,1,0:T(8,128)(2,1)} %get-tuple-element.114), channel_id=1, source_target_pairs={{0,12},{4,8},{8,4},{12,0},{1,13},{5,9},{9,5},{13,1},{2,14},{6,10},... | collective-permute-start | bytes 393224 | tf_op jit(solution)/shard_map/ppermute | solution.py:407

commit v3 on v2

--- a/solution.py
+++ b/solution.py
@@ -10,6 +10,7 @@
 
 HEADS = 8
 LANES = 128
+LAG = 2
 ALONE, ROOM = 60, (57, 46)
 GATHER_US, GATE_US, NEAR_US, FAR_US, TEMPORAL_US, PLACE_US = 3, 0.5, 3, 2, 3, 1
 NEG = -1e30
@@ -91,21 +92,23 @@
 
 
 def gate_kernel(*refs):
-    pass
+    refs[-1][0] = jnp.int32(0)
 
 
 def gate(after, xs):
     hbm = pl.BlockSpec(memory_space=pltpu.HBM)
-    return pl.pallas_call(
+    *out, done = pl.pallas_call(
         gate_kernel,
-        out_shape=[pltpu.HBM(x.shape, x.dtype) for x in xs],
+        out_shape=[pltpu.HBM(x.shape, x.dtype) for x in xs]
+        + [jax.ShapeDtypeStruct((1,), jnp.int32)],
         in_specs=[pl.BlockSpec(memory_space=pl.ANY)] * len(after) + [hbm] * len(xs),
-        out_specs=[hbm] * len(xs),
+        out_specs=[hbm] * len(xs) + [pl.BlockSpec(memory_space=pltpu.SMEM)],
         input_output_aliases={i + len(after): i for i in range(len(xs))},
         compiler_params=pltpu.CompilerParams(vmem_limit_bytes=1 << 20),
         cost_estimate=cost(GATE_US),
         name="gate",
     )(*after, *xs)
+    return out, done
 
 
 def near_kernel(
@@ -357,7 +360,8 @@
         functools.partial(temporal_kernel, n_snap, per, blocks, chunk),
         out_shape=[pltpu.HBM((per, chunks * n_snap * block, width), BF16)]
         + [pltpu.HBM((per, block, width), BF16)] * (n_snap - 1),
-        in_specs=[vmem] * (len(ins) + len(weights)) + [hbm] * len(before + waits),
+        in_specs=[vmem] * (len(ins) + len(weights)) + [hbm] * len(before)
+        + [pl.BlockSpec(memory_space=pltpu.SMEM)] * len(waits),
         out_specs=[hbm] * n_snap,
         input_output_aliases={n_in: 0} if before else {},
         scratch_shapes=[
@@ -422,9 +426,11 @@
             ins, blocks, weights, n_snap, per, c, chunks, result, first if c == 0 else []
         )
         backs.append([shift(x, d + 1, n_snap) for d, x in enumerate(sent)])
-        if c > 0:
-            result = place(result, backs[c - 1], n_snap, c - 1)
-    return place(result, backs[-1], n_snap, chunks - 1)
+        if c >= LAG:
+            result = place(result, backs[c - LAG], n_snap, c - LAG)
+    for c in range(max(chunks - LAG, 0), chunks):
+        result = place(result, backs[c], n_snap, c)
+    return result
 
 
 def temporal_plain(zvals, w_query, w_key, w_value, w_out, w_up, up_bias, w_down):
@@ -481,7 +487,7 @@
         near = near_sum(done, nbr, feat, adj_tiles, w_struct, t, n_clus, most, ROOM[min(t, 1)])
         if t == 0:
             for later in range(1, snap_dev):
-                sets[later] = gate(near[-1:], sets[later])
+                sets[later], _ = gate(near[:1], sets[later])
         remote = [
             lax.ppermute(x, "clus", [(i, partner(i, d + 1, n_clus)) for i in range(n_clus)])
             for d, x in enumerate(sets[t])
@@ -492,14 +498,14 @@
         got.append([])
         for e, part in enumerate(sent):
             if t > 0 and n_snap > 2:
-                waits = got[-2][-1][1:3] if e == 0 else got[-2][-1][3:] + got[-1][-1][1:2]
-                part[1:] = gate(waits, part[1:])
+                waits = got[-2][-1][1:2] if e == 0 else got[-2][-1][2:3] + got[-1][-1][1:2]
+                part[1:], done = gate(waits, part[1:])
             got[-1].append([x if d == 0 else shift(x, d, n_snap) for d, x in enumerate(part)])
         if t == 0 and fast:
             prepared = prepare(done, pos_embed, w_query, w_key, w_value, w_out)
     if fast:
         weights = (*prepared, w_up, up_bias.reshape(1, -1), w_down)
-        return temporal_fast(got, parts, weights, n_snap, sent[-1][1:2])
+        return temporal_fast(got, parts, weights, n_snap, [done])
     vert_dev = vert_cl // n_snap
     struct_out = jnp.stack([g[0][0].reshape(n_snap, vert_dev, width) for g in got])
     inputs = lax.all_to_all(struct_out, "snap", split_axis=1, concat_axis=0, tiled=True)[:, 0]

time: 121 us -> 117 us (0.967)
  starting transfers between devices: 48.7 us -> 43.8 us
  local copies, waits for them, and re-layouts: 2.3 us -> 0.08 us
  Pallas kernels: 41.6 us -> 43.6 us
  waiting for transfers between devices: 27.4 us -> 29 us
    ppermute x21, starting transfers between devices: 43.4 us -> 38.5 us  [shift(): return lax.ppermute(x, 'snap', [(i, partner(i, d, n)) for i in range(n)])]
    unnamed x28 -> x30, local copies, waits for them, and re-layouts: 2.3 us -> 0.08 us
    pallas_call x3, Pallas kernels: 0.01 us -> 1.55 us  [gate(): pl.pallas_call(gate_kernel, out_shape=[pltpu.HBM(x.shape, x.dtype) for x...]
    ppermute x21, waiting for transfers between devices: 27 us -> 28.5 us  [shift(): return lax.ppermute(x, 'snap', [(i, partner(i, d, n)) for i in range(n)])]
  transfers between devices with their start and end apart: 27 -> 27, of which waited for: 8 -> 7; matrix products, arithmetic and copies ran while one was open for 0% -> 0% of each run, Pallas kernels for 31% -> 34%
where the time goes in v3:
time: 117 us
  starting transfers between devices  43.8 us (37%)
  Pallas kernels  43.6 us (37%)
  waiting for transfers between devices  29 us (25%)
    ppermute x21, starting transfers between devices, shift(): return lax.ppermute(x, 'snap', [(i, partner(i, d, n)) for i in range(n)])  38.5 us
    ppermute x21, waiting for transfers between devices, shift(): return lax.ppermute(x, 'snap', [(i, partner(i, d, n)) for i in range(n)])  28.5 us
    pallas_call x4, Pallas kernels, temporal_chunk(): pl.pallas_call(functools.partial(temporal_kernel, n_snap, per, blocks, ch...  15.2 us
    pallas_call x2, Pallas kernels, near_sum(): pl.pallas_call(functools.partial(near_kernel, t, n_clus, most), out_shape...  10.4 us
    pallas_call x2, Pallas kernels, gather_blocks(): pl.pallas_call(functools.partial(gather_kernel, t, most, n_clus), grid=(1...  6.94 us
    pallas_call x2, Pallas kernels, far_sum(): pl.pallas_call(functools.partial(far_kernel, n_snap, parts), out_shape=[(...  5.47 us
    ppermute x6, starting transfers between devices, on_device(): lax.ppermute(x, 'clus', [(i, partner(i, d + 1, n_clus)) for i in range(n_...  5.29 us
    pallas_call x4, Pallas kernels, place(): pl.pallas_call(functools.partial(place_kernel, n_snap, chunk), out_shape=...  3.07 us
  transfers between devices with their start and end apart: 27, of which 7 were waited for; matrix products, arithmetic and copies ran while one was open for 0% of the time, Pallas kernels for 34%

profile of v3, /device:TPU:0, one launch (start us, length us, event | category | flops | bytes accessed | tf_op | source)
XLA Modules:
  0.0 117.1 jit_solution(1301951828919266424)
XLA Ops:
  0.0 3.1 %gather_blocks.2 = (bf16[4,128,256]{2,1,0:T(8,128)(2,1)}, bf16[4,128,256]{2,1,0:T(8,128)(2,1)}, bf16[4,128,256]{2,1,0:T(8,128)(2,1)}, s32[1]{0:T(128)}) custom-call(s32[1]{0:T(128)} %constant.0.clone.1.after_ref, s32[2,4,64]{2,1,0:T(4,128)} %bitcast.11, bf16[2,16,128,256]{3,2,1,0:T(8,128)(2,1)} %bitcast.3), custom_call_target="tpu_custom_call" | custom-call | bytes 90000 | tf_op jit(solution)/shard_map/gather_blocks/pallas_call | solution.py:74
  3.1 0.5 collective-permute-start
  3.6 2.6 %collective-permute-start.1 = (bf16[4,128,256]{2,1,0:T(8,128)(2,1)}, bf16[4,128,256]{2,1,0:T(8,128)(2,1)S(1)}, u32[]{:S(2)}, u32[]{:S(2)}) collective-permute-start(bf16[4,128,256]{2,1,0:T(8,128)(2,1)} %get-tuple-element.70), channel_id=1, source_target_pairs={{0,2},{1,3},{2,0},{3,1},{4,6},{5,7},{6,4},{7,5},{8,10},{9,11},{10,... | collective-permute-start | bytes 786440 | tf_op jit(solution)/shard_map/ppermute | solution.py:492
  6.2 0.1 collective-permute-start.2
  6.3 3.8 %gather_blocks.3 = (bf16[4,128,256]{2,1,0:T(8,128)(2,1)}, bf16[4,128,256]{2,1,0:T(8,128)(2,1)}, bf16[4,128,256]{2,1,0:T(8,128)(2,1)}, s32[1]{0:T(128)}) custom-call(s32[1]{0:T(128)} %get-tuple-element.63.after_ref, s32[2,4,64]{2,1,0:T(4,128)} %bitcast.12, bf16[2,16,128,256]{3,2,1,0:T(8,128)(2,1)} %bitcast.4), custom_call_target="tpu_custom_call" | custom-call | bytes 90000 | tf_op jit(solution)/shard_map/gather_blocks/pallas_call | solution.py:74
  10.1 5.3 %near_sum.2 = (f32[16,128,256]{2,1,0:T(8,128)S(1)}, bf16[16,128,256]{2,1,0:T(8,128)(2,1)S(1)}, bf16[16,4,128,128]{3,2,1,0:T(8,128)(2,1)S(1)}, s32[16]{0:T(128)}) custom-call(s32[1]{0:T(128)} %get-tuple-element.64.after_ref, s32[2,4,64]{2,1,0:T(4,128)} %bitcast.13, bf16[2,16,128,256]{3,2,1,0:T(8,128)(2,1)} %bitcast.5, bf16[2,16,4,128,128]{4,3,2,1,0:T(8,128)(2,1)} %adj_ref.3, ...), custom_call_target="tpu_custom_call" | custom-call | bytes 90000 | tf_op jit(solution)/shard_map/near_sum/pallas_call | solution.py:168
  15.4 0.0 copy-start.3
  15.4 0.5 gate.3
  16.0 0.2 collective-permute-start.3
  16.2 1.9 %collective-permute-start.4 = (bf16[4,128,256]{2,1,0:T(8,128)(2,1)}, bf16[4,128,256]{2,1,0:T(8,128)(2,1)S(1)}, u32[]{:S(2)}, u32[]{:S(2)}) collective-permute-start(bf16[4,128,256]{2,1,0:T(8,128)(2,1)} %get-tuple-element.82), channel_id=1, source_target_pairs={{0,2},{1,3},{2,0},{3,1},{4,6},{5,7},{6,4},{7,5},{8,10},{9,11},{10,... | collective-permute-start | bytes 786440 | tf_op jit(solution)/shard_map/ppermute | solution.py:492
  18.1 0.0 collective-permute-done.refs_0_
  18.1 0.0 collective-permute-start.5
  18.1 0.5 collective-permute-done.2.refs_2_
  18.7 2.7 %far_sum.2 = (bf16[4,128,256]{2,1,0:T(8,128)(2,1)S(1)}, bf16[4,128,256]{2,1,0:T(8,128)(2,1)}, bf16[4,128,256]{2,1,0:T(8,128)(2,1)}, bf16[4,128,256]{2,1,0:T(8,128)(2,1)}, s32[1]{0:T(128)}) custom-call(s32[16]{0:T(128)S(1)} %copy-done.11, f32[16,128,256]{2,1,0:T(8,128)S(1)} %get-tuple-element.66.acc_ref.refs_0_, ...), custom_call_target="tpu_custom_call" | custom-call | bytes 60000 | tf_op jit(solution)/shard_map/far_sum/pallas_call | solution.py:229
  21.4 1.7 %collective-permute-start.6 = (bf16[4,128,256]{2,1,0:T(8,128)(2,1)}, bf16[4,128,256]{2,1,0:T(8,128)(2,1)S(1)}, u32[]{:S(2)}, u32[]{:S(2)}) collective-permute-start(bf16[4,128,256]{2,1,0:T(8,128)(2,1)} %get-tuple-element.85), channel_id=1, source_target_pairs={{0,4},{4,0},{8,12},{12,8},{1,5},{5,1},{9,13},{13,9},{2,6},{6,2},{1... | collective-permute-start | bytes 786440 | tf_op jit(solution)/shard_map/ppermute | solution.py:411
  23.1 2.6 %collective-permute-start.7 = (bf16[4,128,256]{2,1,0:T(8,128)(2,1)}, bf16[4,128,256]{2,1,0:T(8,128)(2,1)S(1)}, u32[]{:S(2)}, u32[]{:S(2)}) collective-permute-start(bf16[4,128,256]{2,1,0:T(8,128)(2,1)} %get-tuple-element.86), channel_id=1, source_target_pairs={{0,8},{4,12},{8,0},{12,4},{1,9},{5,13},{9,1},{13,5},{2,10},{6,14},... | collective-permute-start | bytes 786440 | tf_op jit(solution)/shard_map/ppermute | solution.py:411
  25.7 0.0 collective-permute-done.3.refs_0_
  25.7 0.1 collective-permute-start.11
  25.8 5.1 %near_sum.3 = (f32[16,128,256]{2,1,0:T(8,128)S(1)}, bf16[16,128,256]{2,1,0:T(8,128)(2,1)S(1)}, bf16[16,4,128,128]{3,2,1,0:T(8,128)(2,1)S(1)}, s32[16]{0:T(128)S(1)}) custom-call(s32[1]{0:T(128)} %get-tuple-element.73.after_ref, s32[2,4,64]{2,1,0:T(4,128)S(1)} %bitcast.14, bf16[2,16,128,256]{3,2,1,0:T(8,128)(2,1)S(1)} %bitcast.6, ...), custom_call_target="tpu_custom_call" | custom-call | bytes 90000 | tf_op jit(solution)/shard_map/near_sum/pallas_call | solution.py:168
  30.9 0.0 collective-permute-done.5.refs_2_
  30.9 0.0 copy-start.4
  30.9 0.0 copy-start.5
  30.9 0.0 copy-start.6
  30.9 0.0 copy-start.7
  31.0 0.0 copy-start.10
  31.0 0.0 copy-start.8
  31.0 2.8 %far_sum.3 = (bf16[1,128,256]{2,1,0:T(8,128)(2,1)S(1)}, bf16[1,128,256]{2,1,0:T(8,128)(2,1)}, bf16[1,128,256]{2,1,0:T(8,128)(2,1)}, bf16[1,128,256]{2,1,0:T(8,12...) custom-call(s32[16]{0:T(128)S(1)} %get-tuple-element.74.slots, ...), custom_call_target="tpu_custom_call" | custom-call | bytes 60000 | tf_op jit(solution)/shard_map/far_sum/pallas_call | solution.py:229
  33.8 0.0 copy-start.1
  33.8 0.0 copy-start.2
  33.8 1.3 %collective-permute-done.6.refs_0_.refs_2_ = bf16[4,128,256]{2,1,0:T(8,128)(2,1)S(1)} collective-permute-done((bf16[4,128,256]{2,1,0:T(8,128)(2,1)}, bf16[4,128,256]{2,1,0:T(8,128)(2,1)S(1)}, u32[]{:S(2)}, u32[]{:S(2)}) %collective-permute-start.6) | collective-permute-done | bytes 262176 | tf_op jit(solution)/shard_map/ppermute | solution.py:411
  35.1 0.5 gate.4
  35.6 0.1 collective-permute-start.8
  35.7 3.6 %collective-permute-start.13 = (bf16[1,128,256]{2,1,0:T(8,128)(2,1)}, bf16[1,128,256]{2,1,0:T(8,128)(2,1)S(1)}, u32[]{:S(2)}, u32[]{:S(2)}) collective-permute-start(bf16[1,128,256]{2,1,0:T(8,128)(2,1)} %get-tuple-element.102), channel_id=1, source_target_pairs={{0,8},{4,12},{8,0},{12,4},{1,9},{5,13},{9,1},{13,5},{2,10},{6,14},... | collective-permute-start | bytes 196616 | tf_op jit(solution)/shard_map/ppermute | solution.py:411
  39.3 0.8 collective-permute-start.14
  40.1 5.0 %collective-permute-done.7.refs_0_.refs_4_ = bf16[4,128,256]{2,1,0:T(8,128)(2,1)S(1)} collective-permute-done((bf16[4,128,256]{2,1,0:T(8,128)(2,1)}, bf16[4,128,256]{2,1,0:T(8,128)(2,1)S(1)}, u32[]{:S(2)}, u32[]{:S(2)}) %collective-permute-start.7) | collective-permute-done | bytes 262176 | tf_op jit(solution)/shard_map/ppermute | solution.py:411
  45.0 0.1 collective-permute-done.8.refs_1_.refs_3_
  45.1 0.5 gate.5
  45.7 2.2 %collective-permute-start.9 = (bf16[3,128,256]{2,1,0:T(8,128)(2,1)}, bf16[3,128,256]{2,1,0:T(8,128)(2,1)S(1)}, u32[]{:S(2)}, u32[]{:S(2)}) collective-permute-start(bf16[3,128,256]{2,1,0:T(8,128)(2,1)} %get-tuple-element.94), channel_id=1, source_target_pairs={{0,4},{4,0},{8,12},{12,8},{1,5},{5,1},{9,13},{13,9},{2,6},{6,2},{1... | collective-permute-start | bytes 589832 | tf_op jit(solution)/shard_map/ppermute | solution.py:411
  47.8 3.3 %collective-permute-start.10 = (bf16[3,128,256]{2,1,0:T(8,128)(2,1)}, bf16[3,128,256]{2,1,0:T(8,128)(2,1)S(1)}, u32[]{:S(2)}, u32[]{:S(2)}) collective-permute-start(bf16[3,128,256]{2,1,0:T(8,128)(2,1)} %get-tuple-element.95), channel_id=1, source_target_pairs={{0,8},{4,12},{8,0},{12,4},{1,9},{5,13},{9,1},{13,5},{2,10},{6,14},... | collective-permute-start | bytes 589832 | tf_op jit(solution)/shard_map/ppermute | solution.py:411
  51.1 0.0 collective-permute-done.11.refs_6_
  51.2 1.0 prepare.1
  52.2 10.7 %collective-permute-done.13.refs_5_ = bf16[1,128,256]{2,1,0:T(8,128)(2,1)S(1)} collective-permute-done((bf16[1,128,256]{2,1,0:T(8,128)(2,1)}, bf16[1,128,256]{2,1,0:T(8,128)(2,1)S(1)}, u32[]{:S(2)}, u32[]{:S(2)}) %collective-permute-start.13) | collective-permute-done | bytes 65568 | tf_op jit(solution)/shard_map/ppermute | solution.py:411
  63.0 4.2 %temporal_chunk.4 = (bf16[2,2048,256]{2,1,0:T(8,128)(2,1)}, bf16[2,128,256]{2,1,0:T(8,128)(2,1)}, bf16[2,128,256]{2,1,0:T(8,128)(2,1)}, bf16[2,128,256]{2,1,0:T(8,128)(2,1)}) custom-call(bf16[4,128,256]{2,1,0:T(8,128)(2,1)S(1)} %get-tuple-element.72.refs_0_, bf16[1,128,256]{2,1,0:T(8,128)(2,1)S(1)} %get-tuple-element.101.refs_1_, ...), custom_call_target="tpu_custom_call" | custom-call | bytes 90000 | tf_op jit(solution)/shard_map/temporal_chunk/pallas_call | solution.py:359
  67.2 2.0 %collective-permute-start.15 = (bf16[2,128,256]{2,1,0:T(8,128)(2,1)}, bf16[2,128,256]{2,1,0:T(8,128)(2,1)S(1)}, u32[]{:S(2)}, u32[]{:S(2)}) collective-permute-start(bf16[2,128,256]{2,1,0:T(8,128)(2,1)} %get-tuple-element.105), channel_id=1, source_target_pairs={{0,4},{4,0},{8,12},{12,8},{1,5},{5,1},{9,13},{13,9},{2,6},{6,2},{1... | collective-permute-start | bytes 393224 | tf_op jit(solution)/shard_map/ppermute | solution.py:411
  69.2 1.1 collective-permute-start.16
  70.3 1.4 %collective-permute-start.17 = (bf16[2,128,256]{2,1,0:T(8,128)(2,1)}, bf16[2,128,256]{2,1,0:T(8,128)(2,1)S(1)}, u32[]{:S(2)}, u32[]{:S(2)}) collective-permute-start(bf16[2,128,256]{2,1,0:T(8,128)(2,1)} %get-tuple-element.107), channel_id=1, source_target_pairs={{0,12},{4,8},{8,4},{12,0},{1,13},{5,9},{9,5},{13,1},{2,14},{6,10},... | collective-permute-start | bytes 393224 | tf_op jit(solution)/shard_map/ppermute | solution.py:411
  71.7 3.6 %temporal_chunk.5 = (bf16[2,2048,256]{2,1,0:T(8,128)(2,1)}, bf16[2,128,256]{2,1,0:T(8,128)(2,1)}, bf16[2,128,256]{2,1,0:T(8,128)(2,1)}, bf16[2,128,256]{2,1,0:T(8,128)(2,1)}) custom-call(bf16[4,128,256]{2,1,0:T(8,128)(2,1)S(1)} %get-tuple-element.72.refs_0_, bf16[3,128,256]{2,1,0:T(8,128)(2,1)S(1)} %get-tuple-element.84.refs_1_, ...), custom_call_target="tpu_custom_call", output_to_operand_aliasing={{0}: (14, {})} | custom-call | bytes 90000 | tf_op jit(solution)/shard_map/temporal_chunk/pallas_call | solution.py:359
  75.3 6.2 %collective-permute-start.24 = (bf16[2,128,256]{2,1,0:T(8,128)(2,1)}, bf16[2,128,256]{2,1,0:T(8,128)(2,1)S(1)}, u32[]{:S(2)}, u32[]{:S(2)}) collective-permute-start(bf16[2,128,256]{2,1,0:T(8,128)(2,1)} %get-tuple-element.117), channel_id=1, source_target_pairs={{0,4},{4,0},{8,12},{12,8},{1,5},{5,1},{9,13},{13,9},{2,6},{6,2},{1... | collective-permute-start | bytes 393224 | tf_op jit(solution)/shard_map/ppermute | solution.py:411
  81.5 2.2 %collective-permute-start.25 = (bf16[2,128,256]{2,1,0:T(8,128)(2,1)}, bf16[2,128,256]{2,1,0:T(8,128)(2,1)S(1)}, u32[]{:S(2)}, u32[]{:S(2)}) collective-permute-start(bf16[2,128,256]{2,1,0:T(8,128)(2,1)} %get-tuple-element.118), channel_id=1, source_target_pairs={{0,8},{4,12},{8,0},{12,4},{1,9},{5,13},{9,1},{13,5},{2,10},{6,14},... | collective-permute-start | bytes 393224 | tf_op jit(solution)/shard_map/ppermute | solution.py:411
  83.7 3.8 %temporal_chunk.6 = (bf16[2,2048,256]{2,1,0:T(8,128)(2,1)}, bf16[2,128,256]{2,1,0:T(8,128)(2,1)}, bf16[2,128,256]{2,1,0:T(8,128)(2,1)}, bf16[2,128,256]{2,1,0:T(8,128)(2,1)}) custom-call(bf16[4,128,256]{2,1,0:T(8,128)(2,1)S(1)} %get-tuple-element.72.refs_0_, bf16[3,128,256]{2,1,0:T(8,128)(2,1)S(1)} %get-tuple-element.84.refs_1_, ...), custom_call_target="tpu_custom_call", output_to_operand_aliasing={{0}: (14, {})} | custom-call | bytes 90000 | tf_op jit(solution)/shard_map/temporal_chunk/pallas_call | solution.py:359
  87.5 1.5 %collective-permute-start.26 = (bf16[2,128,256]{2,1,0:T(8,128)(2,1)S(1)}, bf16[2,128,256]{2,1,0:T(8,128)(2,1)S(1)}, u32[]{:S(2)}, u32[]{:S(2)}) collective-permute-start(bf16[2,128,256]{2,1,0:T(8,128)(2,1)S(1)} %copy-done.14), channel_id=1, source_target_pairs={{0,12},{4,8},{8,4},{12,0},{1,13},{5,9},{9,5},{13,1},{2,14},{6,10},... | collective-permute-start | bytes 393224 | tf_op jit(solution)/shard_map/ppermute | solution.py:411
  89.0 0.6 collective-permute-start.21
  89.6 0.8 place.4.refs_14_
  90.4 3.6 %temporal_chunk.7 = (bf16[2,2048,256]{2,1,0:T(8,128)(2,1)}, bf16[2,128,256]{2,1,0:T(8,128)(2,1)}, bf16[2,128,256]{2,1,0:T(8,128)(2,1)}, bf16[2,128,256]{2,1,0:T(8,128)(2,1)}) custom-call(bf16[4,128,256]{2,1,0:T(8,128)(2,1)S(1)} %get-tuple-element.72.refs_0_, bf16[3,128,256]{2,1,0:T(8,128)(2,1)S(1)} %get-tuple-element.84.refs_1_, ...), custom_call_target="tpu_custom_call", output_to_operand_aliasing={{0}: (14, {})} | custom-call | bytes 90000 | tf_op jit(solution)/shard_map/temporal_chunk/pallas_call | solution.py:359
  94.0 1.5 %collective-permute-start.18 = (bf16[2,128,256]{2,1,0:T(8,128)(2,1)}, bf16[2,128,256]{2,1,0:T(8,128)(2,1)S(1)}, u32[]{:S(2)}, u32[]{:S(2)}) collective-permute-start(bf16[2,128,256]{2,1,0:T(8,128)(2,1)} %get-tuple-element.111), channel_id=1, source_target_pairs={{0,4},{4,0},{8,12},{12,8},{1,5},{5,1},{9,13},{13,9},{2,6},{6,2},{1... | collective-permute-start | bytes 393224 | tf_op jit(solution)/shard_map/ppermute | solution.py:411
  95.5 2.0 %collective-permute-start.22 = (bf16[2,128,256]{2,1,0:T(8,128)(2,1)S(1)}, bf16[2,128,256]{2,1,0:T(8,128)(2,1)S(1)}, u32[]{:S(2)}, u32[]{:S(2)}) collective-permute-start(bf16[2,128,256]{2,1,0:T(8,128)(2,1)S(1)} %copy-done.13), channel_id=1, source_target_pairs={{0,8},{4,12},{8,0},{12,4},{1,9},{5,13},{9,1},{13,5},{2,10},{6,14},... | collective-permute-start | bytes 393224 | tf_op jit(solution)/shard_map/ppermute | solution.py:411
  97.5 1.0 collective-permute-start.23
  98.5 1.5 %collective-permute-start.19 = (bf16[2,128,256]{2,1,0:T(8,128)(2,1)}, bf16[2,128,256]{2,1,0:T(8,128)(2,1)S(1)}, u32[]{:S(2)}, u32[]{:S(2)}) collective-permute-start(bf16[2,128,256]{2,1,0:T(8,128)(2,1)} %get-tuple-element.112), channel_id=1, source_target_pairs={{0,8},{4,12},{8,0},{12,4},{1,9},{5,13},{9,1},{13,5},{2,10},{6,14},... | collective-permute-start | bytes 393224 | tf_op jit(solution)/shard_map/ppermute | solution.py:411
  100.0 3.3 %collective-permute-start.20 = (bf16[2,128,256]{2,1,0:T(8,128)(2,1)}, bf16[2,128,256]{2,1,0:T(8,128)(2,1)S(1)}, u32[]{:S(2)}, u32[]{:S(2)}) collective-permute-start(bf16[2,128,256]{2,1,0:T(8,128)(2,1)} %get-tuple-element.113), channel_id=1, source_target_pairs={{0,12},{4,8},{8,4},{12,0},{1,13},{5,9},{9,5},{13,1},{2,14},{6,10},... | collective-permute-start | bytes 393224 | tf_op jit(solution)/shard_map/ppermute | solution.py:411
  103.2 0.8 place.5.refs_3_
  104.0 6.8 %collective-permute-done.22.refs_1_ = bf16[2,128,256]{2,1,0:T(8,128)(2,1)S(1)} collective-permute-done((bf16[2,128,256]{2,1,0:T(8,128)(2,1)S(1)}, bf16[2,128,256]{2,1,0:T(8,128)(2,1)S(1)}, u32[]{:S(2)}, u32[]{:S(2)}) %collective-permute-start.22) | collective-permute-done | bytes 131104 | tf_op jit(solution)/shard_map/ppermute | solution.py:411
  110.8 0.8 place.6.refs_3_
  111.6 4.5 %collective-permute-done.19.refs_1_ = bf16[2,128,256]{2,1,0:T(8,128)(2,1)S(1)} collective-permute-done((bf16[2,128,256]{2,1,0:T(8,128)(2,1)}, bf16[2,128,256]{2,1,0:T(8,128)(2,1)S(1)}, u32[]{:S(2)}, u32[]{:S(2)}) %collective-permute-start.19) | collective-permute-done | bytes 131104 | tf_op jit(solution)/shard_map/ppermute | solution.py:411
  116.1 0.8 place.7
  (38 shorter events, 0.1 us)
Async XLA Ops:
  3.1 15.0 %collective-permute-start = (bf16[4,128,256]{2,1,0:T(8,128)(2,1)}, bf16[4,128,256]{2,1,0:T(8,128)(2,1)S(1)}, u32[]{:S(2)}, u32[]{:S(2)}) collective-permute-start(bf16[4,128,256]{2,1,0:T(8,128)(2,1)} %get-tuple-element.69), channel_id=1, source_target_pairs={{0,1},{1,0},{2,3},{3,2},{4,5},{5,4},{6,7},{7,6},{8,9},{9,8},{10,11... | collective-permute-start | bytes 786440 | tf_op jit(solution)/shard_map/ppermute | solution.py:492
  3.6 14.5 %collective-permute-start.1 = (bf16[4,128,256]{2,1,0:T(8,128)(2,1)}, bf16[4,128,256]{2,1,0:T(8,128)(2,1)S(1)}, u32[]{:S(2)}, u32[]{:S(2)}) collective-permute-start(bf16[4,128,256]{2,1,0:T(8,128)(2,1)} %get-tuple-element.70), channel_id=1, source_target_pairs={{0,2},{1,3},{2,0},{3,1},{4,6},{5,7},{6,4},{7,5},{8,10},{9,11},{10,... | collective-permute-start | bytes 786440 | tf_op jit(solution)/shard_map/ppermute | solution.py:492
  6.2 12.5 %collective-permute-start.2 = (bf16[4,128,256]{2,1,0:T(8,128)(2,1)}, bf16[4,128,256]{2,1,0:T(8,128)(2,1)S(1)}, u32[]{:S(2)}, u32[]{:S(2)}) collective-permute-start(bf16[4,128,256]{2,1,0:T(8,128)(2,1)} %get-tuple-element.71), channel_id=1, source_target_pairs={{0,3},{1,2},{2,1},{3,0},{4,7},{5,6},{6,5},{7,4},{8,11},{9,10},{10,... | collective-permute-start | bytes 786440 | tf_op jit(solution)/shard_map/ppermute | solution.py:492
  15.4 3.2 %copy-start.3 = (bf16[256,256]{1,0:T(8,128)(2,1)S(1)}, bf16[256,256]{1,0:T(8,128)(2,1)}, u32[]{:S(2)}) copy-start(bf16[256,256]{1,0:T(8,128)(2,1)} %w_ref.7) | copy-start | bytes 393220
  15.4 3.2 %copy-start.11 = (s32[16]{0:T(128)S(1)}, s32[16]{0:T(128)}, u32[]{:S(2)}) copy-start(s32[16]{0:T(128)} %get-tuple-element.65.slots) | copy-start | bytes 196
  16.0 9.7 %collective-permute-start.3 = (bf16[4,128,256]{2,1,0:T(8,128)(2,1)}, bf16[4,128,256]{2,1,0:T(8,128)(2,1)S(1)}, u32[]{:S(2)}, u32[]{:S(2)}) collective-permute-start(bf16[4,128,256]{2,1,0:T(8,128)(2,1)} %get-tuple-element.81), channel_id=1, source_target_pairs={{0,1},{1,0},{2,3},{3,2},{4,5},{5,4},{6,7},{7,6},{8,9},{9,8},{10,11... | collective-permute-start | bytes 786440 | tf_op jit(solution)/shard_map/ppermute | solution.py:492
  16.2 14.7 %collective-permute-start.4 = (bf16[4,128,256]{2,1,0:T(8,128)(2,1)}, bf16[4,128,256]{2,1,0:T(8,128)(2,1)S(1)}, u32[]{:S(2)}, u32[]{:S(2)}) collective-permute-start(bf16[4,128,256]{2,1,0:T(8,128)(2,1)} %get-tuple-element.82), channel_id=1, source_target_pairs={{0,2},{1,3},{2,0},{3,1},{4,6},{5,7},{6,4},{7,5},{8,10},{9,11},{10,... | collective-permute-start | bytes 786440 | tf_op jit(solution)/shard_map/ppermute | solution.py:492
  18.1 12.8 %collective-permute-start.5 = (bf16[4,128,256]{2,1,0:T(8,128)(2,1)}, bf16[4,128,256]{2,1,0:T(8,128)(2,1)S(1)}, u32[]{:S(2)}, u32[]{:S(2)}) collective-permute-start(bf16[4,128,256]{2,1,0:T(8,128)(2,1)} %get-tuple-element.83), channel_id=1, source_target_pairs={{0,3},{1,2},{2,1},{3,0},{4,7},{5,6},{6,5},{7,4},{8,11},{9,10},{10,... | collective-permute-start | bytes 786440 | tf_op jit(solution)/shard_map/ppermute | solution.py:492
  18.7 7.2 %copy-start = (bf16[2,2048,256]{2,1,0:T(8,128)(2,1)S(1)}, bf16[2,2048,256]{2,1,0:T(8,128)(2,1)}, u32[]{:S(2)}) copy-start(bf16[2,2048,256]{2,1,0:T(8,128)(2,1)} %param.12) | copy-start | bytes 6291460
  18.7 7.2 %copy-start.9 = (s32[2,64,4]{1,2,0:T(4,128)S(1)}, s32[2,64,4]{1,2,0:T(4,128)}, u32[]{:S(2)}) copy-start(s32[2,64,4]{1,2,0:T(4,128)} %param.14) | copy-start | bytes 6148
  21.4 13.8 %collective-permute-start.6 = (bf16[4,128,256]{2,1,0:T(8,128)(2,1)}, bf16[4,128,256]{2,1,0:T(8,128)(2,1)S(1)}, u32[]{:S(2)}, u32[]{:S(2)}) collective-permute-start(bf16[4,128,256]{2,1,0:T(8,128)(2,1)} %get-tuple-element.85), channel_id=1, source_target_pairs={{0,4},{4,0},{8,12},{12,8},{1,5},{5,1},{9,13},{13,9},{2,6},{6,2},{1... | collective-permute-start | bytes 786440 | tf_op jit(solution)/shard_map/ppermute | solution.py:411
  23.1 22.0 %collective-permute-start.7 = (bf16[4,128,256]{2,1,0:T(8,128)(2,1)}, bf16[4,128,256]{2,1,0:T(8,128)(2,1)S(1)}, u32[]{:S(2)}, u32[]{:S(2)}) collective-permute-start(bf16[4,128,256]{2,1,0:T(8,128)(2,1)} %get-tuple-element.86), channel_id=1, source_target_pairs={{0,8},{4,12},{8,0},{12,4},{1,9},{5,13},{9,1},{13,5},{2,10},{6,14},... | collective-permute-start | bytes 786440 | tf_op jit(solution)/shard_map/ppermute | solution.py:411
  25.7 25.4 %collective-permute-start.11 = (bf16[4,128,256]{2,1,0:T(8,128)(2,1)}, bf16[4,128,256]{2,1,0:T(8,128)(2,1)S(1)}, u32[]{:S(2)}, u32[]{:S(2)}) collective-permute-start(bf16[4,128,256]{2,1,0:T(8,128)(2,1)} %get-tuple-element.96), channel_id=1, source_target_pairs={{0,12},{4,8},{8,4},{12,0},{1,13},{5,9},{9,5},{13,1},{2,14},{6,10},... | collective-permute-start | bytes 786440 | tf_op jit(solution)/shard_map/ppermute | solution.py:411
  30.9 20.2 %copy-start.4 = (bf16[256,256]{1,0:T(8,128)(2,1)S(1)}, bf16[256,256]{1,0:T(8,128)(2,1)}, u32[]{:S(2)}) copy-start(bf16[256,256]{1,0:T(8,128)(2,1)} %wq_ref.1) | copy-start | bytes 393220
  30.9 20.2 %copy-start.5 = (bf16[256,256]{1,0:T(8,128)(2,1)S(1)}, bf16[256,256]{1,0:T(8,128)(2,1)}, u32[]{:S(2)}) copy-start(bf16[256,256]{1,0:T(8,128)(2,1)} %wk_ref.1) | copy-start | bytes 393220
  30.9 20.2 %copy-start.6 = (bf16[256,256]{1,0:T(8,128)(2,1)S(1)}, bf16[256,256]{1,0:T(8,128)(2,1)}, u32[]{:S(2)}) copy-start(bf16[256,256]{1,0:T(8,128)(2,1)} %wv_ref.1) | copy-start | bytes 393220
  30.9 20.2 %copy-start.7 = (bf16[256,256]{1,0:T(8,128)(2,1)S(1)}, bf16[256,256]{1,0:T(8,128)(2,1)}, u32[]{:S(2)}) copy-start(bf16[256,256]{1,0:T(8,128)(2,1)} %wo_ref.1) | copy-start | bytes 393220
  31.0 20.2 %copy-start.10 = (bf16[8,256]{1,0:T(8,128)(2,1)S(1)}, bf16[8,256]{1,0:T(8,128)(2,1)}, u32[]{:S(2)}) copy-start(bf16[8,256]{1,0:T(8,128)(2,1)} %pos_ref.1) | copy-start | bytes 12292
  31.0 32.0 %copy-start.8 = (f32[1024]{0:T(1024)S(1)}, f32[1024]{0:T(1024)}, u32[]{:S(2)}) copy-start(f32[1024]{0:T(1024)} %param.22) | copy-start | bytes 12292
  33.8 29.2 %copy-start.1 = (bf16[256,1024]{1,0:T(8,128)(2,1)S(1)}, bf16[256,1024]{1,0:T(8,128)(2,1)}, u32[]{:S(2)}) copy-start(bf16[256,1024]{1,0:T(8,128)(2,1)} %refs_11_.7) | copy-start | bytes 1572868
  33.8 29.2 %copy-start.2 = (bf16[1024,256]{1,0:T(8,128)(2,1)S(1)}, bf16[1024,256]{1,0:T(8,128)(2,1)}, u32[]{:S(2)}) copy-start(bf16[1024,256]{1,0:T(8,128)(2,1)} %refs_13_.7) | copy-start | bytes 1572868
  35.6 9.5 %collective-permute-start.8 = (bf16[1,128,256]{2,1,0:T(8,128)(2,1)}, bf16[1,128,256]{2,1,0:T(8,128)(2,1)S(1)}, u32[]{:S(2)}, u32[]{:S(2)}) collective-permute-start(bf16[1,128,256]{2,1,0:T(8,128)(2,1)} %get-tuple-element.90), channel_id=1, source_target_pairs={{0,4},{4,0},{8,12},{12,8},{1,5},{5,1},{9,13},{13,9},{2,6},{6,2},{1... | collective-permute-start | bytes 196616 | tf_op jit(solution)/shard_map/ppermute | solution.py:411
  35.7 27.2 %collective-permute-start.13 = (bf16[1,128,256]{2,1,0:T(8,128)(2,1)}, bf16[1,128,256]{2,1,0:T(8,128)(2,1)S(1)}, u32[]{:S(2)}, u32[]{:S(2)}) collective-permute-start(bf16[1,128,256]{2,1,0:T(8,128)(2,1)} %get-tuple-element.102), channel_id=1, source_target_pairs={{0,8},{4,12},{8,0},{12,4},{1,9},{5,13},{9,1},{13,5},{2,10},{6,14},... | collective-permute-start | bytes 196616 | tf_op jit(solution)/shard_map/ppermute | solution.py:411
  39.3 23.6 %collective-permute-start.14 = (bf16[1,128,256]{2,1,0:T(8,128)(2,1)}, bf16[1,128,256]{2,1,0:T(8,128)(2,1)S(1)}, u32[]{:S(2)}, u32[]{:S(2)}) collective-permute-start(bf16[1,128,256]{2,1,0:T(8,128)(2,1)} %get-tuple-element.103), channel_id=1, source_target_pairs={{0,12},{4,8},{8,4},{12,0},{1,13},{5,9},{9,5},{13,1},{2,14},{6,10},... | collective-permute-start | bytes 196616 | tf_op jit(solution)/shard_map/ppermute | solution.py:411
  45.7 24.7 %collective-permute-start.9 = (bf16[3,128,256]{2,1,0:T(8,128)(2,1)}, bf16[3,128,256]{2,1,0:T(8,128)(2,1)S(1)}, u32[]{:S(2)}, u32[]{:S(2)}) collective-permute-start(bf16[3,128,256]{2,1,0:T(8,128)(2,1)} %get-tuple-element.94), channel_id=1, source_target_pairs={{0,4},{4,0},{8,12},{12,8},{1,5},{5,1},{9,13},{13,9},{2,6},{6,2},{1... | collective-permute-start | bytes 589832 | tf_op jit(solution)/shard_map/ppermute | solution.py:411
  47.8 23.9 %collective-permute-start.10 = (bf16[3,128,256]{2,1,0:T(8,128)(2,1)}, bf16[3,128,256]{2,1,0:T(8,128)(2,1)S(1)}, u32[]{:S(2)}, u32[]{:S(2)}) collective-permute-start(bf16[3,128,256]{2,1,0:T(8,128)(2,1)} %get-tuple-element.95), channel_id=1, source_target_pairs={{0,8},{4,12},{8,0},{12,4},{1,9},{5,13},{9,1},{13,5},{2,10},{6,14},... | collective-permute-start | bytes 589832 | tf_op jit(solution)/shard_map/ppermute | solution.py:411
  51.1 20.6 %collective-permute-start.12 = (bf16[3,128,256]{2,1,0:T(8,128)(2,1)}, bf16[3,128,256]{2,1,0:T(8,128)(2,1)S(1)}, u32[]{:S(2)}, u32[]{:S(2)}) collective-permute-start(bf16[3,128,256]{2,1,0:T(8,128)(2,1)} %get-tuple-element.97), channel_id=1, source_target_pairs={{0,12},{4,8},{8,4},{12,0},{1,13},{5,9},{9,5},{13,1},{2,14},{6,10},... | collective-permute-start | bytes 589832 | tf_op jit(solution)/shard_map/ppermute | solution.py:411
  67.2 20.3 %collective-permute-start.15 = (bf16[2,128,256]{2,1,0:T(8,128)(2,1)}, bf16[2,128,256]{2,1,0:T(8,128)(2,1)S(1)}, u32[]{:S(2)}, u32[]{:S(2)}) collective-permute-start(bf16[2,128,256]{2,1,0:T(8,128)(2,1)} %get-tuple-element.105), channel_id=1, source_target_pairs={{0,4},{4,0},{8,12},{12,8},{1,5},{5,1},{9,13},{13,9},{2,6},{6,2},{1... | collective-permute-start | bytes 393224 | tf_op jit(solution)/shard_map/ppermute | solution.py:411
  69.2 19.8 %collective-permute-start.16 = (bf16[2,128,256]{2,1,0:T(8,128)(2,1)}, bf16[2,128,256]{2,1,0:T(8,128)(2,1)S(1)}, u32[]{:S(2)}, u32[]{:S(2)}) collective-permute-start(bf16[2,128,256]{2,1,0:T(8,128)(2,1)} %get-tuple-element.106), channel_id=1, source_target_pairs={{0,8},{4,12},{8,0},{12,4},{1,9},{5,13},{9,1},{13,5},{2,10},{6,14},... | collective-permute-start | bytes 393224 | tf_op jit(solution)/shard_map/ppermute | solution.py:411
  70.3 19.3 %collective-permute-start.17 = (bf16[2,128,256]{2,1,0:T(8,128)(2,1)}, bf16[2,128,256]{2,1,0:T(8,128)(2,1)S(1)}, u32[]{:S(2)}, u32[]{:S(2)}) collective-permute-start(bf16[2,128,256]{2,1,0:T(8,128)(2,1)} %get-tuple-element.107), channel_id=1, source_target_pairs={{0,12},{4,8},{8,4},{12,0},{1,13},{5,9},{9,5},{13,1},{2,14},{6,10},... | collective-permute-start | bytes 393224 | tf_op jit(solution)/shard_map/ppermute | solution.py:411
  75.3 20.2 %collective-permute-start.24 = (bf16[2,128,256]{2,1,0:T(8,128)(2,1)}, bf16[2,128,256]{2,1,0:T(8,128)(2,1)S(1)}, u32[]{:S(2)}, u32[]{:S(2)}) collective-permute-start(bf16[2,128,256]{2,1,0:T(8,128)(2,1)} %get-tuple-element.117), channel_id=1, source_target_pairs={{0,4},{4,0},{8,12},{12,8},{1,5},{5,1},{9,13},{13,9},{2,6},{6,2},{1... | collective-permute-start | bytes 393224 | tf_op jit(solution)/shard_map/ppermute | solution.py:411
  81.5 16.0 %collective-permute-start.25 = (bf16[2,128,256]{2,1,0:T(8,128)(2,1)}, bf16[2,128,256]{2,1,0:T(8,128)(2,1)S(1)}, u32[]{:S(2)}, u32[]{:S(2)}) collective-permute-start(bf16[2,128,256]{2,1,0:T(8,128)(2,1)} %get-tuple-element.118), channel_id=1, source_target_pairs={{0,8},{4,12},{8,0},{12,4},{1,9},{5,13},{9,1},{13,5},{2,10},{6,14},... | collective-permute-start | bytes 393224 | tf_op jit(solution)/shard_map/ppermute | solution.py:411
  83.7 3.8 %copy-start.14 = (bf16[2,128,256]{2,1,0:T(8,128)(2,1)S(1)}, bf16[2,128,256]{2,1,0:T(8,128)(2,1)}, u32[]{:S(2)}) copy-start(bf16[2,128,256]{2,1,0:T(8,128)(2,1)} %get-tuple-element.119) | copy-start | bytes 393220
  87.5 11.0 %collective-permute-start.26 = (bf16[2,128,256]{2,1,0:T(8,128)(2,1)S(1)}, bf16[2,128,256]{2,1,0:T(8,128)(2,1)S(1)}, u32[]{:S(2)}, u32[]{:S(2)}) collective-permute-start(bf16[2,128,256]{2,1,0:T(8,128)(2,1)S(1)} %copy-done.14), channel_id=1, source_target_pairs={{0,12},{4,8},{8,4},{12,0},{1,13},{5,9},{9,5},{13,1},{2,14},{6,10},... | collective-permute-start | bytes 393224 | tf_op jit(solution)/shard_map/ppermute | solution.py:411
  89.0 11.0 %collective-permute-start.21 = (bf16[2,128,256]{2,1,0:T(8,128)(2,1)}, bf16[2,128,256]{2,1,0:T(8,128)(2,1)S(1)}, u32[]{:S(2)}, u32[]{:S(2)}) collective-permute-start(bf16[2,128,256]{2,1,0:T(8,128)(2,1)} %get-tuple-element.114), channel_id=1, source_target_pairs={{0,4},{4,0},{8,12},{12,8},{1,5},{5,1},{9,13},{13,9},{2,6},{6,2},{1... | collective-permute-start | bytes 393224 | tf_op jit(solution)/shard_map/ppermute | solution.py:411
  90.4 5.1 %copy-start.13 = (bf16[2,128,256]{2,1,0:T(8,128)(2,1)S(1)}, bf16[2,128,256]{2,1,0:T(8,128)(2,1)}, u32[]{:S(2)}) copy-start(bf16[2,128,256]{2,1,0:T(8,128)(2,1)} %get-tuple-element.115) | copy-start | bytes 393220
  90.4 7.1 %copy-start.12 = (bf16[2,128,256]{2,1,0:T(8,128)(2,1)S(1)}, bf16[2,128,256]{2,1,0:T(8,128)(2,1)}, u32[]{:S(2)}) copy-start(bf16[2,128,256]{2,1,0:T(8,128)(2,1)} %get-tuple-element.116) | copy-start | bytes 393220
  94.0 17.6 %collective-permute-start.18 = (bf16[2,128,256]{2,1,0:T(8,128)(2,1)}, bf16[2,128,256]{2,1,0:T(8,128)(2,1)S(1)}, u32[]{:S(2)}, u32[]{:S(2)}) collective-permute-start(bf16[2,128,256]{2,1,0:T(8,128)(2,1)} %get-tuple-element.111), channel_id=1, source_target_pairs={{0,4},{4,0},{8,12},{12,8},{1,5},{5,1},{9,13},{13,9},{2,6},{6,2},{1... | collective-permute-start | bytes 393224 | tf_op jit(solution)/shard_map/ppermute | solution.py:411
  95.5 15.3 %collective-permute-start.22 = (bf16[2,128,256]{2,1,0:T(8,128)(2,1)S(1)}, bf16[2,128,256]{2,1,0:T(8,128)(2,1)S(1)}, u32[]{:S(2)}, u32[]{:S(2)}) collective-permute-start(bf16[2,128,256]{2,1,0:T(8,128)(2,1)S(1)} %copy-done.13), channel_id=1, source_target_pairs={{0,8},{4,12},{8,0},{12,4},{1,9},{5,13},{9,1},{13,5},{2,10},{6,14},... | collective-permute-start | bytes 393224 | tf_op jit(solution)/shard_map/ppermute | solution.py:411
  97.5 13.3 %collective-permute-start.23 = (bf16[2,128,256]{2,1,0:T(8,128)(2,1)S(1)}, bf16[2,128,256]{2,1,0:T(8,128)(2,1)S(1)}, u32[]{:S(2)}, u32[]{:S(2)}) collective-permute-start(bf16[2,128,256]{2,1,0:T(8,128)(2,1)S(1)} %copy-done.12), channel_id=1, source_target_pairs={{0,12},{4,8},{8,4},{12,0},{1,13},{5,9},{9,5},{13,1},{2,14},{6,10},... | collective-permute-start | bytes 393224 | tf_op jit(solution)/shard_map/ppermute | solution.py:411
  98.5 17.6 %collective-permute-start.19 = (bf16[2,128,256]{2,1,0:T(8,128)(2,1)}, bf16[2,128,256]{2,1,0:T(8,128)(2,1)S(1)}, u32[]{:S(2)}, u32[]{:S(2)}) collective-permute-start(bf16[2,128,256]{2,1,0:T(8,128)(2,1)} %get-tuple-element.112), channel_id=1, source_target_pairs={{0,8},{4,12},{8,0},{12,4},{1,9},{5,13},{9,1},{13,5},{2,10},{6,14},... | collective-permute-start | bytes 393224 | tf_op jit(solution)/shard_map/ppermute | solution.py:411
  100.0 16.2 %collective-permute-start.20 = (bf16[2,128,256]{2,1,0:T(8,128)(2,1)}, bf16[2,128,256]{2,1,0:T(8,128)(2,1)S(1)}, u32[]{:S(2)}, u32[]{:S(2)}) collective-permute-start(bf16[2,128,256]{2,1,0:T(8,128)(2,1)} %get-tuple-element.113), channel_id=1, source_target_pairs={{0,12},{4,8},{8,4},{12,0},{1,13},{5,9},{9,5},{13,1},{2,14},{6,10},... | collective-permute-start | bytes 393224 | tf_op jit(solution)/shard_map/ppermute | solution.py:411

commit v4 on v3

--- a/solution.py
+++ b/solution.py
@@ -36,54 +36,69 @@
 
 def named_mask(nbr_ref, t, first, cluster, blk_cl):
     last = nbr_ref.shape[1] - 1
+    base = cluster * blk_cl
     mask = jnp.int32(0)
     for i in range(blk_cl):
-        g = nbr_ref[t, last, first + i] - cluster * blk_cl
+        g = nbr_ref[t, last, first + i] - base
         mask |= jnp.where((g >= 0) & (g < blk_cl), jnp.left_shift(1, g & 31), 0)
     return mask
 
 
-def gather_kernel(t, most, n_clus, after_ref, nbr_ref, feat_ref, *refs):
+def lowest_bit(mask, blk_cl):
+    low = mask & -mask
+    place = jnp.int32(0)
+    for i in range((blk_cl - 1).bit_length()):
+        holes = sum(1 << b for b in range(blk_cl) if b >> i & 1)
+        place += jnp.where((low & holes) != 0, 1 << i, 0)
+    return place
+
+
+def gather_kernel(t, most, n_clus, direct, after_ref, nbr_ref, feat_ref, *refs):
     blk_cl = feat_ref.shape[1]
-    outs, done_ref, sems = refs[:-2], refs[-2], refs[-1]
+    outs, (done_ref, held, in_sems, out_sems) = refs[: n_clus - 1], refs[n_clus - 1 :]
     done_ref[0] = jnp.int32(0)
     me = lax.axis_index("clus")
-    copies = []
-    for d in range(1, n_clus):
+    arrivals, copies = {}, []
+    order = list(range(n_clus - 1, 0, -1))
+    for d in order:
         mask = named_mask(nbr_ref, t, partner(me, d, n_clus) * blk_cl, me, blk_cl)
-        picked = [jnp.int32(0)] * most
-        count = jnp.int32(0)
-        for b in range(blk_cl):
-            bit = jnp.right_shift(mask, b) & 1
-            for j in range(most):
-                picked[j] = jnp.where((bit == 1) & (count == j), b, picked[j])
-            count += bit
-        for j in range(most):
-            copy = pltpu.make_async_copy(
-                feat_ref.at[t, picked[j]], outs[d - 1].at[j], sems.at[d - 1, j]
-            )
+        picked = []
+        for _ in range(most):
+            picked.append(lowest_bit(mask, blk_cl))
+            mask &= mask - 1
+        target = outs[d - 1] if direct else held.at[d - 1]
+        arrivals[d] = [
+            pltpu.make_async_copy(feat_ref.at[t, picked[j]], target.at[j], in_sems.at[d - 1, j])
+            for j in range(most)
+        ]
+        for copy in arrivals[d]:
             copy.start()
-            copies.append(copy)
+    for d in order:
+        for copy in arrivals[d]:
+            copy.wait()
+        if not direct:
+            copies.append(pltpu.make_async_copy(held.at[d - 1], outs[d - 1], out_sems.at[d - 1]))
+            copies[-1].start()
     for copy in copies:
         copy.wait()
 
 
 def gather_blocks(after, nbr, feat, t, most, n_clus):
+    direct = t == 0
     _, _, block, width = feat.shape
     shape = (most, block, width)
+    smem = pl.BlockSpec(memory_space=pltpu.SMEM)
+    space = pltpu.VMEM if direct else pltpu.HBM
     *out, done = pl.pallas_call(
-        functools.partial(gather_kernel, t, most, n_clus),
-        grid=(1,),
-        out_shape=[pltpu.HBM(shape, BF16)] * (n_clus - 1)
-        + [jax.ShapeDtypeStruct((1,), jnp.int32)],
-        in_specs=[
-            pl.BlockSpec(memory_space=pltpu.SMEM),
-            pl.BlockSpec(memory_space=pltpu.SMEM),
-            pl.BlockSpec(memory_space=pltpu.HBM),
+        functools.partial(gather_kernel, t, most, n_clus, direct),
+        out_shape=[space(shape, BF16)] * (n_clus - 1) + [jax.ShapeDtypeStruct((1,), jnp.int32)],
+        in_specs=[smem, smem, pl.BlockSpec(memory_space=pltpu.HBM)],
+        out_specs=[pl.BlockSpec(memory_space=space)] * (n_clus - 1) + [smem],
+        scratch_shapes=[
+            pltpu.VMEM((n_clus - 1,) + (shape if not direct else (1, 16, 128)), BF16),
+            pltpu.SemaphoreType.DMA((n_clus - 1, most)),
+            pltpu.SemaphoreType.DMA((n_clus - 1,)),
         ],
-        out_specs=[pl.BlockSpec(shape, lambda g: (0, 0, 0))] * (n_clus - 1)
-        + [pl.BlockSpec(memory_space=pltpu.SMEM)],
-        scratch_shapes=[pltpu.SemaphoreType.DMA((n_clus - 1, most))],
         compiler_params=pltpu.CompilerParams(vmem_limit_bytes=ALONE << 20),
         cost_estimate=cost(GATHER_US),
         name="gather_blocks",
@@ -185,7 +200,7 @@
     )(after, nbr, feat, adj, w)
 
 
-def far_kernel(n_snap, parts, slots, acc_ref, own, tiles, w_ref, *refs):
+def far_kernel(n_snap, parts, direct, slots, acc_ref, own, tiles, w_ref, *refs):
     n_out = n_snap * len(parts)
     remote, outs = refs[: -n_out - 4], refs[-n_out - 4 : -4]
     done_ref, table, held, sems = refs[-4:]
@@ -205,11 +220,11 @@
                 row = g * n_snap + p
                 total = acc_ref[row] + dot(tiles[row, tiles.shape[1] - 1], table[slots[row]])
                 total = (own[row].astype(F32) + jnp.maximum(total, 0.0)).astype(BF16)
-                if d == 0:
-                    outs[e * n_snap][g - lo] = total
+                if d == 0 or direct:
+                    outs[e * n_snap + d][g - lo] = total
                 else:
                     held[d - 1, g] = total
-            if d > 0:
+            if d > 0 and not direct:
                 copies.append(
                     pltpu.make_async_copy(
                         held.at[d - 1, lo:hi], outs[e * n_snap + d], sems.at[e, d - 1]
@@ -220,20 +235,20 @@
         copy.wait()
 
 
-def far_sum(near, remote, w, n_snap, parts):
+def far_sum(near, remote, w, n_snap, parts, direct):
     acc, own, tiles, slots = near
     most, block, width = remote[0].shape
     vmem = pl.BlockSpec(memory_space=pltpu.VMEM)
     hbm = pl.BlockSpec(memory_space=pltpu.HBM)
     shapes = [(hi - lo, block, width) for lo, hi in parts]
     *out, done = pl.pallas_call(
-        functools.partial(far_kernel, n_snap, parts),
+        functools.partial(far_kernel, n_snap, parts, direct),
         out_shape=[
-            (pltpu.HBM if d else pltpu.VMEM)(shape, BF16) for shape in shapes for d in range(n_snap)
+            (pltpu.VMEM if d == 0 or direct else pltpu.HBM)(shape, BF16) for shape in shapes for d in range(n_snap)
         ]
         + [jax.ShapeDtypeStruct((1,), jnp.int32)],
         in_specs=[pl.BlockSpec(memory_space=pltpu.SMEM)] + [vmem] * (4 + len(remote)),
-        out_specs=[hbm if d else vmem for _ in shapes for d in range(n_snap)]
+        out_specs=[vmem if d == 0 or direct else hbm for _ in shapes for d in range(n_snap)]
         + [pl.BlockSpec(memory_space=pltpu.SMEM)],
         scratch_shapes=[
             pltpu.VMEM((len(remote) * most + 1, block, width), BF16),
@@ -488,13 +503,14 @@
         if t == 0:
             for later in range(1, snap_dev):
                 sets[later], _ = gate(near[:1], sets[later])
-        remote = [
-            lax.ppermute(x, "clus", [(i, partner(i, d + 1, n_clus)) for i in range(n_clus)])
-            for d, x in enumerate(sets[t])
-        ]
+        remote = {}
+        for d in range(n_clus - 1, 0, -1):
+            pairs = [(i, partner(i, d, n_clus)) for i in range(n_clus)]
+            remote[d] = lax.ppermute(sets[t][d - 1], "clus", pairs)
+        remote = [remote[d] for d in range(1, n_clus)]
         last = t == snap_dev - 1 and fast and chunks > 1
         parts.append([(0, 1), (1, chunks)] if last else [(0, chunks)])
-        sent, done = far_sum(near, remote, w_struct, groups, parts[-1])
+        sent, done = far_sum(near, remote, w_struct, groups, parts[-1], t == 0)
         got.append([])
         for e, part in enumerate(sent):
             if t > 0 and n_snap > 2:

time: 117 us -> 116 us (level)
  transfers between devices with their start and end apart: 27 -> 27, of which waited for: 7 -> 8; matrix products, arithmetic and copies ran while one was open for 0% -> 0% of each run, Pallas kernels for 34% -> 34%
where the time goes in v4:
time: 116 us
  starting transfers between devices  43.7 us (38%)
  Pallas kernels  42.9 us (37%)
  waiting for transfers between devices  28.8 us (25%)
    ppermute x21, starting transfers between devices, shift(): return lax.ppermute(x, 'snap', [(i, partner(i, d, n)) for i in range(n)])  38.4 us
    ppermute x21, waiting for transfers between devices, shift(): return lax.ppermute(x, 'snap', [(i, partner(i, d, n)) for i in range(n)])  28.3 us
    pallas_call x4, Pallas kernels, temporal_chunk(): pl.pallas_call(functools.partial(temporal_kernel, n_snap, per, blocks, ch...  15.2 us
    pallas_call x2, Pallas kernels, near_sum(): pl.pallas_call(functools.partial(near_kernel, t, n_clus, most), out_shape...  10.4 us
    pallas_call x2, Pallas kernels, gather_blocks(): pl.pallas_call(functools.partial(gather_kernel, t, most, n_clus, direct),...  7.04 us
    ppermute x6, starting transfers between devices, on_device(): remote[d] = lax.ppermute(sets[t][d - 1], 'clus', pairs)  5.29 us
    pallas_call x2, Pallas kernels, far_sum(): pl.pallas_call(functools.partial(far_kernel, n_snap, parts, direct), out_...  4.66 us
    pallas_call x4, Pallas kernels, place(): pl.pallas_call(functools.partial(place_kernel, n_snap, chunk), out_shape=...  3.07 us
  transfers between devices with their start and end apart: 27, of which 8 were waited for; matrix products, arithmetic and copies ran while one was open for 0% of the time, Pallas kernels for 34%

profile of v4, /device:TPU:0, one launch (start us, length us, event | category | flops | bytes accessed | tf_op | source)
XLA Modules:
  0.0 116.0 jit_solution(2982489392824800464)
XLA Ops:
  0.0 3.0 %gather_blocks.2 = (bf16[4,128,256]{2,1,0:T(8,128)(2,1)}, bf16[4,128,256]{2,1,0:T(8,128)(2,1)}, bf16[4,128,256]{2,1,0:T(8,128)(2,1)}, s32[1]{0:T(128)}) custom-call(s32[1]{0:T(128)} %constant.0.clone.1.after_ref, s32[2,4,64]{2,1,0:T(4,128)} %bitcast.11, bf16[2,16,128,256]{3,2,1,0:T(8,128)(2,1)} %bitcast.3), custom_call_target="tpu_custom_call" | custom-call | bytes 90000 | tf_op jit(solution)/shard_map/gather_blocks/pallas_call | solution.py:92
  3.0 0.5 collective-permute-start
  3.5 2.6 %collective-permute-start.1 = (bf16[4,128,256]{2,1,0:T(8,128)(2,1)}, bf16[4,128,256]{2,1,0:T(8,128)(2,1)S(1)}, u32[]{:S(2)}, u32[]{:S(2)}) collective-permute-start(bf16[4,128,256]{2,1,0:T(8,128)(2,1)} %get-tuple-element.70), channel_id=1, source_target_pairs={{0,2},{1,3},{2,0},{3,1},{4,6},{5,7},{6,4},{7,5},{8,10},{9,11},{10,... | collective-permute-start | bytes 786440 | tf_op jit(solution)/shard_map/ppermute | solution.py:509
  6.1 0.1 collective-permute-start.2
  6.2 4.0 %gather_blocks.3 = (bf16[4,128,256]{2,1,0:T(8,128)(2,1)}, bf16[4,128,256]{2,1,0:T(8,128)(2,1)}, bf16[4,128,256]{2,1,0:T(8,128)(2,1)}, s32[1]{0:T(128)}) custom-call(s32[1]{0:T(128)} %get-tuple-element.63.after_ref, s32[2,4,64]{2,1,0:T(4,128)} %bitcast.12, bf16[2,16,128,256]{3,2,1,0:T(8,128)(2,1)} %bitcast.4), custom_call_target="tpu_custom_call" | custom-call | bytes 90000 | tf_op jit(solution)/shard_map/gather_blocks/pallas_call | solution.py:92
  10.2 5.3 %near_sum.2 = (f32[16,128,256]{2,1,0:T(8,128)S(1)}, bf16[16,128,256]{2,1,0:T(8,128)(2,1)S(1)}, bf16[16,4,128,128]{3,2,1,0:T(8,128)(2,1)S(1)}, s32[16]{0:T(128)}) custom-call(s32[1]{0:T(128)} %get-tuple-element.64.after_ref, s32[2,4,64]{2,1,0:T(4,128)} %bitcast.13, bf16[2,16,128,256]{3,2,1,0:T(8,128)(2,1)} %bitcast.5, bf16[2,16,4,128,128]{4,3,2,1,0:T(8,128)(2,1)} %adj_ref.3, ...), custom_call_target="tpu_custom_call" | custom-call | bytes 90000 | tf_op jit(solution)/shard_map/near_sum/pallas_call | solution.py:183
  15.5 0.0 copy-start.3
  15.6 0.5 gate.3
  16.1 0.2 collective-permute-start.3
  16.3 1.9 %collective-permute-start.4 = (bf16[4,128,256]{2,1,0:T(8,128)(2,1)}, bf16[4,128,256]{2,1,0:T(8,128)(2,1)S(1)}, u32[]{:S(2)}, u32[]{:S(2)}) collective-permute-start(bf16[4,128,256]{2,1,0:T(8,128)(2,1)} %get-tuple-element.82), channel_id=1, source_target_pairs={{0,2},{1,3},{2,0},{3,1},{4,6},{5,7},{6,4},{7,5},{8,10},{9,11},{10,... | collective-permute-start | bytes 786440 | tf_op jit(solution)/shard_map/ppermute | solution.py:509
  18.2 0.0 collective-permute-start.5
  18.2 0.0 collective-permute-done.1.refs_1_
  18.2 0.3 collective-permute-done.2.refs_2_
  18.6 1.9 %far_sum.2 = (bf16[4,128,256]{2,1,0:T(8,128)(2,1)S(1)}, bf16[4,128,256]{2,1,0:T(8,128)(2,1)S(1)}, bf16[4,128,256]{2,1,0:T(8,128)(2,1)S(1)}, bf16[4,128,256]{2,1,0:T(8,128)(2,1)S(1)}, s32[1]{0:T(128)}) custom-call(s32[16]{0:T(128)S(1)} %copy-done.11, f32[16,128,256]{2,1,0:T(8,128)S(1)} %get-tuple-element.66.acc_ref.refs_0_, ...), custom_call_target="tpu_custom_call" | custom-call | bytes 60000 | tf_op jit(solution)/shard_map/far_sum/pallas_call | solution.py:244
  20.5 1.7 %collective-permute-start.6 = (bf16[4,128,256]{2,1,0:T(8,128)(2,1)S(1)}, bf16[4,128,256]{2,1,0:T(8,128)(2,1)S(1)}, u32[]{:S(2)}, u32[]{:S(2)}) collective-permute-start(bf16[4,128,256]{2,1,0:T(8,128)(2,1)S(1)} %get-tuple-element.85), channel_id=1, source_target_pairs={{0,4},{4,0},{8,12},{12,8},{1,5},{5,1},{9,13},{13,9},{2,6},{6,2},{1... | collective-permute-start | bytes 786440 | tf_op jit(solution)/shard_map/ppermute | solution.py:426
  22.2 2.6 %collective-permute-start.7 = (bf16[4,128,256]{2,1,0:T(8,128)(2,1)S(1)}, bf16[4,128,256]{2,1,0:T(8,128)(2,1)S(1)}, u32[]{:S(2)}, u32[]{:S(2)}) collective-permute-start(bf16[4,128,256]{2,1,0:T(8,128)(2,1)S(1)} %get-tuple-element.86), channel_id=1, source_target_pairs={{0,8},{4,12},{8,0},{12,4},{1,9},{5,13},{9,1},{13,5},{2,10},{6,14},... | collective-permute-start | bytes 786440 | tf_op jit(solution)/shard_map/ppermute | solution.py:426
  24.8 0.0 collective-permute-done.3.refs_0_
  24.8 0.1 collective-permute-start.11
  25.0 5.0 %near_sum.3 = (f32[16,128,256]{2,1,0:T(8,128)S(1)}, bf16[16,128,256]{2,1,0:T(8,128)(2,1)S(1)}, bf16[16,4,128,128]{3,2,1,0:T(8,128)(2,1)S(1)}, s32[16]{0:T(128)S(1)}) custom-call(s32[1]{0:T(128)} %get-tuple-element.73.after_ref, s32[2,4,64]{2,1,0:T(4,128)S(1)} %bitcast.14, bf16[2,16,128,256]{3,2,1,0:T(8,128)(2,1)S(1)} %bitcast.6, ...), custom_call_target="tpu_custom_call" | custom-call | bytes 90000 | tf_op jit(solution)/shard_map/near_sum/pallas_call | solution.py:183
  30.0 0.0 collective-permute-done.4.refs_1_
  30.0 0.1 collective-permute-done.5.refs_2_
  30.1 0.0 copy-start.10
  30.2 0.0 copy-start.8
  30.2 2.8 %far_sum.3 = (bf16[1,128,256]{2,1,0:T(8,128)(2,1)S(1)}, bf16[1,128,256]{2,1,0:T(8,128)(2,1)}, bf16[1,128,256]{2,1,0:T(8,128)(2,1)}, bf16[1,128,256]{2,1,0:T(8,12...) custom-call(s32[16]{0:T(128)S(1)} %get-tuple-element.74.slots, ...), custom_call_target="tpu_custom_call" | custom-call | bytes 60000 | tf_op jit(solution)/shard_map/far_sum/pallas_call | solution.py:244
  32.9 0.0 copy-start.1
  33.0 0.0 copy-start.2
  33.0 1.1 collective-permute-done.6.refs_0_.refs_2_
  34.0 0.5 gate.4
  34.6 0.6 collective-permute-start.8
  35.2 3.1 %collective-permute-start.13 = (bf16[1,128,256]{2,1,0:T(8,128)(2,1)}, bf16[1,128,256]{2,1,0:T(8,128)(2,1)S(1)}, u32[]{:S(2)}, u32[]{:S(2)}) collective-permute-start(bf16[1,128,256]{2,1,0:T(8,128)(2,1)} %get-tuple-element.102), channel_id=1, source_target_pairs={{0,8},{4,12},{8,0},{12,4},{1,9},{5,13},{9,1},{13,5},{2,10},{6,14},... | collective-permute-start | bytes 196616 | tf_op jit(solution)/shard_map/ppermute | solution.py:426
  38.3 0.8 collective-permute-start.14
  39.0 5.0 %collective-permute-done.7.refs_0_.refs_4_ = bf16[4,128,256]{2,1,0:T(8,128)(2,1)S(1)} collective-permute-done((bf16[4,128,256]{2,1,0:T(8,128)(2,1)S(1)}, bf16[4,128,256]{2,1,0:T(8,128)(2,1)S(1)}, u32[]{:S(2)}, u32[]{:S(2)}) %collective-permute-start.7) | collective-permute-done | bytes 262176 | tf_op jit(solution)/shard_map/ppermute | solution.py:426
  44.0 0.3 collective-permute-done.8.refs_1_.refs_3_
  44.2 0.5 gate.5
  44.8 1.9 %collective-permute-start.9 = (bf16[3,128,256]{2,1,0:T(8,128)(2,1)}, bf16[3,128,256]{2,1,0:T(8,128)(2,1)S(1)}, u32[]{:S(2)}, u32[]{:S(2)}) collective-permute-start(bf16[3,128,256]{2,1,0:T(8,128)(2,1)} %get-tuple-element.94), channel_id=1, source_target_pairs={{0,4},{4,0},{8,12},{12,8},{1,5},{5,1},{9,13},{13,9},{2,6},{6,2},{1... | collective-permute-start | bytes 589832 | tf_op jit(solution)/shard_map/ppermute | solution.py:426
  46.7 3.4 %collective-permute-start.10 = (bf16[3,128,256]{2,1,0:T(8,128)(2,1)}, bf16[3,128,256]{2,1,0:T(8,128)(2,1)S(1)}, u32[]{:S(2)}, u32[]{:S(2)}) collective-permute-start(bf16[3,128,256]{2,1,0:T(8,128)(2,1)} %get-tuple-element.95), channel_id=1, source_target_pairs={{0,8},{4,12},{8,0},{12,4},{1,9},{5,13},{9,1},{13,5},{2,10},{6,14},... | collective-permute-start | bytes 589832 | tf_op jit(solution)/shard_map/ppermute | solution.py:426
  50.1 1.0 prepare.1
  51.1 10.7 %collective-permute-done.13.refs_5_ = bf16[1,128,256]{2,1,0:T(8,128)(2,1)S(1)} collective-permute-done((bf16[1,128,256]{2,1,0:T(8,128)(2,1)}, bf16[1,128,256]{2,1,0:T(8,128)(2,1)S(1)}, u32[]{:S(2)}, u32[]{:S(2)}) %collective-permute-start.13) | collective-permute-done | bytes 65568 | tf_op jit(solution)/shard_map/ppermute | solution.py:426
  61.9 4.3 %temporal_chunk.4 = (bf16[2,2048,256]{2,1,0:T(8,128)(2,1)}, bf16[2,128,256]{2,1,0:T(8,128)(2,1)}, bf16[2,128,256]{2,1,0:T(8,128)(2,1)}, bf16[2,128,256]{2,1,0:T(8,128)(2,1)}) custom-call(bf16[4,128,256]{2,1,0:T(8,128)(2,1)S(1)} %get-tuple-element.72.refs_0_, bf16[1,128,256]{2,1,0:T(8,128)(2,1)S(1)} %get-tuple-element.101.refs_1_, ...), custom_call_target="tpu_custom_call" | custom-call | bytes 90000 | tf_op jit(solution)/shard_map/temporal_chunk/pallas_call | solution.py:374
  66.1 2.0 %collective-permute-start.15 = (bf16[2,128,256]{2,1,0:T(8,128)(2,1)}, bf16[2,128,256]{2,1,0:T(8,128)(2,1)S(1)}, u32[]{:S(2)}, u32[]{:S(2)}) collective-permute-start(bf16[2,128,256]{2,1,0:T(8,128)(2,1)} %get-tuple-element.105), channel_id=1, source_target_pairs={{0,4},{4,0},{8,12},{12,8},{1,5},{5,1},{9,13},{13,9},{2,6},{6,2},{1... | collective-permute-start | bytes 393224 | tf_op jit(solution)/shard_map/ppermute | solution.py:426
  68.2 1.1 collective-permute-start.16
  69.3 0.0 collective-permute-done.9.refs_3_
  69.3 1.4 %collective-permute-start.17 = (bf16[2,128,256]{2,1,0:T(8,128)(2,1)}, bf16[2,128,256]{2,1,0:T(8,128)(2,1)S(1)}, u32[]{:S(2)}, u32[]{:S(2)}) collective-permute-start(bf16[2,128,256]{2,1,0:T(8,128)(2,1)} %get-tuple-element.107), channel_id=1, source_target_pairs={{0,12},{4,8},{8,4},{12,0},{1,13},{5,9},{9,5},{13,1},{2,14},{6,10},... | collective-permute-start | bytes 393224 | tf_op jit(solution)/shard_map/ppermute | solution.py:426
  70.6 0.0 collective-permute-done.10.refs_5_
  70.7 0.0 collective-permute-done.12.refs_7_
  70.7 3.6 %temporal_chunk.5 = (bf16[2,2048,256]{2,1,0:T(8,128)(2,1)}, bf16[2,128,256]{2,1,0:T(8,128)(2,1)}, bf16[2,128,256]{2,1,0:T(8,128)(2,1)}, bf16[2,128,256]{2,1,0:T(8,128)(2,1)}) custom-call(bf16[4,128,256]{2,1,0:T(8,128)(2,1)S(1)} %get-tuple-element.72.refs_0_, bf16[3,128,256]{2,1,0:T(8,128)(2,1)S(1)} %get-tuple-element.84.refs_1_, ...), custom_call_target="tpu_custom_call", output_to_operand_aliasing={{0}: (14, {})} | custom-call | bytes 90000 | tf_op jit(solution)/shard_map/temporal_chunk/pallas_call | solution.py:374
  74.2 6.3 %collective-permute-start.24 = (bf16[2,128,256]{2,1,0:T(8,128)(2,1)}, bf16[2,128,256]{2,1,0:T(8,128)(2,1)S(1)}, u32[]{:S(2)}, u32[]{:S(2)}) collective-permute-start(bf16[2,128,256]{2,1,0:T(8,128)(2,1)} %get-tuple-element.117), channel_id=1, source_target_pairs={{0,4},{4,0},{8,12},{12,8},{1,5},{5,1},{9,13},{13,9},{2,6},{6,2},{1... | collective-permute-start | bytes 393224 | tf_op jit(solution)/shard_map/ppermute | solution.py:426
  80.5 2.1 %collective-permute-start.25 = (bf16[2,128,256]{2,1,0:T(8,128)(2,1)}, bf16[2,128,256]{2,1,0:T(8,128)(2,1)S(1)}, u32[]{:S(2)}, u32[]{:S(2)}) collective-permute-start(bf16[2,128,256]{2,1,0:T(8,128)(2,1)} %get-tuple-element.118), channel_id=1, source_target_pairs={{0,8},{4,12},{8,0},{12,4},{1,9},{5,13},{9,1},{13,5},{2,10},{6,14},... | collective-permute-start | bytes 393224 | tf_op jit(solution)/shard_map/ppermute | solution.py:426
  82.6 3.8 %temporal_chunk.6 = (bf16[2,2048,256]{2,1,0:T(8,128)(2,1)}, bf16[2,128,256]{2,1,0:T(8,128)(2,1)}, bf16[2,128,256]{2,1,0:T(8,128)(2,1)}, bf16[2,128,256]{2,1,0:T(8,128)(2,1)}) custom-call(bf16[4,128,256]{2,1,0:T(8,128)(2,1)S(1)} %get-tuple-element.72.refs_0_, bf16[3,128,256]{2,1,0:T(8,128)(2,1)S(1)} %get-tuple-element.84.refs_1_, ...), custom_call_target="tpu_custom_call", output_to_operand_aliasing={{0}: (14, {})} | custom-call | bytes 90000 | tf_op jit(solution)/shard_map/temporal_chunk/pallas_call | solution.py:374
  86.4 1.5 %collective-permute-start.26 = (bf16[2,128,256]{2,1,0:T(8,128)(2,1)S(1)}, bf16[2,128,256]{2,1,0:T(8,128)(2,1)S(1)}, u32[]{:S(2)}, u32[]{:S(2)}) collective-permute-start(bf16[2,128,256]{2,1,0:T(8,128)(2,1)S(1)} %copy-done.14), channel_id=1, source_target_pairs={{0,12},{4,8},{8,4},{12,0},{1,13},{5,9},{9,5},{13,1},{2,14},{6,10},... | collective-permute-start | bytes 393224 | tf_op jit(solution)/shard_map/ppermute | solution.py:426
  87.9 0.6 collective-permute-start.21
  88.5 0.0 collective-permute-done.17.refs_2_
  88.5 0.8 place.4.refs_14_
  89.3 3.6 %temporal_chunk.7 = (bf16[2,2048,256]{2,1,0:T(8,128)(2,1)}, bf16[2,128,256]{2,1,0:T(8,128)(2,1)}, bf16[2,128,256]{2,1,0:T(8,128)(2,1)}, bf16[2,128,256]{2,1,0:T(8,128)(2,1)}) custom-call(bf16[4,128,256]{2,1,0:T(8,128)(2,1)S(1)} %get-tuple-element.72.refs_0_, bf16[3,128,256]{2,1,0:T(8,128)(2,1)S(1)} %get-tuple-element.84.refs_1_, ...), custom_call_target="tpu_custom_call", output_to_operand_aliasing={{0}: (14, {})} | custom-call | bytes 90000 | tf_op jit(solution)/shard_map/temporal_chunk/pallas_call | solution.py:374
  92.9 1.5 %collective-permute-start.18 = (bf16[2,128,256]{2,1,0:T(8,128)(2,1)}, bf16[2,128,256]{2,1,0:T(8,128)(2,1)S(1)}, u32[]{:S(2)}, u32[]{:S(2)}) collective-permute-start(bf16[2,128,256]{2,1,0:T(8,128)(2,1)} %get-tuple-element.111), channel_id=1, source_target_pairs={{0,4},{4,0},{8,12},{12,8},{1,5},{5,1},{9,13},{13,9},{2,6},{6,2},{1... | collective-permute-start | bytes 393224 | tf_op jit(solution)/shard_map/ppermute | solution.py:426
  94.4 2.0 %collective-permute-start.22 = (bf16[2,128,256]{2,1,0:T(8,128)(2,1)S(1)}, bf16[2,128,256]{2,1,0:T(8,128)(2,1)S(1)}, u32[]{:S(2)}, u32[]{:S(2)}) collective-permute-start(bf16[2,128,256]{2,1,0:T(8,128)(2,1)S(1)} %copy-done.13), channel_id=1, source_target_pairs={{0,8},{4,12},{8,0},{12,4},{1,9},{5,13},{9,1},{13,5},{2,10},{6,14},... | collective-permute-start | bytes 393224 | tf_op jit(solution)/shard_map/ppermute | solution.py:426
  96.4 1.0 collective-permute-start.23
  97.4 1.5 %collective-permute-start.19 = (bf16[2,128,256]{2,1,0:T(8,128)(2,1)}, bf16[2,128,256]{2,1,0:T(8,128)(2,1)S(1)}, u32[]{:S(2)}, u32[]{:S(2)}) collective-permute-start(bf16[2,128,256]{2,1,0:T(8,128)(2,1)} %get-tuple-element.112), channel_id=1, source_target_pairs={{0,8},{4,12},{8,0},{12,4},{1,9},{5,13},{9,1},{13,5},{2,10},{6,14},... | collective-permute-start | bytes 393224 | tf_op jit(solution)/shard_map/ppermute | solution.py:426
  98.9 3.3 %collective-permute-start.20 = (bf16[2,128,256]{2,1,0:T(8,128)(2,1)}, bf16[2,128,256]{2,1,0:T(8,128)(2,1)S(1)}, u32[]{:S(2)}, u32[]{:S(2)}) collective-permute-start(bf16[2,128,256]{2,1,0:T(8,128)(2,1)} %get-tuple-element.113), channel_id=1, source_target_pairs={{0,12},{4,8},{8,4},{12,0},{1,13},{5,9},{9,5},{13,1},{2,14},{6,10},... | collective-permute-start | bytes 393224 | tf_op jit(solution)/shard_map/ppermute | solution.py:426
  102.2 0.8 place.5.refs_3_
  103.0 6.8 %collective-permute-done.22.refs_1_ = bf16[2,128,256]{2,1,0:T(8,128)(2,1)S(1)} collective-permute-done((bf16[2,128,256]{2,1,0:T(8,128)(2,1)S(1)}, bf16[2,128,256]{2,1,0:T(8,128)(2,1)S(1)}, u32[]{:S(2)}, u32[]{:S(2)}) %collective-permute-start.22) | collective-permute-done | bytes 131104 | tf_op jit(solution)/shard_map/ppermute | solution.py:426
  109.7 0.8 place.6.refs_3_
  110.5 4.5 %collective-permute-done.19.refs_1_ = bf16[2,128,256]{2,1,0:T(8,128)(2,1)S(1)} collective-permute-done((bf16[2,128,256]{2,1,0:T(8,128)(2,1)}, bf16[2,128,256]{2,1,0:T(8,128)(2,1)S(1)}, u32[]{:S(2)}, u32[]{:S(2)}) %collective-permute-start.19) | collective-permute-done | bytes 131104 | tf_op jit(solution)/shard_map/ppermute | solution.py:426
  115.0 0.8 place.7
  (38 shorter events, 0.1 us)
Async XLA Ops:
  3.0 15.2 %collective-permute-start = (bf16[4,128,256]{2,1,0:T(8,128)(2,1)}, bf16[4,128,256]{2,1,0:T(8,128)(2,1)S(1)}, u32[]{:S(2)}, u32[]{:S(2)}) collective-permute-start(bf16[4,128,256]{2,1,0:T(8,128)(2,1)} %get-tuple-element.69), channel_id=1, source_target_pairs={{0,1},{1,0},{2,3},{3,2},{4,5},{5,4},{6,7},{7,6},{8,9},{9,8},{10,11... | collective-permute-start | bytes 786440 | tf_op jit(solution)/shard_map/ppermute | solution.py:509
  3.5 14.7 %collective-permute-start.1 = (bf16[4,128,256]{2,1,0:T(8,128)(2,1)}, bf16[4,128,256]{2,1,0:T(8,128)(2,1)S(1)}, u32[]{:S(2)}, u32[]{:S(2)}) collective-permute-start(bf16[4,128,256]{2,1,0:T(8,128)(2,1)} %get-tuple-element.70), channel_id=1, source_target_pairs={{0,2},{1,3},{2,0},{3,1},{4,6},{5,7},{6,4},{7,5},{8,10},{9,11},{10,... | collective-permute-start | bytes 786440 | tf_op jit(solution)/shard_map/ppermute | solution.py:509
  6.1 12.5 %collective-permute-start.2 = (bf16[4,128,256]{2,1,0:T(8,128)(2,1)}, bf16[4,128,256]{2,1,0:T(8,128)(2,1)S(1)}, u32[]{:S(2)}, u32[]{:S(2)}) collective-permute-start(bf16[4,128,256]{2,1,0:T(8,128)(2,1)} %get-tuple-element.71), channel_id=1, source_target_pairs={{0,3},{1,2},{2,1},{3,0},{4,7},{5,6},{6,5},{7,4},{8,11},{9,10},{10,... | collective-permute-start | bytes 786440 | tf_op jit(solution)/shard_map/ppermute | solution.py:509
  15.5 3.0 %copy-start.3 = (bf16[256,256]{1,0:T(8,128)(2,1)S(1)}, bf16[256,256]{1,0:T(8,128)(2,1)}, u32[]{:S(2)}) copy-start(bf16[256,256]{1,0:T(8,128)(2,1)} %w_ref.7) | copy-start | bytes 393220
  15.5 3.0 %copy-start.11 = (s32[16]{0:T(128)S(1)}, s32[16]{0:T(128)}, u32[]{:S(2)}) copy-start(s32[16]{0:T(128)} %get-tuple-element.65.slots) | copy-start | bytes 196
  16.1 8.7 %collective-permute-start.3 = (bf16[4,128,256]{2,1,0:T(8,128)(2,1)}, bf16[4,128,256]{2,1,0:T(8,128)(2,1)S(1)}, u32[]{:S(2)}, u32[]{:S(2)}) collective-permute-start(bf16[4,128,256]{2,1,0:T(8,128)(2,1)} %get-tuple-element.81), channel_id=1, source_target_pairs={{0,1},{1,0},{2,3},{3,2},{4,5},{5,4},{6,7},{7,6},{8,9},{9,8},{10,11... | collective-permute-start | bytes 786440 | tf_op jit(solution)/shard_map/ppermute | solution.py:509
  16.3 13.7 %collective-permute-start.4 = (bf16[4,128,256]{2,1,0:T(8,128)(2,1)}, bf16[4,128,256]{2,1,0:T(8,128)(2,1)S(1)}, u32[]{:S(2)}, u32[]{:S(2)}) collective-permute-start(bf16[4,128,256]{2,1,0:T(8,128)(2,1)} %get-tuple-element.82), channel_id=1, source_target_pairs={{0,2},{1,3},{2,0},{3,1},{4,6},{5,7},{6,4},{7,5},{8,10},{9,11},{10,... | collective-permute-start | bytes 786440 | tf_op jit(solution)/shard_map/ppermute | solution.py:509
  18.2 11.9 %collective-permute-start.5 = (bf16[4,128,256]{2,1,0:T(8,128)(2,1)}, bf16[4,128,256]{2,1,0:T(8,128)(2,1)S(1)}, u32[]{:S(2)}, u32[]{:S(2)}) collective-permute-start(bf16[4,128,256]{2,1,0:T(8,128)(2,1)} %get-tuple-element.83), channel_id=1, source_target_pairs={{0,3},{1,2},{2,1},{3,0},{4,7},{5,6},{6,5},{7,4},{8,11},{9,10},{10,... | collective-permute-start | bytes 786440 | tf_op jit(solution)/shard_map/ppermute | solution.py:509
  18.6 6.4 %copy-start = (bf16[2,2048,256]{2,1,0:T(8,128)(2,1)S(1)}, bf16[2,2048,256]{2,1,0:T(8,128)(2,1)}, u32[]{:S(2)}) copy-start(bf16[2,2048,256]{2,1,0:T(8,128)(2,1)} %param.12) | copy-start | bytes 6291460
  18.6 6.4 %copy-start.9 = (s32[2,64,4]{1,2,0:T(4,128)S(1)}, s32[2,64,4]{1,2,0:T(4,128)}, u32[]{:S(2)}) copy-start(s32[2,64,4]{1,2,0:T(4,128)} %param.14) | copy-start | bytes 6148
  20.5 13.5 %collective-permute-start.6 = (bf16[4,128,256]{2,1,0:T(8,128)(2,1)S(1)}, bf16[4,128,256]{2,1,0:T(8,128)(2,1)S(1)}, u32[]{:S(2)}, u32[]{:S(2)}) collective-permute-start(bf16[4,128,256]{2,1,0:T(8,128)(2,1)S(1)} %get-tuple-element.85), channel_id=1, source_target_pairs={{0,4},{4,0},{8,12},{12,8},{1,5},{5,1},{9,13},{13,9},{2,6},{6,2},{1... | collective-permute-start | bytes 786440 | tf_op jit(solution)/shard_map/ppermute | solution.py:426
  22.2 21.8 %collective-permute-start.7 = (bf16[4,128,256]{2,1,0:T(8,128)(2,1)S(1)}, bf16[4,128,256]{2,1,0:T(8,128)(2,1)S(1)}, u32[]{:S(2)}, u32[]{:S(2)}) collective-permute-start(bf16[4,128,256]{2,1,0:T(8,128)(2,1)S(1)} %get-tuple-element.86), channel_id=1, source_target_pairs={{0,8},{4,12},{8,0},{12,4},{1,9},{5,13},{9,1},{13,5},{2,10},{6,14},... | collective-permute-start | bytes 786440 | tf_op jit(solution)/shard_map/ppermute | solution.py:426
  24.8 25.2 %collective-permute-start.11 = (bf16[4,128,256]{2,1,0:T(8,128)(2,1)S(1)}, bf16[4,128,256]{2,1,0:T(8,128)(2,1)S(1)}, u32[]{:S(2)}, u32[]{:S(2)}) collective-permute-start(bf16[4,128,256]{2,1,0:T(8,128)(2,1)S(1)} %get-tuple-element.96), channel_id=1, source_target_pairs={{0,12},{4,8},{8,4},{12,0},{1,13},{5,9},{9,5},{13,1},{2,14},{6,10},... | collective-permute-start | bytes 786440 | tf_op jit(solution)/shard_map/ppermute | solution.py:426
  30.1 19.9 %copy-start.4 = (bf16[256,256]{1,0:T(8,128)(2,1)S(1)}, bf16[256,256]{1,0:T(8,128)(2,1)}, u32[]{:S(2)}) copy-start(bf16[256,256]{1,0:T(8,128)(2,1)} %wq_ref.1) | copy-start | bytes 393220
  30.1 19.9 %copy-start.5 = (bf16[256,256]{1,0:T(8,128)(2,1)S(1)}, bf16[256,256]{1,0:T(8,128)(2,1)}, u32[]{:S(2)}) copy-start(bf16[256,256]{1,0:T(8,128)(2,1)} %wk_ref.1) | copy-start | bytes 393220
  30.1 19.9 %copy-start.6 = (bf16[256,256]{1,0:T(8,128)(2,1)S(1)}, bf16[256,256]{1,0:T(8,128)(2,1)}, u32[]{:S(2)}) copy-start(bf16[256,256]{1,0:T(8,128)(2,1)} %wv_ref.1) | copy-start | bytes 393220
  30.1 19.9 %copy-start.7 = (bf16[256,256]{1,0:T(8,128)(2,1)S(1)}, bf16[256,256]{1,0:T(8,128)(2,1)}, u32[]{:S(2)}) copy-start(bf16[256,256]{1,0:T(8,128)(2,1)} %wo_ref.1) | copy-start | bytes 393220
  30.1 19.9 %copy-start.10 = (bf16[8,256]{1,0:T(8,128)(2,1)S(1)}, bf16[8,256]{1,0:T(8,128)(2,1)}, u32[]{:S(2)}) copy-start(bf16[8,256]{1,0:T(8,128)(2,1)} %pos_ref.1) | copy-start | bytes 12292
  30.2 31.7 %copy-start.8 = (f32[1024]{0:T(1024)S(1)}, f32[1024]{0:T(1024)}, u32[]{:S(2)}) copy-start(f32[1024]{0:T(1024)} %param.22) | copy-start | bytes 12292
  32.9 28.9 %copy-start.1 = (bf16[256,1024]{1,0:T(8,128)(2,1)S(1)}, bf16[256,1024]{1,0:T(8,128)(2,1)}, u32[]{:S(2)}) copy-start(bf16[256,1024]{1,0:T(8,128)(2,1)} %refs_11_.7) | copy-start | bytes 1572868
  33.0 28.9 %copy-start.2 = (bf16[1024,256]{1,0:T(8,128)(2,1)S(1)}, bf16[1024,256]{1,0:T(8,128)(2,1)}, u32[]{:S(2)}) copy-start(bf16[1024,256]{1,0:T(8,128)(2,1)} %refs_13_.7) | copy-start | bytes 1572868
  34.6 9.7 %collective-permute-start.8 = (bf16[1,128,256]{2,1,0:T(8,128)(2,1)}, bf16[1,128,256]{2,1,0:T(8,128)(2,1)S(1)}, u32[]{:S(2)}, u32[]{:S(2)}) collective-permute-start(bf16[1,128,256]{2,1,0:T(8,128)(2,1)} %get-tuple-element.90), channel_id=1, source_target_pairs={{0,4},{4,0},{8,12},{12,8},{1,5},{5,1},{9,13},{13,9},{2,6},{6,2},{1... | collective-permute-start | bytes 196616 | tf_op jit(solution)/shard_map/ppermute | solution.py:426
  35.2 26.7 %collective-permute-start.13 = (bf16[1,128,256]{2,1,0:T(8,128)(2,1)}, bf16[1,128,256]{2,1,0:T(8,128)(2,1)S(1)}, u32[]{:S(2)}, u32[]{:S(2)}) collective-permute-start(bf16[1,128,256]{2,1,0:T(8,128)(2,1)} %get-tuple-element.102), channel_id=1, source_target_pairs={{0,8},{4,12},{8,0},{12,4},{1,9},{5,13},{9,1},{13,5},{2,10},{6,14},... | collective-permute-start | bytes 196616 | tf_op jit(solution)/shard_map/ppermute | solution.py:426
  38.3 23.6 %collective-permute-start.14 = (bf16[1,128,256]{2,1,0:T(8,128)(2,1)}, bf16[1,128,256]{2,1,0:T(8,128)(2,1)S(1)}, u32[]{:S(2)}, u32[]{:S(2)}) collective-permute-start(bf16[1,128,256]{2,1,0:T(8,128)(2,1)} %get-tuple-element.103), channel_id=1, source_target_pairs={{0,12},{4,8},{8,4},{12,0},{1,13},{5,9},{9,5},{13,1},{2,14},{6,10},... | collective-permute-start | bytes 196616 | tf_op jit(solution)/shard_map/ppermute | solution.py:426
  44.8 24.5 %collective-permute-start.9 = (bf16[3,128,256]{2,1,0:T(8,128)(2,1)}, bf16[3,128,256]{2,1,0:T(8,128)(2,1)S(1)}, u32[]{:S(2)}, u32[]{:S(2)}) collective-permute-start(bf16[3,128,256]{2,1,0:T(8,128)(2,1)} %get-tuple-element.94), channel_id=1, source_target_pairs={{0,4},{4,0},{8,12},{12,8},{1,5},{5,1},{9,13},{13,9},{2,6},{6,2},{1... | collective-permute-start | bytes 589832 | tf_op jit(solution)/shard_map/ppermute | solution.py:426
  46.7 24.0 %collective-permute-start.10 = (bf16[3,128,256]{2,1,0:T(8,128)(2,1)}, bf16[3,128,256]{2,1,0:T(8,128)(2,1)S(1)}, u32[]{:S(2)}, u32[]{:S(2)}) collective-permute-start(bf16[3,128,256]{2,1,0:T(8,128)(2,1)} %get-tuple-element.95), channel_id=1, source_target_pairs={{0,8},{4,12},{8,0},{12,4},{1,9},{5,13},{9,1},{13,5},{2,10},{6,14},... | collective-permute-start | bytes 589832 | tf_op jit(solution)/shard_map/ppermute | solution.py:426
  50.0 20.6 %collective-permute-start.12 = (bf16[3,128,256]{2,1,0:T(8,128)(2,1)}, bf16[3,128,256]{2,1,0:T(8,128)(2,1)S(1)}, u32[]{:S(2)}, u32[]{:S(2)}) collective-permute-start(bf16[3,128,256]{2,1,0:T(8,128)(2,1)} %get-tuple-element.97), channel_id=1, source_target_pairs={{0,12},{4,8},{8,4},{12,0},{1,13},{5,9},{9,5},{13,1},{2,14},{6,10},... | collective-permute-start | bytes 589832 | tf_op jit(solution)/shard_map/ppermute | solution.py:426
  66.1 20.3 %collective-permute-start.15 = (bf16[2,128,256]{2,1,0:T(8,128)(2,1)}, bf16[2,128,256]{2,1,0:T(8,128)(2,1)S(1)}, u32[]{:S(2)}, u32[]{:S(2)}) collective-permute-start(bf16[2,128,256]{2,1,0:T(8,128)(2,1)} %get-tuple-element.105), channel_id=1, source_target_pairs={{0,4},{4,0},{8,12},{12,8},{1,5},{5,1},{9,13},{13,9},{2,6},{6,2},{1... | collective-permute-start | bytes 393224 | tf_op jit(solution)/shard_map/ppermute | solution.py:426
  68.2 19.8 %collective-permute-start.16 = (bf16[2,128,256]{2,1,0:T(8,128)(2,1)}, bf16[2,128,256]{2,1,0:T(8,128)(2,1)S(1)}, u32[]{:S(2)}, u32[]{:S(2)}) collective-permute-start(bf16[2,128,256]{2,1,0:T(8,128)(2,1)} %get-tuple-element.106), channel_id=1, source_target_pairs={{0,8},{4,12},{8,0},{12,4},{1,9},{5,13},{9,1},{13,5},{2,10},{6,14},... | collective-permute-start | bytes 393224 | tf_op jit(solution)/shard_map/ppermute | solution.py:426
  69.3 19.3 %collective-permute-start.17 = (bf16[2,128,256]{2,1,0:T(8,128)(2,1)}, bf16[2,128,256]{2,1,0:T(8,128)(2,1)S(1)}, u32[]{:S(2)}, u32[]{:S(2)}) collective-permute-start(bf16[2,128,256]{2,1,0:T(8,128)(2,1)} %get-tuple-element.107), channel_id=1, source_target_pairs={{0,12},{4,8},{8,4},{12,0},{1,13},{5,9},{9,5},{13,1},{2,14},{6,10},... | collective-permute-start | bytes 393224 | tf_op jit(solution)/shard_map/ppermute | solution.py:426
  74.2 20.2 %collective-permute-start.24 = (bf16[2,128,256]{2,1,0:T(8,128)(2,1)}, bf16[2,128,256]{2,1,0:T(8,128)(2,1)S(1)}, u32[]{:S(2)}, u32[]{:S(2)}) collective-permute-start(bf16[2,128,256]{2,1,0:T(8,128)(2,1)} %get-tuple-element.117), channel_id=1, source_target_pairs={{0,4},{4,0},{8,12},{12,8},{1,5},{5,1},{9,13},{13,9},{2,6},{6,2},{1... | collective-permute-start | bytes 393224 | tf_op jit(solution)/shard_map/ppermute | solution.py:426
  80.5 15.9 %collective-permute-start.25 = (bf16[2,128,256]{2,1,0:T(8,128)(2,1)}, bf16[2,128,256]{2,1,0:T(8,128)(2,1)S(1)}, u32[]{:S(2)}, u32[]{:S(2)}) collective-permute-start(bf16[2,128,256]{2,1,0:T(8,128)(2,1)} %get-tuple-element.118), channel_id=1, source_target_pairs={{0,8},{4,12},{8,0},{12,4},{1,9},{5,13},{9,1},{13,5},{2,10},{6,14},... | collective-permute-start | bytes 393224 | tf_op jit(solution)/shard_map/ppermute | solution.py:426
  82.6 3.8 %copy-start.14 = (bf16[2,128,256]{2,1,0:T(8,128)(2,1)S(1)}, bf16[2,128,256]{2,1,0:T(8,128)(2,1)}, u32[]{:S(2)}) copy-start(bf16[2,128,256]{2,1,0:T(8,128)(2,1)} %get-tuple-element.119) | copy-start | bytes 393220
  86.4 11.0 %collective-permute-start.26 = (bf16[2,128,256]{2,1,0:T(8,128)(2,1)S(1)}, bf16[2,128,256]{2,1,0:T(8,128)(2,1)S(1)}, u32[]{:S(2)}, u32[]{:S(2)}) collective-permute-start(bf16[2,128,256]{2,1,0:T(8,128)(2,1)S(1)} %copy-done.14), channel_id=1, source_target_pairs={{0,12},{4,8},{8,4},{12,0},{1,13},{5,9},{9,5},{13,1},{2,14},{6,10},... | collective-permute-start | bytes 393224 | tf_op jit(solution)/shard_map/ppermute | solution.py:426
  87.9 11.0 %collective-permute-start.21 = (bf16[2,128,256]{2,1,0:T(8,128)(2,1)}, bf16[2,128,256]{2,1,0:T(8,128)(2,1)S(1)}, u32[]{:S(2)}, u32[]{:S(2)}) collective-permute-start(bf16[2,128,256]{2,1,0:T(8,128)(2,1)} %get-tuple-element.114), channel_id=1, source_target_pairs={{0,4},{4,0},{8,12},{12,8},{1,5},{5,1},{9,13},{13,9},{2,6},{6,2},{1... | collective-permute-start | bytes 393224 | tf_op jit(solution)/shard_map/ppermute | solution.py:426
  89.3 5.1 %copy-start.13 = (bf16[2,128,256]{2,1,0:T(8,128)(2,1)S(1)}, bf16[2,128,256]{2,1,0:T(8,128)(2,1)}, u32[]{:S(2)}) copy-start(bf16[2,128,256]{2,1,0:T(8,128)(2,1)} %get-tuple-element.115) | copy-start | bytes 393220
  89.3 7.1 %copy-start.12 = (bf16[2,128,256]{2,1,0:T(8,128)(2,1)S(1)}, bf16[2,128,256]{2,1,0:T(8,128)(2,1)}, u32[]{:S(2)}) copy-start(bf16[2,128,256]{2,1,0:T(8,128)(2,1)} %get-tuple-element.116) | copy-start | bytes 393220
  92.9 17.6 %collective-permute-start.18 = (bf16[2,128,256]{2,1,0:T(8,128)(2,1)}, bf16[2,128,256]{2,1,0:T(8,128)(2,1)S(1)}, u32[]{:S(2)}, u32[]{:S(2)}) collective-permute-start(bf16[2,128,256]{2,1,0:T(8,128)(2,1)} %get-tuple-element.111), channel_id=1, source_target_pairs={{0,4},{4,0},{8,12},{12,8},{1,5},{5,1},{9,13},{13,9},{2,6},{6,2},{1... | collective-permute-start | bytes 393224 | tf_op jit(solution)/shard_map/ppermute | solution.py:426
  94.4 15.3 %collective-permute-start.22 = (bf16[2,128,256]{2,1,0:T(8,128)(2,1)S(1)}, bf16[2,128,256]{2,1,0:T(8,128)(2,1)S(1)}, u32[]{:S(2)}, u32[]{:S(2)}) collective-permute-start(bf16[2,128,256]{2,1,0:T(8,128)(2,1)S(1)} %copy-done.13), channel_id=1, source_target_pairs={{0,8},{4,12},{8,0},{12,4},{1,9},{5,13},{9,1},{13,5},{2,10},{6,14},... | collective-permute-start | bytes 393224 | tf_op jit(solution)/shard_map/ppermute | solution.py:426
  96.4 13.3 %collective-permute-start.23 = (bf16[2,128,256]{2,1,0:T(8,128)(2,1)S(1)}, bf16[2,128,256]{2,1,0:T(8,128)(2,1)S(1)}, u32[]{:S(2)}, u32[]{:S(2)}) collective-permute-start(bf16[2,128,256]{2,1,0:T(8,128)(2,1)S(1)} %copy-done.12), channel_id=1, source_target_pairs={{0,12},{4,8},{8,4},{12,0},{1,13},{5,9},{9,5},{13,1},{2,14},{6,10},... | collective-permute-start | bytes 393224 | tf_op jit(solution)/shard_map/ppermute | solution.py:426
  97.4 17.6 %collective-permute-start.19 = (bf16[2,128,256]{2,1,0:T(8,128)(2,1)}, bf16[2,128,256]{2,1,0:T(8,128)(2,1)S(1)}, u32[]{:S(2)}, u32[]{:S(2)}) collective-permute-start(bf16[2,128,256]{2,1,0:T(8,128)(2,1)} %get-tuple-element.112), channel_id=1, source_target_pairs={{0,8},{4,12},{8,0},{12,4},{1,9},{5,13},{9,1},{13,5},{2,10},{6,14},... | collective-permute-start | bytes 393224 | tf_op jit(solution)/shard_map/ppermute | solution.py:426
  98.9 16.2 %collective-permute-start.20 = (bf16[2,128,256]{2,1,0:T(8,128)(2,1)}, bf16[2,128,256]{2,1,0:T(8,128)(2,1)S(1)}, u32[]{:S(2)}, u32[]{:S(2)}) collective-permute-start(bf16[2,128,256]{2,1,0:T(8,128)(2,1)} %get-tuple-element.113), channel_id=1, source_target_pairs={{0,12},{4,8},{8,4},{12,0},{1,13},{5,9},{9,5},{13,1},{2,14},{6,10},... | collective-permute-start | bytes 393224 | tf_op jit(solution)/shard_map/ppermute | solution.py:426

commit v5 on v4

--- a/solution.py
+++ b/solution.py
@@ -10,7 +10,7 @@
 
 HEADS = 8
 LANES = 128
-LAG = 2
+LAG = 3
 ALONE, ROOM = 60, (57, 46)
 GATHER_US, GATE_US, NEAR_US, FAR_US, TEMPORAL_US, PLACE_US = 3, 0.5, 3, 2, 3, 1
 NEG = -1e30
@@ -262,7 +262,8 @@
     return [out[e * n_snap : (e + 1) * n_snap] for e in range(len(parts))], done
 
 
-def prepare_kernel(after_ref, pos_ref, wq_ref, wk_ref, wv_ref, wo_ref, pos, wqkv, wo):
+def prepare_kernel(after_ref, pos_ref, wq_ref, wk_ref, wv_ref, wo_ref, pos, wqkv, wo, done_ref):
+    done_ref[0] = jnp.int32(0)
     width = wo.shape[0]
     head_dim = width // HEADS
     to = lax.broadcasted_iota(jnp.int32, (width, width), 0)
@@ -287,9 +288,10 @@
             pltpu.VMEM(pos.shape, F32),
             pltpu.VMEM((3 * width, width), BF16),
             pltpu.VMEM((width, width), BF16),
+            jax.ShapeDtypeStruct((1,), jnp.int32),
         ],
         in_specs=[pl.BlockSpec(memory_space=pltpu.SMEM)] + [vmem] * 5,
-        out_specs=[vmem] * 3,
+        out_specs=[vmem] * 3 + [pl.BlockSpec(memory_space=pltpu.SMEM)],
         compiler_params=pltpu.CompilerParams(vmem_limit_bytes=4 << 20),
         cost_estimate=cost(1),
         name="prepare",
@@ -497,7 +499,7 @@
     for t in range(snap_dev):
         some, done = gather_blocks(done, nbr, feat, t, most, n_clus)
         sets.append(some)
-    got, parts, prepared = [], [], None
+    got, parts = [], []
     for t in range(snap_dev):
         near = near_sum(done, nbr, feat, adj_tiles, w_struct, t, n_clus, most, ROOM[min(t, 1)])
         if t == 0:
@@ -511,14 +513,14 @@
         last = t == snap_dev - 1 and fast and chunks > 1
         parts.append([(0, 1), (1, chunks)] if last else [(0, chunks)])
         sent, done = far_sum(near, remote, w_struct, groups, parts[-1], t == 0)
+        if t == 0 and fast:
+            *prepared, done = prepare(done, pos_embed, w_query, w_key, w_value, w_out)
         got.append([])
         for e, part in enumerate(sent):
             if t > 0 and n_snap > 2:
-                waits = got[-2][-1][1:2] if e == 0 else got[-2][-1][2:3] + got[-1][-1][1:2]
+                waits = got[-2][-1][1:2] if e == 0 else got[-1][-1][1:2]
                 part[1:], done = gate(waits, part[1:])
             got[-1].append([x if d == 0 else shift(x, d, n_snap) for d, x in enumerate(part)])
-        if t == 0 and fast:
-            prepared = prepare(done, pos_embed, w_query, w_key, w_value, w_out)
     if fast:
         weights = (*prepared, w_up, up_bias.reshape(1, -1), w_down)
         return temporal_fast(got, parts, weights, n_snap, [done])

time: 116 us -> 116 us (level)
  transfers between devices with their start and end apart: 27 -> 27, of which waited for: 8 -> 5; matrix products, arithmetic and copies ran while one was open for 0% -> 0% of each run, Pallas kernels for 34% -> 34%
where the time goes in v5:
time: 116 us
  starting transfers between devices  44.1 us (38%)
  Pallas kernels  43 us (37%)
  waiting for transfers between devices  27.8 us (24%)
    ppermute x21, starting transfers between devices, shift(): return lax.ppermute(x, 'snap', [(i, partner(i, d, n)) for i in range(n)])  38.8 us
    ppermute x21, waiting for transfers between devices, shift(): return lax.ppermute(x, 'snap', [(i, partner(i, d, n)) for i in range(n)])  27.4 us
    pallas_call x4, Pallas kernels, temporal_chunk(): pl.pallas_call(functools.partial(temporal_kernel, n_snap, per, blocks, ch...  15.2 us
    pallas_call x2, Pallas kernels, near_sum(): pl.pallas_call(functools.partial(near_kernel, t, n_clus, most), out_shape...  10.3 us
    pallas_call x2, Pallas kernels, gather_blocks(): pl.pallas_call(functools.partial(gather_kernel, t, most, n_clus, direct),...  7.04 us
    ppermute x6, starting transfers between devices, on_device(): remote[d] = lax.ppermute(sets[t][d - 1], 'clus', pairs)  5.29 us
    pallas_call x2, Pallas kernels, far_sum(): pl.pallas_call(functools.partial(far_kernel, n_snap, parts, direct), out_...  4.67 us
    pallas_call x4, Pallas kernels, place(): pl.pallas_call(functools.partial(place_kernel, n_snap, chunk), out_shape=...  3.08 us
  transfers between devices with their start and end apart: 27, of which 5 were waited for; matrix products, arithmetic and copies ran while one was open for 0% of the time, Pallas kernels for 34%

profile of v5, /device:TPU:0, one launch (start us, length us, event | category | flops | bytes accessed | tf_op | source)
XLA Modules:
  0.0 115.5 jit_solution(3624424679495559519)
XLA Ops:
  0.0 3.0 %gather_blocks.2 = (bf16[4,128,256]{2,1,0:T(8,128)(2,1)}, bf16[4,128,256]{2,1,0:T(8,128)(2,1)}, bf16[4,128,256]{2,1,0:T(8,128)(2,1)}, s32[1]{0:T(128)}) custom-call(s32[1]{0:T(128)} %constant.0.clone.1.after_ref, s32[2,4,64]{2,1,0:T(4,128)} %bitcast.11, bf16[2,16,128,256]{3,2,1,0:T(8,128)(2,1)} %bitcast.3), custom_call_target="tpu_custom_call" | custom-call | bytes 90000 | tf_op jit(solution)/shard_map/gather_blocks/pallas_call | solution.py:92
  3.0 0.5 collective-permute-start
  3.5 2.6 %collective-permute-start.1 = (bf16[4,128,256]{2,1,0:T(8,128)(2,1)}, bf16[4,128,256]{2,1,0:T(8,128)(2,1)S(1)}, u32[]{:S(2)}, u32[]{:S(2)}) collective-permute-start(bf16[4,128,256]{2,1,0:T(8,128)(2,1)} %get-tuple-element.71), channel_id=1, source_target_pairs={{0,2},{1,3},{2,0},{3,1},{4,6},{5,7},{6,4},{7,5},{8,10},{9,11},{10,... | collective-permute-start | bytes 786440 | tf_op jit(solution)/shard_map/ppermute | solution.py:511
  6.1 0.1 collective-permute-start.2
  6.2 4.0 %gather_blocks.3 = (bf16[4,128,256]{2,1,0:T(8,128)(2,1)}, bf16[4,128,256]{2,1,0:T(8,128)(2,1)}, bf16[4,128,256]{2,1,0:T(8,128)(2,1)}, s32[1]{0:T(128)}) custom-call(s32[1]{0:T(128)} %get-tuple-element.64.after_ref, s32[2,4,64]{2,1,0:T(4,128)} %bitcast.12, bf16[2,16,128,256]{3,2,1,0:T(8,128)(2,1)} %bitcast.4), custom_call_target="tpu_custom_call" | custom-call | bytes 90000 | tf_op jit(solution)/shard_map/gather_blocks/pallas_call | solution.py:92
  10.2 5.3 %near_sum.2 = (f32[16,128,256]{2,1,0:T(8,128)S(1)}, bf16[16,128,256]{2,1,0:T(8,128)(2,1)S(1)}, bf16[16,4,128,128]{3,2,1,0:T(8,128)(2,1)S(1)}, s32[16]{0:T(128)}) custom-call(s32[1]{0:T(128)} %get-tuple-element.65.after_ref, s32[2,4,64]{2,1,0:T(4,128)} %bitcast.13, bf16[2,16,128,256]{3,2,1,0:T(8,128)(2,1)} %bitcast.5, bf16[2,16,4,128,128]{4,3,2,1,0:T(8,128)(2,1)} %adj_ref.3, ...), custom_call_target="tpu_custom_call" | custom-call | bytes 90000 | tf_op jit(solution)/shard_map/near_sum/pallas_call | solution.py:183
  15.5 0.0 copy-start.3
  15.6 0.5 gate.3
  16.1 0.2 collective-permute-start.3
  16.3 1.9 %collective-permute-start.4 = (bf16[4,128,256]{2,1,0:T(8,128)(2,1)}, bf16[4,128,256]{2,1,0:T(8,128)(2,1)S(1)}, u32[]{:S(2)}, u32[]{:S(2)}) collective-permute-start(bf16[4,128,256]{2,1,0:T(8,128)(2,1)} %get-tuple-element.84), channel_id=1, source_target_pairs={{0,2},{1,3},{2,0},{3,1},{4,6},{5,7},{6,4},{7,5},{8,10},{9,11},{10,... | collective-permute-start | bytes 786440 | tf_op jit(solution)/shard_map/ppermute | solution.py:511
  18.2 0.0 collective-permute-done.refs_0_
  18.2 0.0 collective-permute-start.5
  18.2 0.3 collective-permute-done.2.refs_2_
  18.6 0.0 copy-start.6
  18.6 0.0 copy-start.7
  18.6 0.0 copy-start.10
  18.6 0.0 copy-start
  18.6 0.0 copy-start.9
  18.6 1.9 %far_sum.2 = (bf16[4,128,256]{2,1,0:T(8,128)(2,1)S(1)}, bf16[4,128,256]{2,1,0:T(8,128)(2,1)S(1)}, bf16[4,128,256]{2,1,0:T(8,128)(2,1)S(1)}, bf16[4,128,256]{2,1,0:T(8,128)(2,1)S(1)}, s32[1]{0:T(128)}) custom-call(s32[16]{0:T(128)S(1)} %copy-done.11, f32[16,128,256]{2,1,0:T(8,128)S(1)} %get-tuple-element.67.acc_ref.refs_0_, ...), custom_call_target="tpu_custom_call" | custom-call | bytes 60000 | tf_op jit(solution)/shard_map/far_sum/pallas_call | solution.py:244
  20.6 1.7 %collective-permute-start.6 = (bf16[4,128,256]{2,1,0:T(8,128)(2,1)S(1)}, bf16[4,128,256]{2,1,0:T(8,128)(2,1)S(1)}, u32[]{:S(2)}, u32[]{:S(2)}) collective-permute-start(bf16[4,128,256]{2,1,0:T(8,128)(2,1)S(1)} %get-tuple-element.87), channel_id=1, source_target_pairs={{0,4},{4,0},{8,12},{12,8},{1,5},{5,1},{9,13},{13,9},{2,6},{6,2},{1... | collective-permute-start | bytes 786440 | tf_op jit(solution)/shard_map/ppermute | solution.py:428
  22.3 2.6 %collective-permute-start.9 = (bf16[4,128,256]{2,1,0:T(8,128)(2,1)S(1)}, bf16[4,128,256]{2,1,0:T(8,128)(2,1)S(1)}, u32[]{:S(2)}, u32[]{:S(2)}) collective-permute-start(bf16[4,128,256]{2,1,0:T(8,128)(2,1)S(1)} %get-tuple-element.96), channel_id=1, source_target_pairs={{0,8},{4,12},{8,0},{12,4},{1,9},{5,13},{9,1},{13,5},{2,10},{6,14},... | collective-permute-start | bytes 786440 | tf_op jit(solution)/shard_map/ppermute | solution.py:428
  24.9 0.1 collective-permute-start.11
  25.0 1.2 %prepare.1 = (f32[8,256]{1,0:T(8,128)S(1)}, bf16[768,256]{1,0:T(8,128)(2,1)S(1)}, bf16[256,256]{1,0:T(8,128)(2,1)S(1)}, s32[1]{0:T(128)}) custom-call(s32[1]{0:T(128)} %get-tuple-element.74.after_ref, bf16[8,256]{1,0:T(8,128)(2,1)S(1)} %copy-done.10, bf16[256,256]{1,0:T(8,128)(2,1)S(1)} %copy-done.4, bf16[256,256]{1,0:T(8,128)(2,1)S(1)} %copy-done.5, ...), custom_call_target="tpu_custom_call" | custom-call | bytes 30000 | tf_op jit(solution)/shard_map/prepare/pallas_call | solution.py:285
  26.3 5.0 %near_sum.3 = (f32[16,128,256]{2,1,0:T(8,128)S(1)}, bf16[16,128,256]{2,1,0:T(8,128)(2,1)S(1)}, bf16[16,4,128,128]{3,2,1,0:T(8,128)(2,1)S(1)}, s32[16]{0:T(128)S(1)}) custom-call(s32[1]{0:T(128)} %get-tuple-element.75.after_ref, s32[2,4,64]{2,1,0:T(4,128)S(1)} %bitcast.14, bf16[2,16,128,256]{3,2,1,0:T(8,128)(2,1)S(1)} %bitcast.6, ...), custom_call_target="tpu_custom_call" | custom-call | bytes 90000 | tf_op jit(solution)/shard_map/near_sum/pallas_call | solution.py:183
  31.3 0.0 collective-permute-done.4.refs_1_
  31.3 0.0 copy-start.1
  31.3 0.0 copy-start.2
  31.3 0.0 copy-start.8
  31.3 2.8 %far_sum.3 = (bf16[1,128,256]{2,1,0:T(8,128)(2,1)S(1)}, bf16[1,128,256]{2,1,0:T(8,128)(2,1)}, bf16[1,128,256]{2,1,0:T(8,128)(2,1)}, bf16[1,128,256]{2,1,0:T(8,12...) custom-call(s32[16]{0:T(128)S(1)} %get-tuple-element.76.slots, ...), custom_call_target="tpu_custom_call" | custom-call | bytes 60000 | tf_op jit(solution)/shard_map/far_sum/pallas_call | solution.py:244
  34.1 0.0 collective-permute-done.6.refs_0_.refs_2_
  34.1 0.5 gate.4
  34.6 0.8 collective-permute-start.7
  35.5 3.5 %collective-permute-start.13 = (bf16[1,128,256]{2,1,0:T(8,128)(2,1)}, bf16[1,128,256]{2,1,0:T(8,128)(2,1)S(1)}, u32[]{:S(2)}, u32[]{:S(2)}) collective-permute-start(bf16[1,128,256]{2,1,0:T(8,128)(2,1)} %get-tuple-element.104), channel_id=1, source_target_pairs={{0,8},{4,12},{8,0},{12,4},{1,9},{5,13},{9,1},{13,5},{2,10},{6,14},... | collective-permute-start | bytes 196616 | tf_op jit(solution)/shard_map/ppermute | solution.py:428
  38.9 0.1 collective-permute-start.14
  39.1 5.2 %collective-permute-done.7.refs_0_.refs_3_ = bf16[1,128,256]{2,1,0:T(8,128)(2,1)S(1)} collective-permute-done((bf16[1,128,256]{2,1,0:T(8,128)(2,1)}, bf16[1,128,256]{2,1,0:T(8,128)(2,1)S(1)}, u32[]{:S(2)}, u32[]{:S(2)}) %collective-permute-start.7) | collective-permute-done | bytes 65568 | tf_op jit(solution)/shard_map/ppermute | solution.py:428
  44.2 0.5 gate.5
  44.8 0.1 collective-permute-start.8
  44.9 2.5 %collective-permute-start.10 = (bf16[3,128,256]{2,1,0:T(8,128)(2,1)}, bf16[3,128,256]{2,1,0:T(8,128)(2,1)S(1)}, u32[]{:S(2)}, u32[]{:S(2)}) collective-permute-start(bf16[3,128,256]{2,1,0:T(8,128)(2,1)} %get-tuple-element.97), channel_id=1, source_target_pairs={{0,8},{4,12},{8,0},{12,4},{1,9},{5,13},{9,1},{13,5},{2,10},{6,14},... | collective-permute-start | bytes 589832 | tf_op jit(solution)/shard_map/ppermute | solution.py:428
  47.3 0.0 collective-permute-done.11.refs_6_
  47.3 1.9 %collective-permute-start.12 = (bf16[3,128,256]{2,1,0:T(8,128)(2,1)}, bf16[3,128,256]{2,1,0:T(8,128)(2,1)S(1)}, u32[]{:S(2)}, u32[]{:S(2)}) collective-permute-start(bf16[3,128,256]{2,1,0:T(8,128)(2,1)} %get-tuple-element.99), channel_id=1, source_target_pairs={{0,12},{4,8},{8,4},{12,0},{1,13},{5,9},{9,5},{13,1},{2,14},{6,10},... | collective-permute-start | bytes 589832 | tf_op jit(solution)/shard_map/ppermute | solution.py:428
  49.2 12.7 %collective-permute-done.13.refs_5_ = bf16[1,128,256]{2,1,0:T(8,128)(2,1)S(1)} collective-permute-done((bf16[1,128,256]{2,1,0:T(8,128)(2,1)}, bf16[1,128,256]{2,1,0:T(8,128)(2,1)S(1)}, u32[]{:S(2)}, u32[]{:S(2)}) %collective-permute-start.13) | collective-permute-done | bytes 65568 | tf_op jit(solution)/shard_map/ppermute | solution.py:428
  61.9 4.3 %temporal_chunk.4 = (bf16[2,2048,256]{2,1,0:T(8,128)(2,1)}, bf16[2,128,256]{2,1,0:T(8,128)(2,1)}, bf16[2,128,256]{2,1,0:T(8,128)(2,1)}, bf16[2,128,256]{2,1,0:T(8,128)(2,1)}) custom-call(bf16[4,128,256]{2,1,0:T(8,128)(2,1)S(1)} %get-tuple-element.73.refs_0_, bf16[1,128,256]{2,1,0:T(8,128)(2,1)S(1)} %get-tuple-element.103.refs_1_, ...), custom_call_target="tpu_custom_call" | custom-call | bytes 90000 | tf_op jit(solution)/shard_map/temporal_chunk/pallas_call | solution.py:376
  66.2 2.0 %collective-permute-start.24 = (bf16[2,128,256]{2,1,0:T(8,128)(2,1)}, bf16[2,128,256]{2,1,0:T(8,128)(2,1)S(1)}, u32[]{:S(2)}, u32[]{:S(2)}) collective-permute-start(bf16[2,128,256]{2,1,0:T(8,128)(2,1)} %get-tuple-element.119), channel_id=1, source_target_pairs={{0,4},{4,0},{8,12},{12,8},{1,5},{5,1},{9,13},{13,9},{2,6},{6,2},{1... | collective-permute-start | bytes 393224 | tf_op jit(solution)/shard_map/ppermute | solution.py:428
  68.3 1.1 collective-permute-start.25
  69.4 1.4 %collective-permute-start.26 = (bf16[2,128,256]{2,1,0:T(8,128)(2,1)}, bf16[2,128,256]{2,1,0:T(8,128)(2,1)S(1)}, u32[]{:S(2)}, u32[]{:S(2)}) collective-permute-start(bf16[2,128,256]{2,1,0:T(8,128)(2,1)} %get-tuple-element.121), channel_id=1, source_target_pairs={{0,12},{4,8},{8,4},{12,0},{1,13},{5,9},{9,5},{13,1},{2,14},{6,10},... | collective-permute-start | bytes 393224 | tf_op jit(solution)/shard_map/ppermute | solution.py:428
  70.8 3.6 %temporal_chunk.5 = (bf16[2,2048,256]{2,1,0:T(8,128)(2,1)}, bf16[2,128,256]{2,1,0:T(8,128)(2,1)}, bf16[2,128,256]{2,1,0:T(8,128)(2,1)}, bf16[2,128,256]{2,1,0:T(8,128)(2,1)}) custom-call(bf16[4,128,256]{2,1,0:T(8,128)(2,1)S(1)} %get-tuple-element.73.refs_0_, bf16[3,128,256]{2,1,0:T(8,128)(2,1)S(1)} %get-tuple-element.86.refs_1_, ...), custom_call_target="tpu_custom_call", output_to_operand_aliasing={{0}: (14, {})} | custom-call | bytes 90000 | tf_op jit(solution)/shard_map/temporal_chunk/pallas_call | solution.py:376
  74.4 6.2 %collective-permute-start.21 = (bf16[2,128,256]{2,1,0:T(8,128)(2,1)}, bf16[2,128,256]{2,1,0:T(8,128)(2,1)S(1)}, u32[]{:S(2)}, u32[]{:S(2)}) collective-permute-start(bf16[2,128,256]{2,1,0:T(8,128)(2,1)} %get-tuple-element.116), channel_id=1, source_target_pairs={{0,4},{4,0},{8,12},{12,8},{1,5},{5,1},{9,13},{13,9},{2,6},{6,2},{1... | collective-permute-start | bytes 393224 | tf_op jit(solution)/shard_map/ppermute | solution.py:428
  80.6 2.1 %collective-permute-start.22 = (bf16[2,128,256]{2,1,0:T(8,128)(2,1)}, bf16[2,128,256]{2,1,0:T(8,128)(2,1)S(1)}, u32[]{:S(2)}, u32[]{:S(2)}) collective-permute-start(bf16[2,128,256]{2,1,0:T(8,128)(2,1)} %get-tuple-element.117), channel_id=1, source_target_pairs={{0,8},{4,12},{8,0},{12,4},{1,9},{5,13},{9,1},{13,5},{2,10},{6,14},... | collective-permute-start | bytes 393224 | tf_op jit(solution)/shard_map/ppermute | solution.py:428
  82.7 3.6 %temporal_chunk.6 = (bf16[2,2048,256]{2,1,0:T(8,128)(2,1)}, bf16[2,128,256]{2,1,0:T(8,128)(2,1)}, bf16[2,128,256]{2,1,0:T(8,128)(2,1)}, bf16[2,128,256]{2,1,0:T(8,128)(2,1)}) custom-call(bf16[4,128,256]{2,1,0:T(8,128)(2,1)S(1)} %get-tuple-element.73.refs_0_, bf16[3,128,256]{2,1,0:T(8,128)(2,1)S(1)} %get-tuple-element.86.refs_1_, ...), custom_call_target="tpu_custom_call", output_to_operand_aliasing={{0}: (14, {})} | custom-call | bytes 90000 | tf_op jit(solution)/shard_map/temporal_chunk/pallas_call | solution.py:376
  86.3 0.0 collective-permute-done.24.refs_0_
  86.4 1.7 %collective-permute-start.23 = (bf16[2,128,256]{2,1,0:T(8,128)(2,1)S(1)}, bf16[2,128,256]{2,1,0:T(8,128)(2,1)S(1)}, u32[]{:S(2)}, u32[]{:S(2)}) collective-permute-start(bf16[2,128,256]{2,1,0:T(8,128)(2,1)S(1)} %copy-done.14), channel_id=1, source_target_pairs={{0,12},{4,8},{8,4},{12,0},{1,13},{5,9},{9,5},{13,1},{2,14},{6,10},... | collective-permute-start | bytes 393224 | tf_op jit(solution)/shard_map/ppermute | solution.py:428
  88.0 0.6 collective-permute-start.18
  88.7 3.6 %temporal_chunk.7 = (bf16[2,2048,256]{2,1,0:T(8,128)(2,1)}, bf16[2,128,256]{2,1,0:T(8,128)(2,1)}, bf16[2,128,256]{2,1,0:T(8,128)(2,1)}, bf16[2,128,256]{2,1,0:T(8,128)(2,1)}) custom-call(bf16[4,128,256]{2,1,0:T(8,128)(2,1)S(1)} %get-tuple-element.73.refs_0_, bf16[3,128,256]{2,1,0:T(8,128)(2,1)S(1)} %get-tuple-element.86.refs_1_, ...), custom_call_target="tpu_custom_call", output_to_operand_aliasing={{0}: (14, {})} | custom-call | bytes 90000 | tf_op jit(solution)/shard_map/temporal_chunk/pallas_call | solution.py:376
  92.3 1.5 %collective-permute-start.15 = (bf16[2,128,256]{2,1,0:T(8,128)(2,1)}, bf16[2,128,256]{2,1,0:T(8,128)(2,1)S(1)}, u32[]{:S(2)}, u32[]{:S(2)}) collective-permute-start(bf16[2,128,256]{2,1,0:T(8,128)(2,1)} %get-tuple-element.110), channel_id=1, source_target_pairs={{0,4},{4,0},{8,12},{12,8},{1,5},{5,1},{9,13},{13,9},{2,6},{6,2},{1... | collective-permute-start | bytes 393224 | tf_op jit(solution)/shard_map/ppermute | solution.py:428
  93.8 2.0 %collective-permute-start.19 = (bf16[2,128,256]{2,1,0:T(8,128)(2,1)S(1)}, bf16[2,128,256]{2,1,0:T(8,128)(2,1)S(1)}, u32[]{:S(2)}, u32[]{:S(2)}) collective-permute-start(bf16[2,128,256]{2,1,0:T(8,128)(2,1)S(1)} %copy-done.13), channel_id=1, source_target_pairs={{0,8},{4,12},{8,0},{12,4},{1,9},{5,13},{9,1},{13,5},{2,10},{6,14},... | collective-permute-start | bytes 393224 | tf_op jit(solution)/shard_map/ppermute | solution.py:428
  95.8 1.0 collective-permute-start.20
  96.8 3.6 %collective-permute-start.16 = (bf16[2,128,256]{2,1,0:T(8,128)(2,1)}, bf16[2,128,256]{2,1,0:T(8,128)(2,1)S(1)}, u32[]{:S(2)}, u32[]{:S(2)}) collective-permute-start(bf16[2,128,256]{2,1,0:T(8,128)(2,1)} %get-tuple-element.111), channel_id=1, source_target_pairs={{0,8},{4,12},{8,0},{12,4},{1,9},{5,13},{9,1},{13,5},{2,10},{6,14},... | collective-permute-start | bytes 393224 | tf_op jit(solution)/shard_map/ppermute | solution.py:428
  100.4 2.3 %collective-permute-start.17 = (bf16[2,128,256]{2,1,0:T(8,128)(2,1)}, bf16[2,128,256]{2,1,0:T(8,128)(2,1)S(1)}, u32[]{:S(2)}, u32[]{:S(2)}) collective-permute-start(bf16[2,128,256]{2,1,0:T(8,128)(2,1)} %get-tuple-element.112), channel_id=1, source_target_pairs={{0,12},{4,8},{8,4},{12,0},{1,13},{5,9},{9,5},{13,1},{2,14},{6,10},... | collective-permute-start | bytes 393224 | tf_op jit(solution)/shard_map/ppermute | solution.py:428
  102.7 0.8 place.4.refs_3_
  103.4 0.8 place.5.refs_3_
  104.2 5.6 %collective-permute-done.19.refs_1_ = bf16[2,128,256]{2,1,0:T(8,128)(2,1)S(1)} collective-permute-done((bf16[2,128,256]{2,1,0:T(8,128)(2,1)S(1)}, bf16[2,128,256]{2,1,0:T(8,128)(2,1)S(1)}, u32[]{:S(2)}, u32[]{:S(2)}) %collective-permute-start.19) | collective-permute-done | bytes 131104 | tf_op jit(solution)/shard_map/ppermute | solution.py:428
  109.9 0.8 place.6.refs_3_
  110.6 3.9 %collective-permute-done.16.refs_1_ = bf16[2,128,256]{2,1,0:T(8,128)(2,1)S(1)} collective-permute-done((bf16[2,128,256]{2,1,0:T(8,128)(2,1)}, bf16[2,128,256]{2,1,0:T(8,128)(2,1)S(1)}, u32[]{:S(2)}, u32[]{:S(2)}) %collective-permute-start.16) | collective-permute-done | bytes 131104 | tf_op jit(solution)/shard_map/ppermute | solution.py:428
  114.6 0.8 place.7
  (38 shorter events, 0.1 us)
Async XLA Ops:
  3.0 15.2 %collective-permute-start = (bf16[4,128,256]{2,1,0:T(8,128)(2,1)}, bf16[4,128,256]{2,1,0:T(8,128)(2,1)S(1)}, u32[]{:S(2)}, u32[]{:S(2)}) collective-permute-start(bf16[4,128,256]{2,1,0:T(8,128)(2,1)} %get-tuple-element.70), channel_id=1, source_target_pairs={{0,1},{1,0},{2,3},{3,2},{4,5},{5,4},{6,7},{7,6},{8,9},{9,8},{10,11... | collective-permute-start | bytes 786440 | tf_op jit(solution)/shard_map/ppermute | solution.py:511
  3.5 14.7 %collective-permute-start.1 = (bf16[4,128,256]{2,1,0:T(8,128)(2,1)}, bf16[4,128,256]{2,1,0:T(8,128)(2,1)S(1)}, u32[]{:S(2)}, u32[]{:S(2)}) collective-permute-start(bf16[4,128,256]{2,1,0:T(8,128)(2,1)} %get-tuple-element.71), channel_id=1, source_target_pairs={{0,2},{1,3},{2,0},{3,1},{4,6},{5,7},{6,4},{7,5},{8,10},{9,11},{10,... | collective-permute-start | bytes 786440 | tf_op jit(solution)/shard_map/ppermute | solution.py:511
  6.1 12.5 %collective-permute-start.2 = (bf16[4,128,256]{2,1,0:T(8,128)(2,1)}, bf16[4,128,256]{2,1,0:T(8,128)(2,1)S(1)}, u32[]{:S(2)}, u32[]{:S(2)}) collective-permute-start(bf16[4,128,256]{2,1,0:T(8,128)(2,1)} %get-tuple-element.72), channel_id=1, source_target_pairs={{0,3},{1,2},{2,1},{3,0},{4,7},{5,6},{6,5},{7,4},{8,11},{9,10},{10,... | collective-permute-start | bytes 786440 | tf_op jit(solution)/shard_map/ppermute | solution.py:511
  15.5 3.0 %copy-start.3 = (bf16[256,256]{1,0:T(8,128)(2,1)S(1)}, bf16[256,256]{1,0:T(8,128)(2,1)}, u32[]{:S(2)}) copy-start(bf16[256,256]{1,0:T(8,128)(2,1)} %w_ref.7) | copy-start | bytes 393220
  15.5 3.0 %copy-start.11 = (s32[16]{0:T(128)S(1)}, s32[16]{0:T(128)}, u32[]{:S(2)}) copy-start(s32[16]{0:T(128)} %get-tuple-element.66.slots) | copy-start | bytes 196
  16.1 8.8 %collective-permute-start.3 = (bf16[4,128,256]{2,1,0:T(8,128)(2,1)}, bf16[4,128,256]{2,1,0:T(8,128)(2,1)S(1)}, u32[]{:S(2)}, u32[]{:S(2)}) collective-permute-start(bf16[4,128,256]{2,1,0:T(8,128)(2,1)} %get-tuple-element.83), channel_id=1, source_target_pairs={{0,1},{1,0},{2,3},{3,2},{4,5},{5,4},{6,7},{7,6},{8,9},{9,8},{10,11... | collective-permute-start | bytes 786440 | tf_op jit(solution)/shard_map/ppermute | solution.py:511
  16.3 15.0 %collective-permute-start.4 = (bf16[4,128,256]{2,1,0:T(8,128)(2,1)}, bf16[4,128,256]{2,1,0:T(8,128)(2,1)S(1)}, u32[]{:S(2)}, u32[]{:S(2)}) collective-permute-start(bf16[4,128,256]{2,1,0:T(8,128)(2,1)} %get-tuple-element.84), channel_id=1, source_target_pairs={{0,2},{1,3},{2,0},{3,1},{4,6},{5,7},{6,4},{7,5},{8,10},{9,11},{10,... | collective-permute-start | bytes 786440 | tf_op jit(solution)/shard_map/ppermute | solution.py:511
  18.2 13.1 %collective-permute-start.5 = (bf16[4,128,256]{2,1,0:T(8,128)(2,1)}, bf16[4,128,256]{2,1,0:T(8,128)(2,1)S(1)}, u32[]{:S(2)}, u32[]{:S(2)}) collective-permute-start(bf16[4,128,256]{2,1,0:T(8,128)(2,1)} %get-tuple-element.85), channel_id=1, source_target_pairs={{0,3},{1,2},{2,1},{3,0},{4,7},{5,6},{6,5},{7,4},{8,11},{9,10},{10,... | collective-permute-start | bytes 786440 | tf_op jit(solution)/shard_map/ppermute | solution.py:511
  18.6 6.4 %copy-start.4 = (bf16[256,256]{1,0:T(8,128)(2,1)S(1)}, bf16[256,256]{1,0:T(8,128)(2,1)}, u32[]{:S(2)}) copy-start(bf16[256,256]{1,0:T(8,128)(2,1)} %wq_ref.1) | copy-start | bytes 393220
  18.6 6.4 %copy-start.5 = (bf16[256,256]{1,0:T(8,128)(2,1)S(1)}, bf16[256,256]{1,0:T(8,128)(2,1)}, u32[]{:S(2)}) copy-start(bf16[256,256]{1,0:T(8,128)(2,1)} %wk_ref.1) | copy-start | bytes 393220
  18.6 6.4 %copy-start.6 = (bf16[256,256]{1,0:T(8,128)(2,1)S(1)}, bf16[256,256]{1,0:T(8,128)(2,1)}, u32[]{:S(2)}) copy-start(bf16[256,256]{1,0:T(8,128)(2,1)} %wv_ref.1) | copy-start | bytes 393220
  18.6 6.4 %copy-start.7 = (bf16[256,256]{1,0:T(8,128)(2,1)S(1)}, bf16[256,256]{1,0:T(8,128)(2,1)}, u32[]{:S(2)}) copy-start(bf16[256,256]{1,0:T(8,128)(2,1)} %wo_ref.1) | copy-start | bytes 393220
  18.6 6.4 %copy-start.10 = (bf16[8,256]{1,0:T(8,128)(2,1)S(1)}, bf16[8,256]{1,0:T(8,128)(2,1)}, u32[]{:S(2)}) copy-start(bf16[8,256]{1,0:T(8,128)(2,1)} %pos_ref.1) | copy-start | bytes 12292
  18.6 7.6 %copy-start = (bf16[2,2048,256]{2,1,0:T(8,128)(2,1)S(1)}, bf16[2,2048,256]{2,1,0:T(8,128)(2,1)}, u32[]{:S(2)}) copy-start(bf16[2,2048,256]{2,1,0:T(8,128)(2,1)} %param.12) | copy-start | bytes 6291460
  18.6 7.6 %copy-start.9 = (s32[2,64,4]{1,2,0:T(4,128)S(1)}, s32[2,64,4]{1,2,0:T(4,128)}, u32[]{:S(2)}) copy-start(s32[2,64,4]{1,2,0:T(4,128)} %param.14) | copy-start | bytes 6148
  20.6 13.5 %collective-permute-start.6 = (bf16[4,128,256]{2,1,0:T(8,128)(2,1)S(1)}, bf16[4,128,256]{2,1,0:T(8,128)(2,1)S(1)}, u32[]{:S(2)}, u32[]{:S(2)}) collective-permute-start(bf16[4,128,256]{2,1,0:T(8,128)(2,1)S(1)} %get-tuple-element.87), channel_id=1, source_target_pairs={{0,4},{4,0},{8,12},{12,8},{1,5},{5,1},{9,13},{13,9},{2,6},{6,2},{1... | collective-permute-start | bytes 786440 | tf_op jit(solution)/shard_map/ppermute | solution.py:428
  22.3 22.6 %collective-permute-start.9 = (bf16[4,128,256]{2,1,0:T(8,128)(2,1)S(1)}, bf16[4,128,256]{2,1,0:T(8,128)(2,1)S(1)}, u32[]{:S(2)}, u32[]{:S(2)}) collective-permute-start(bf16[4,128,256]{2,1,0:T(8,128)(2,1)S(1)} %get-tuple-element.96), channel_id=1, source_target_pairs={{0,8},{4,12},{8,0},{12,4},{1,9},{5,13},{9,1},{13,5},{2,10},{6,14},... | collective-permute-start | bytes 786440 | tf_op jit(solution)/shard_map/ppermute | solution.py:428
  24.9 22.5 %collective-permute-start.11 = (bf16[4,128,256]{2,1,0:T(8,128)(2,1)S(1)}, bf16[4,128,256]{2,1,0:T(8,128)(2,1)S(1)}, u32[]{:S(2)}, u32[]{:S(2)}) collective-permute-start(bf16[4,128,256]{2,1,0:T(8,128)(2,1)S(1)} %get-tuple-element.98), channel_id=1, source_target_pairs={{0,12},{4,8},{8,4},{12,0},{1,13},{5,9},{9,5},{13,1},{2,14},{6,10},... | collective-permute-start | bytes 786440 | tf_op jit(solution)/shard_map/ppermute | solution.py:428
  31.3 30.6 %copy-start.1 = (bf16[256,1024]{1,0:T(8,128)(2,1)S(1)}, bf16[256,1024]{1,0:T(8,128)(2,1)}, u32[]{:S(2)}) copy-start(bf16[256,1024]{1,0:T(8,128)(2,1)} %refs_11_.7) | copy-start | bytes 1572868
  31.3 30.6 %copy-start.2 = (bf16[1024,256]{1,0:T(8,128)(2,1)S(1)}, bf16[1024,256]{1,0:T(8,128)(2,1)}, u32[]{:S(2)}) copy-start(bf16[1024,256]{1,0:T(8,128)(2,1)} %refs_13_.7) | copy-start | bytes 1572868
  31.3 30.6 %copy-start.8 = (f32[1024]{0:T(1024)S(1)}, f32[1024]{0:T(1024)}, u32[]{:S(2)}) copy-start(f32[1024]{0:T(1024)} %param.22) | copy-start | bytes 12292
  34.6 9.6 %collective-permute-start.7 = (bf16[1,128,256]{2,1,0:T(8,128)(2,1)}, bf16[1,128,256]{2,1,0:T(8,128)(2,1)S(1)}, u32[]{:S(2)}, u32[]{:S(2)}) collective-permute-start(bf16[1,128,256]{2,1,0:T(8,128)(2,1)} %get-tuple-element.91), channel_id=1, source_target_pairs={{0,4},{4,0},{8,12},{12,8},{1,5},{5,1},{9,13},{13,9},{2,6},{6,2},{1... | collective-permute-start | bytes 196616 | tf_op jit(solution)/shard_map/ppermute | solution.py:428
  35.5 26.5 %collective-permute-start.13 = (bf16[1,128,256]{2,1,0:T(8,128)(2,1)}, bf16[1,128,256]{2,1,0:T(8,128)(2,1)S(1)}, u32[]{:S(2)}, u32[]{:S(2)}) collective-permute-start(bf16[1,128,256]{2,1,0:T(8,128)(2,1)} %get-tuple-element.104), channel_id=1, source_target_pairs={{0,8},{4,12},{8,0},{12,4},{1,9},{5,13},{9,1},{13,5},{2,10},{6,14},... | collective-permute-start | bytes 196616 | tf_op jit(solution)/shard_map/ppermute | solution.py:428
  38.9 23.0 %collective-permute-start.14 = (bf16[1,128,256]{2,1,0:T(8,128)(2,1)}, bf16[1,128,256]{2,1,0:T(8,128)(2,1)S(1)}, u32[]{:S(2)}, u32[]{:S(2)}) collective-permute-start(bf16[1,128,256]{2,1,0:T(8,128)(2,1)} %get-tuple-element.105), channel_id=1, source_target_pairs={{0,12},{4,8},{8,4},{12,0},{1,13},{5,9},{9,5},{13,1},{2,14},{6,10},... | collective-permute-start | bytes 196616 | tf_op jit(solution)/shard_map/ppermute | solution.py:428
  44.8 24.6 %collective-permute-start.8 = (bf16[3,128,256]{2,1,0:T(8,128)(2,1)}, bf16[3,128,256]{2,1,0:T(8,128)(2,1)S(1)}, u32[]{:S(2)}, u32[]{:S(2)}) collective-permute-start(bf16[3,128,256]{2,1,0:T(8,128)(2,1)} %get-tuple-element.95), channel_id=1, source_target_pairs={{0,4},{4,0},{8,12},{12,8},{1,5},{5,1},{9,13},{13,9},{2,6},{6,2},{1... | collective-permute-start | bytes 589832 | tf_op jit(solution)/shard_map/ppermute | solution.py:428
  44.9 25.9 %collective-permute-start.10 = (bf16[3,128,256]{2,1,0:T(8,128)(2,1)}, bf16[3,128,256]{2,1,0:T(8,128)(2,1)S(1)}, u32[]{:S(2)}, u32[]{:S(2)}) collective-permute-start(bf16[3,128,256]{2,1,0:T(8,128)(2,1)} %get-tuple-element.97), channel_id=1, source_target_pairs={{0,8},{4,12},{8,0},{12,4},{1,9},{5,13},{9,1},{13,5},{2,10},{6,14},... | collective-permute-start | bytes 589832 | tf_op jit(solution)/shard_map/ppermute | solution.py:428
  47.3 23.4 %collective-permute-start.12 = (bf16[3,128,256]{2,1,0:T(8,128)(2,1)}, bf16[3,128,256]{2,1,0:T(8,128)(2,1)S(1)}, u32[]{:S(2)}, u32[]{:S(2)}) collective-permute-start(bf16[3,128,256]{2,1,0:T(8,128)(2,1)} %get-tuple-element.99), channel_id=1, source_target_pairs={{0,12},{4,8},{8,4},{12,0},{1,13},{5,9},{9,5},{13,1},{2,14},{6,10},... | collective-permute-start | bytes 589832 | tf_op jit(solution)/shard_map/ppermute | solution.py:428
  66.2 20.1 %collective-permute-start.24 = (bf16[2,128,256]{2,1,0:T(8,128)(2,1)}, bf16[2,128,256]{2,1,0:T(8,128)(2,1)S(1)}, u32[]{:S(2)}, u32[]{:S(2)}) collective-permute-start(bf16[2,128,256]{2,1,0:T(8,128)(2,1)} %get-tuple-element.119), channel_id=1, source_target_pairs={{0,4},{4,0},{8,12},{12,8},{1,5},{5,1},{9,13},{13,9},{2,6},{6,2},{1... | collective-permute-start | bytes 393224 | tf_op jit(solution)/shard_map/ppermute | solution.py:428
  68.3 19.8 %collective-permute-start.25 = (bf16[2,128,256]{2,1,0:T(8,128)(2,1)}, bf16[2,128,256]{2,1,0:T(8,128)(2,1)S(1)}, u32[]{:S(2)}, u32[]{:S(2)}) collective-permute-start(bf16[2,128,256]{2,1,0:T(8,128)(2,1)} %get-tuple-element.120), channel_id=1, source_target_pairs={{0,8},{4,12},{8,0},{12,4},{1,9},{5,13},{9,1},{13,5},{2,10},{6,14},... | collective-permute-start | bytes 393224 | tf_op jit(solution)/shard_map/ppermute | solution.py:428
  69.4 23.0 %collective-permute-start.26 = (bf16[2,128,256]{2,1,0:T(8,128)(2,1)}, bf16[2,128,256]{2,1,0:T(8,128)(2,1)S(1)}, u32[]{:S(2)}, u32[]{:S(2)}) collective-permute-start(bf16[2,128,256]{2,1,0:T(8,128)(2,1)} %get-tuple-element.121), channel_id=1, source_target_pairs={{0,12},{4,8},{8,4},{12,0},{1,13},{5,9},{9,5},{13,1},{2,14},{6,10},... | collective-permute-start | bytes 393224 | tf_op jit(solution)/shard_map/ppermute | solution.py:428
  74.4 19.4 %collective-permute-start.21 = (bf16[2,128,256]{2,1,0:T(8,128)(2,1)}, bf16[2,128,256]{2,1,0:T(8,128)(2,1)S(1)}, u32[]{:S(2)}, u32[]{:S(2)}) collective-permute-start(bf16[2,128,256]{2,1,0:T(8,128)(2,1)} %get-tuple-element.116), channel_id=1, source_target_pairs={{0,4},{4,0},{8,12},{12,8},{1,5},{5,1},{9,13},{13,9},{2,6},{6,2},{1... | collective-permute-start | bytes 393224 | tf_op jit(solution)/shard_map/ppermute | solution.py:428
  80.6 15.3 %collective-permute-start.22 = (bf16[2,128,256]{2,1,0:T(8,128)(2,1)}, bf16[2,128,256]{2,1,0:T(8,128)(2,1)S(1)}, u32[]{:S(2)}, u32[]{:S(2)}) collective-permute-start(bf16[2,128,256]{2,1,0:T(8,128)(2,1)} %get-tuple-element.117), channel_id=1, source_target_pairs={{0,8},{4,12},{8,0},{12,4},{1,9},{5,13},{9,1},{13,5},{2,10},{6,14},... | collective-permute-start | bytes 393224 | tf_op jit(solution)/shard_map/ppermute | solution.py:428
  82.7 3.6 %copy-start.14 = (bf16[2,128,256]{2,1,0:T(8,128)(2,1)S(1)}, bf16[2,128,256]{2,1,0:T(8,128)(2,1)}, u32[]{:S(2)}) copy-start(bf16[2,128,256]{2,1,0:T(8,128)(2,1)} %get-tuple-element.118) | copy-start | bytes 393220
  86.4 10.4 %collective-permute-start.23 = (bf16[2,128,256]{2,1,0:T(8,128)(2,1)S(1)}, bf16[2,128,256]{2,1,0:T(8,128)(2,1)S(1)}, u32[]{:S(2)}, u32[]{:S(2)}) collective-permute-start(bf16[2,128,256]{2,1,0:T(8,128)(2,1)S(1)} %copy-done.14), channel_id=1, source_target_pairs={{0,12},{4,8},{8,4},{12,0},{1,13},{5,9},{9,5},{13,1},{2,14},{6,10},... | collective-permute-start | bytes 393224 | tf_op jit(solution)/shard_map/ppermute | solution.py:428
  88.0 12.3 %collective-permute-start.18 = (bf16[2,128,256]{2,1,0:T(8,128)(2,1)}, bf16[2,128,256]{2,1,0:T(8,128)(2,1)S(1)}, u32[]{:S(2)}, u32[]{:S(2)}) collective-permute-start(bf16[2,128,256]{2,1,0:T(8,128)(2,1)} %get-tuple-element.113), channel_id=1, source_target_pairs={{0,4},{4,0},{8,12},{12,8},{1,5},{5,1},{9,13},{13,9},{2,6},{6,2},{1... | collective-permute-start | bytes 393224 | tf_op jit(solution)/shard_map/ppermute | solution.py:428
  88.7 5.1 %copy-start.13 = (bf16[2,128,256]{2,1,0:T(8,128)(2,1)S(1)}, bf16[2,128,256]{2,1,0:T(8,128)(2,1)}, u32[]{:S(2)}) copy-start(bf16[2,128,256]{2,1,0:T(8,128)(2,1)} %get-tuple-element.114) | copy-start | bytes 393220
  88.7 7.1 %copy-start.12 = (bf16[2,128,256]{2,1,0:T(8,128)(2,1)S(1)}, bf16[2,128,256]{2,1,0:T(8,128)(2,1)}, u32[]{:S(2)}) copy-start(bf16[2,128,256]{2,1,0:T(8,128)(2,1)} %get-tuple-element.115) | copy-start | bytes 393220
  92.3 18.3 %collective-permute-start.15 = (bf16[2,128,256]{2,1,0:T(8,128)(2,1)}, bf16[2,128,256]{2,1,0:T(8,128)(2,1)S(1)}, u32[]{:S(2)}, u32[]{:S(2)}) collective-permute-start(bf16[2,128,256]{2,1,0:T(8,128)(2,1)} %get-tuple-element.110), channel_id=1, source_target_pairs={{0,4},{4,0},{8,12},{12,8},{1,5},{5,1},{9,13},{13,9},{2,6},{6,2},{1... | collective-permute-start | bytes 393224 | tf_op jit(solution)/shard_map/ppermute | solution.py:428
  93.8 16.1 %collective-permute-start.19 = (bf16[2,128,256]{2,1,0:T(8,128)(2,1)S(1)}, bf16[2,128,256]{2,1,0:T(8,128)(2,1)S(1)}, u32[]{:S(2)}, u32[]{:S(2)}) collective-permute-start(bf16[2,128,256]{2,1,0:T(8,128)(2,1)S(1)} %copy-done.13), channel_id=1, source_target_pairs={{0,8},{4,12},{8,0},{12,4},{1,9},{5,13},{9,1},{13,5},{2,10},{6,14},... | collective-permute-start | bytes 393224 | tf_op jit(solution)/shard_map/ppermute | solution.py:428
  95.8 14.0 %collective-permute-start.20 = (bf16[2,128,256]{2,1,0:T(8,128)(2,1)S(1)}, bf16[2,128,256]{2,1,0:T(8,128)(2,1)S(1)}, u32[]{:S(2)}, u32[]{:S(2)}) collective-permute-start(bf16[2,128,256]{2,1,0:T(8,128)(2,1)S(1)} %copy-done.12), channel_id=1, source_target_pairs={{0,12},{4,8},{8,4},{12,0},{1,13},{5,9},{9,5},{13,1},{2,14},{6,10},... | collective-permute-start | bytes 393224 | tf_op jit(solution)/shard_map/ppermute | solution.py:428
  96.8 17.8 %collective-permute-start.16 = (bf16[2,128,256]{2,1,0:T(8,128)(2,1)}, bf16[2,128,256]{2,1,0:T(8,128)(2,1)S(1)}, u32[]{:S(2)}, u32[]{:S(2)}) collective-permute-start(bf16[2,128,256]{2,1,0:T(8,128)(2,1)} %get-tuple-element.111), channel_id=1, source_target_pairs={{0,8},{4,12},{8,0},{12,4},{1,9},{5,13},{9,1},{13,5},{2,10},{6,14},... | collective-permute-start | bytes 393224 | tf_op jit(solution)/shard_map/ppermute | solution.py:428
  100.4 14.2 %collective-permute-start.17 = (bf16[2,128,256]{2,1,0:T(8,128)(2,1)}, bf16[2,128,256]{2,1,0:T(8,128)(2,1)S(1)}, u32[]{:S(2)}, u32[]{:S(2)}) collective-permute-start(bf16[2,128,256]{2,1,0:T(8,128)(2,1)} %get-tuple-element.112), channel_id=1, source_target_pairs={{0,12},{4,8},{8,4},{12,0},{1,13},{5,9},{9,5},{13,1},{2,14},{6,10},... | collective-permute-start | bytes 393224 | tf_op jit(solution)/shard_map/ppermute | solution.py:428

commit v6 on v5

--- a/solution.py
+++ b/solution.py
@@ -92,7 +92,7 @@
     *out, done = pl.pallas_call(
         functools.partial(gather_kernel, t, most, n_clus, direct),
         out_shape=[space(shape, BF16)] * (n_clus - 1) + [jax.ShapeDtypeStruct((1,), jnp.int32)],
-        in_specs=[smem, smem, pl.BlockSpec(memory_space=pltpu.HBM)],
+        in_specs=[pl.BlockSpec(memory_space=pl.ANY), smem, pl.BlockSpec(memory_space=pltpu.HBM)],
         out_specs=[pl.BlockSpec(memory_space=space)] * (n_clus - 1) + [smem],
         scratch_shapes=[
             pltpu.VMEM((n_clus - 1,) + (shape if not direct else (1, 16, 128)), BF16),
@@ -188,7 +188,7 @@
             pltpu.VMEM((blk_cl, nbr_k, block, block), BF16),
             jax.ShapeDtypeStruct((blk_cl,), jnp.int32),
         ],
-        in_specs=[smem, smem, hbm, hbm, vmem],
+        in_specs=[pl.BlockSpec(memory_space=pl.ANY), smem, hbm, hbm, vmem],
         out_specs=[vmem, vmem, vmem, smem],
         scratch_shapes=[
             pltpu.VMEM((blk_cl + 1, block, width), BF16),
@@ -290,7 +290,7 @@
             pltpu.VMEM((width, width), BF16),
             jax.ShapeDtypeStruct((1,), jnp.int32),
         ],
-        in_specs=[pl.BlockSpec(memory_space=pltpu.SMEM)] + [vmem] * 5,
+        in_specs=[pl.BlockSpec(memory_space=pl.ANY)] + [vmem] * 5,
         out_specs=[vmem] * 3 + [pl.BlockSpec(memory_space=pltpu.SMEM)],
         compiler_params=pltpu.CompilerParams(vmem_limit_bytes=4 << 20),
         cost_estimate=cost(1),

time: 116 us -> 116 us (level)
  no operation moved by 1% of the time
where the time goes in v6:
time: 116 us
  starting transfers between devices  44.1 us (38%)
  Pallas kernels  43 us (37%)
  waiting for transfers between devices  27.8 us (24%)
    ppermute x21, starting transfers between devices, shift(): return lax.ppermute(x, 'snap', [(i, partner(i, d, n)) for i in range(n)])  38.8 us
    ppermute x21, waiting for transfers between devices, shift(): return lax.ppermute(x, 'snap', [(i, partner(i, d, n)) for i in range(n)])  27.4 us
    pallas_call x4, Pallas kernels, temporal_chunk(): pl.pallas_call(functools.partial(temporal_kernel, n_snap, per, blocks, ch...  15.2 us
    pallas_call x2, Pallas kernels, near_sum(): pl.pallas_call(functools.partial(near_kernel, t, n_clus, most), out_shape...  10.3 us
    pallas_call x2, Pallas kernels, gather_blocks(): pl.pallas_call(functools.partial(gather_kernel, t, most, n_clus, direct),...  7.04 us
    ppermute x6, starting transfers between devices, on_device(): remote[d] = lax.ppermute(sets[t][d - 1], 'clus', pairs)  5.29 us
    pallas_call x2, Pallas kernels, far_sum(): pl.pallas_call(functools.partial(far_kernel, n_snap, parts, direct), out_...  4.67 us
    pallas_call x4, Pallas kernels, place(): pl.pallas_call(functools.partial(place_kernel, n_snap, chunk), out_shape=...  3.08 us
  transfers between devices with their start and end apart: 27, of which 5 were waited for; matrix products, arithmetic and copies ran while one was open for 0% of the time, Pallas kernels for 34%

profile of v6, /device:TPU:0, one launch (start us, length us, event | category | flops | bytes accessed | tf_op | source)
XLA Modules:
  0.0 115.5 jit_solution(15576612277420282977)
XLA Ops:
  0.0 3.0 %gather_blocks.2 = (bf16[4,128,256]{2,1,0:T(8,128)(2,1)}, bf16[4,128,256]{2,1,0:T(8,128)(2,1)}, bf16[4,128,256]{2,1,0:T(8,128)(2,1)}, s32[1]{0:T(128)}) custom-call(s32[1]{0:T(128)} %constant.0.clone.1.after_ref, s32[2,4,64]{2,1,0:T(4,128)} %bitcast.11, bf16[2,16,128,256]{3,2,1,0:T(8,128)(2,1)} %bitcast.3), custom_call_target="tpu_custom_call" | custom-call | bytes 90000 | tf_op jit(solution)/shard_map/gather_blocks/pallas_call | solution.py:92
  3.0 0.5 collective-permute-start
  3.5 2.6 %collective-permute-start.1 = (bf16[4,128,256]{2,1,0:T(8,128)(2,1)}, bf16[4,128,256]{2,1,0:T(8,128)(2,1)S(1)}, u32[]{:S(2)}, u32[]{:S(2)}) collective-permute-start(bf16[4,128,256]{2,1,0:T(8,128)(2,1)} %get-tuple-element.71), channel_id=1, source_target_pairs={{0,2},{1,3},{2,0},{3,1},{4,6},{5,7},{6,4},{7,5},{8,10},{9,11},{10,... | collective-permute-start | bytes 786440 | tf_op jit(solution)/shard_map/ppermute | solution.py:511
  6.1 0.1 collective-permute-start.2
  6.2 4.0 %gather_blocks.3 = (bf16[4,128,256]{2,1,0:T(8,128)(2,1)}, bf16[4,128,256]{2,1,0:T(8,128)(2,1)}, bf16[4,128,256]{2,1,0:T(8,128)(2,1)}, s32[1]{0:T(128)}) custom-call(s32[1]{0:T(128)} %get-tuple-element.64.after_ref, s32[2,4,64]{2,1,0:T(4,128)} %bitcast.12, bf16[2,16,128,256]{3,2,1,0:T(8,128)(2,1)} %bitcast.4), custom_call_target="tpu_custom_call" | custom-call | bytes 90000 | tf_op jit(solution)/shard_map/gather_blocks/pallas_call | solution.py:92
  10.2 5.3 %near_sum.2 = (f32[16,128,256]{2,1,0:T(8,128)S(1)}, bf16[16,128,256]{2,1,0:T(8,128)(2,1)S(1)}, bf16[16,4,128,128]{3,2,1,0:T(8,128)(2,1)S(1)}, s32[16]{0:T(128)}) custom-call(s32[1]{0:T(128)} %get-tuple-element.65.after_ref, s32[2,4,64]{2,1,0:T(4,128)} %bitcast.13, bf16[2,16,128,256]{3,2,1,0:T(8,128)(2,1)} %bitcast.5, bf16[2,16,4,128,128]{4,3,2,1,0:T(8,128)(2,1)} %adj_ref.3, ...), custom_call_target="tpu_custom_call" | custom-call | bytes 90000 | tf_op jit(solution)/shard_map/near_sum/pallas_call | solution.py:183
  15.5 0.0 copy-start.3
  15.6 0.5 gate.3
  16.1 0.2 collective-permute-start.3
  16.3 1.9 %collective-permute-start.4 = (bf16[4,128,256]{2,1,0:T(8,128)(2,1)}, bf16[4,128,256]{2,1,0:T(8,128)(2,1)S(1)}, u32[]{:S(2)}, u32[]{:S(2)}) collective-permute-start(bf16[4,128,256]{2,1,0:T(8,128)(2,1)} %get-tuple-element.84), channel_id=1, source_target_pairs={{0,2},{1,3},{2,0},{3,1},{4,6},{5,7},{6,4},{7,5},{8,10},{9,11},{10,... | collective-permute-start | bytes 786440 | tf_op jit(solution)/shard_map/ppermute | solution.py:511
  18.2 0.0 collective-permute-done.refs_0_
  18.2 0.0 collective-permute-start.5
  18.2 0.3 collective-permute-done.2.refs_2_
  18.6 0.0 copy-start.6
  18.6 0.0 copy-start.7
  18.6 0.0 copy-start.10
  18.6 0.0 copy-start
  18.6 0.0 copy-start.9
  18.6 1.9 %far_sum.2 = (bf16[4,128,256]{2,1,0:T(8,128)(2,1)S(1)}, bf16[4,128,256]{2,1,0:T(8,128)(2,1)S(1)}, bf16[4,128,256]{2,1,0:T(8,128)(2,1)S(1)}, bf16[4,128,256]{2,1,0:T(8,128)(2,1)S(1)}, s32[1]{0:T(128)}) custom-call(s32[16]{0:T(128)S(1)} %copy-done.11, f32[16,128,256]{2,1,0:T(8,128)S(1)} %get-tuple-element.67.acc_ref.refs_0_, ...), custom_call_target="tpu_custom_call" | custom-call | bytes 60000 | tf_op jit(solution)/shard_map/far_sum/pallas_call | solution.py:244
  20.6 1.7 %collective-permute-start.6 = (bf16[4,128,256]{2,1,0:T(8,128)(2,1)S(1)}, bf16[4,128,256]{2,1,0:T(8,128)(2,1)S(1)}, u32[]{:S(2)}, u32[]{:S(2)}) collective-permute-start(bf16[4,128,256]{2,1,0:T(8,128)(2,1)S(1)} %get-tuple-element.87), channel_id=1, source_target_pairs={{0,4},{4,0},{8,12},{12,8},{1,5},{5,1},{9,13},{13,9},{2,6},{6,2},{1... | collective-permute-start | bytes 786440 | tf_op jit(solution)/shard_map/ppermute | solution.py:428
  22.3 2.6 %collective-permute-start.9 = (bf16[4,128,256]{2,1,0:T(8,128)(2,1)S(1)}, bf16[4,128,256]{2,1,0:T(8,128)(2,1)S(1)}, u32[]{:S(2)}, u32[]{:S(2)}) collective-permute-start(bf16[4,128,256]{2,1,0:T(8,128)(2,1)S(1)} %get-tuple-element.96), channel_id=1, source_target_pairs={{0,8},{4,12},{8,0},{12,4},{1,9},{5,13},{9,1},{13,5},{2,10},{6,14},... | collective-permute-start | bytes 786440 | tf_op jit(solution)/shard_map/ppermute | solution.py:428
  24.9 0.1 collective-permute-start.11
  25.0 1.2 %prepare.1 = (f32[8,256]{1,0:T(8,128)S(1)}, bf16[768,256]{1,0:T(8,128)(2,1)S(1)}, bf16[256,256]{1,0:T(8,128)(2,1)S(1)}, s32[1]{0:T(128)}) custom-call(s32[1]{0:T(128)} %get-tuple-element.74.after_ref, bf16[8,256]{1,0:T(8,128)(2,1)S(1)} %copy-done.10, bf16[256,256]{1,0:T(8,128)(2,1)S(1)} %copy-done.4, bf16[256,256]{1,0:T(8,128)(2,1)S(1)} %copy-done.5, ...), custom_call_target="tpu_custom_call" | custom-call | bytes 30000 | tf_op jit(solution)/shard_map/prepare/pallas_call | solution.py:285
  26.3 5.0 %near_sum.3 = (f32[16,128,256]{2,1,0:T(8,128)S(1)}, bf16[16,128,256]{2,1,0:T(8,128)(2,1)S(1)}, bf16[16,4,128,128]{3,2,1,0:T(8,128)(2,1)S(1)}, s32[16]{0:T(128)S(1)}) custom-call(s32[1]{0:T(128)} %get-tuple-element.75.after_ref, s32[2,4,64]{2,1,0:T(4,128)S(1)} %bitcast.14, bf16[2,16,128,256]{3,2,1,0:T(8,128)(2,1)S(1)} %bitcast.6, ...), custom_call_target="tpu_custom_call" | custom-call | bytes 90000 | tf_op jit(solution)/shard_map/near_sum/pallas_call | solution.py:183
  31.3 0.0 collective-permute-done.4.refs_1_
  31.3 0.0 copy-start.1
  31.3 0.0 copy-start.2
  31.3 0.0 copy-start.8
  31.3 2.8 %far_sum.3 = (bf16[1,128,256]{2,1,0:T(8,128)(2,1)S(1)}, bf16[1,128,256]{2,1,0:T(8,128)(2,1)}, bf16[1,128,256]{2,1,0:T(8,128)(2,1)}, bf16[1,128,256]{2,1,0:T(8,12...) custom-call(s32[16]{0:T(128)S(1)} %get-tuple-element.76.slots, ...), custom_call_target="tpu_custom_call" | custom-call | bytes 60000 | tf_op jit(solution)/shard_map/far_sum/pallas_call | solution.py:244
  34.1 0.0 collective-permute-done.6.refs_0_.refs_2_
  34.1 0.5 gate.4
  34.6 0.8 collective-permute-start.7
  35.5 3.5 %collective-permute-start.13 = (bf16[1,128,256]{2,1,0:T(8,128)(2,1)}, bf16[1,128,256]{2,1,0:T(8,128)(2,1)S(1)}, u32[]{:S(2)}, u32[]{:S(2)}) collective-permute-start(bf16[1,128,256]{2,1,0:T(8,128)(2,1)} %get-tuple-element.104), channel_id=1, source_target_pairs={{0,8},{4,12},{8,0},{12,4},{1,9},{5,13},{9,1},{13,5},{2,10},{6,14},... | collective-permute-start | bytes 196616 | tf_op jit(solution)/shard_map/ppermute | solution.py:428
  38.9 0.1 collective-permute-start.14
  39.1 5.2 %collective-permute-done.7.refs_0_.refs_3_ = bf16[1,128,256]{2,1,0:T(8,128)(2,1)S(1)} collective-permute-done((bf16[1,128,256]{2,1,0:T(8,128)(2,1)}, bf16[1,128,256]{2,1,0:T(8,128)(2,1)S(1)}, u32[]{:S(2)}, u32[]{:S(2)}) %collective-permute-start.7) | collective-permute-done | bytes 65568 | tf_op jit(solution)/shard_map/ppermute | solution.py:428
  44.2 0.5 gate.5
  44.8 0.1 collective-permute-start.8
  44.9 2.5 %collective-permute-start.10 = (bf16[3,128,256]{2,1,0:T(8,128)(2,1)}, bf16[3,128,256]{2,1,0:T(8,128)(2,1)S(1)}, u32[]{:S(2)}, u32[]{:S(2)}) collective-permute-start(bf16[3,128,256]{2,1,0:T(8,128)(2,1)} %get-tuple-element.97), channel_id=1, source_target_pairs={{0,8},{4,12},{8,0},{12,4},{1,9},{5,13},{9,1},{13,5},{2,10},{6,14},... | collective-permute-start | bytes 589832 | tf_op jit(solution)/shard_map/ppermute | solution.py:428
  47.3 1.9 %collective-permute-start.12 = (bf16[3,128,256]{2,1,0:T(8,128)(2,1)}, bf16[3,128,256]{2,1,0:T(8,128)(2,1)S(1)}, u32[]{:S(2)}, u32[]{:S(2)}) collective-permute-start(bf16[3,128,256]{2,1,0:T(8,128)(2,1)} %get-tuple-element.99), channel_id=1, source_target_pairs={{0,12},{4,8},{8,4},{12,0},{1,13},{5,9},{9,5},{13,1},{2,14},{6,10},... | collective-permute-start | bytes 589832 | tf_op jit(solution)/shard_map/ppermute | solution.py:428
  49.2 12.7 %collective-permute-done.13.refs_5_ = bf16[1,128,256]{2,1,0:T(8,128)(2,1)S(1)} collective-permute-done((bf16[1,128,256]{2,1,0:T(8,128)(2,1)}, bf16[1,128,256]{2,1,0:T(8,128)(2,1)S(1)}, u32[]{:S(2)}, u32[]{:S(2)}) %collective-permute-start.13) | collective-permute-done | bytes 65568 | tf_op jit(solution)/shard_map/ppermute | solution.py:428
  61.9 4.3 %temporal_chunk.4 = (bf16[2,2048,256]{2,1,0:T(8,128)(2,1)}, bf16[2,128,256]{2,1,0:T(8,128)(2,1)}, bf16[2,128,256]{2,1,0:T(8,128)(2,1)}, bf16[2,128,256]{2,1,0:T(8,128)(2,1)}) custom-call(bf16[4,128,256]{2,1,0:T(8,128)(2,1)S(1)} %get-tuple-element.73.refs_0_, bf16[1,128,256]{2,1,0:T(8,128)(2,1)S(1)} %get-tuple-element.103.refs_1_, ...), custom_call_target="tpu_custom_call" | custom-call | bytes 90000 | tf_op jit(solution)/shard_map/temporal_chunk/pallas_call | solution.py:376
  66.2 2.0 %collective-permute-start.24 = (bf16[2,128,256]{2,1,0:T(8,128)(2,1)}, bf16[2,128,256]{2,1,0:T(8,128)(2,1)S(1)}, u32[]{:S(2)}, u32[]{:S(2)}) collective-permute-start(bf16[2,128,256]{2,1,0:T(8,128)(2,1)} %get-tuple-element.119), channel_id=1, source_target_pairs={{0,4},{4,0},{8,12},{12,8},{1,5},{5,1},{9,13},{13,9},{2,6},{6,2},{1... | collective-permute-start | bytes 393224 | tf_op jit(solution)/shard_map/ppermute | solution.py:428
  68.3 1.1 collective-permute-start.25
  69.4 1.4 %collective-permute-start.26 = (bf16[2,128,256]{2,1,0:T(8,128)(2,1)}, bf16[2,128,256]{2,1,0:T(8,128)(2,1)S(1)}, u32[]{:S(2)}, u32[]{:S(2)}) collective-permute-start(bf16[2,128,256]{2,1,0:T(8,128)(2,1)} %get-tuple-element.121), channel_id=1, source_target_pairs={{0,12},{4,8},{8,4},{12,0},{1,13},{5,9},{9,5},{13,1},{2,14},{6,10},... | collective-permute-start | bytes 393224 | tf_op jit(solution)/shard_map/ppermute | solution.py:428
  70.8 3.6 %temporal_chunk.5 = (bf16[2,2048,256]{2,1,0:T(8,128)(2,1)}, bf16[2,128,256]{2,1,0:T(8,128)(2,1)}, bf16[2,128,256]{2,1,0:T(8,128)(2,1)}, bf16[2,128,256]{2,1,0:T(8,128)(2,1)}) custom-call(bf16[4,128,256]{2,1,0:T(8,128)(2,1)S(1)} %get-tuple-element.73.refs_0_, bf16[3,128,256]{2,1,0:T(8,128)(2,1)S(1)} %get-tuple-element.86.refs_1_, ...), custom_call_target="tpu_custom_call", output_to_operand_aliasing={{0}: (14, {})} | custom-call | bytes 90000 | tf_op jit(solution)/shard_map/temporal_chunk/pallas_call | solution.py:376
  74.4 6.1 %collective-permute-start.21 = (bf16[2,128,256]{2,1,0:T(8,128)(2,1)}, bf16[2,128,256]{2,1,0:T(8,128)(2,1)S(1)}, u32[]{:S(2)}, u32[]{:S(2)}) collective-permute-start(bf16[2,128,256]{2,1,0:T(8,128)(2,1)} %get-tuple-element.116), channel_id=1, source_target_pairs={{0,4},{4,0},{8,12},{12,8},{1,5},{5,1},{9,13},{13,9},{2,6},{6,2},{1... | collective-permute-start | bytes 393224 | tf_op jit(solution)/shard_map/ppermute | solution.py:428
  80.6 2.2 %collective-permute-start.22 = (bf16[2,128,256]{2,1,0:T(8,128)(2,1)}, bf16[2,128,256]{2,1,0:T(8,128)(2,1)S(1)}, u32[]{:S(2)}, u32[]{:S(2)}) collective-permute-start(bf16[2,128,256]{2,1,0:T(8,128)(2,1)} %get-tuple-element.117), channel_id=1, source_target_pairs={{0,8},{4,12},{8,0},{12,4},{1,9},{5,13},{9,1},{13,5},{2,10},{6,14},... | collective-permute-start | bytes 393224 | tf_op jit(solution)/shard_map/ppermute | solution.py:428
  82.7 3.6 %temporal_chunk.6 = (bf16[2,2048,256]{2,1,0:T(8,128)(2,1)}, bf16[2,128,256]{2,1,0:T(8,128)(2,1)}, bf16[2,128,256]{2,1,0:T(8,128)(2,1)}, bf16[2,128,256]{2,1,0:T(8,128)(2,1)}) custom-call(bf16[4,128,256]{2,1,0:T(8,128)(2,1)S(1)} %get-tuple-element.73.refs_0_, bf16[3,128,256]{2,1,0:T(8,128)(2,1)S(1)} %get-tuple-element.86.refs_1_, ...), custom_call_target="tpu_custom_call", output_to_operand_aliasing={{0}: (14, {})} | custom-call | bytes 90000 | tf_op jit(solution)/shard_map/temporal_chunk/pallas_call | solution.py:376
  86.3 0.0 collective-permute-done.24.refs_0_
  86.4 1.7 %collective-permute-start.23 = (bf16[2,128,256]{2,1,0:T(8,128)(2,1)S(1)}, bf16[2,128,256]{2,1,0:T(8,128)(2,1)S(1)}, u32[]{:S(2)}, u32[]{:S(2)}) collective-permute-start(bf16[2,128,256]{2,1,0:T(8,128)(2,1)S(1)} %copy-done.14), channel_id=1, source_target_pairs={{0,12},{4,8},{8,4},{12,0},{1,13},{5,9},{9,5},{13,1},{2,14},{6,10},... | collective-permute-start | bytes 393224 | tf_op jit(solution)/shard_map/ppermute | solution.py:428
  88.1 0.0 collective-permute-done.25.refs_1_
  88.1 0.6 collective-permute-start.18
  88.7 3.6 %temporal_chunk.7 = (bf16[2,2048,256]{2,1,0:T(8,128)(2,1)}, bf16[2,128,256]{2,1,0:T(8,128)(2,1)}, bf16[2,128,256]{2,1,0:T(8,128)(2,1)}, bf16[2,128,256]{2,1,0:T(8,128)(2,1)}) custom-call(bf16[4,128,256]{2,1,0:T(8,128)(2,1)S(1)} %get-tuple-element.73.refs_0_, bf16[3,128,256]{2,1,0:T(8,128)(2,1)S(1)} %get-tuple-element.86.refs_1_, ...), custom_call_target="tpu_custom_call", output_to_operand_aliasing={{0}: (14, {})} | custom-call | bytes 90000 | tf_op jit(solution)/shard_map/temporal_chunk/pallas_call | solution.py:376
  92.3 1.5 %collective-permute-start.15 = (bf16[2,128,256]{2,1,0:T(8,128)(2,1)}, bf16[2,128,256]{2,1,0:T(8,128)(2,1)S(1)}, u32[]{:S(2)}, u32[]{:S(2)}) collective-permute-start(bf16[2,128,256]{2,1,0:T(8,128)(2,1)} %get-tuple-element.110), channel_id=1, source_target_pairs={{0,4},{4,0},{8,12},{12,8},{1,5},{5,1},{9,13},{13,9},{2,6},{6,2},{1... | collective-permute-start | bytes 393224 | tf_op jit(solution)/shard_map/ppermute | solution.py:428
  93.8 2.0 %collective-permute-start.19 = (bf16[2,128,256]{2,1,0:T(8,128)(2,1)S(1)}, bf16[2,128,256]{2,1,0:T(8,128)(2,1)S(1)}, u32[]{:S(2)}, u32[]{:S(2)}) collective-permute-start(bf16[2,128,256]{2,1,0:T(8,128)(2,1)S(1)} %copy-done.13), channel_id=1, source_target_pairs={{0,8},{4,12},{8,0},{12,4},{1,9},{5,13},{9,1},{13,5},{2,10},{6,14},... | collective-permute-start | bytes 393224 | tf_op jit(solution)/shard_map/ppermute | solution.py:428
  95.8 1.0 collective-permute-start.20
  96.8 3.6 %collective-permute-start.16 = (bf16[2,128,256]{2,1,0:T(8,128)(2,1)}, bf16[2,128,256]{2,1,0:T(8,128)(2,1)S(1)}, u32[]{:S(2)}, u32[]{:S(2)}) collective-permute-start(bf16[2,128,256]{2,1,0:T(8,128)(2,1)} %get-tuple-element.111), channel_id=1, source_target_pairs={{0,8},{4,12},{8,0},{12,4},{1,9},{5,13},{9,1},{13,5},{2,10},{6,14},... | collective-permute-start | bytes 393224 | tf_op jit(solution)/shard_map/ppermute | solution.py:428
  100.4 2.3 %collective-permute-start.17 = (bf16[2,128,256]{2,1,0:T(8,128)(2,1)}, bf16[2,128,256]{2,1,0:T(8,128)(2,1)S(1)}, u32[]{:S(2)}, u32[]{:S(2)}) collective-permute-start(bf16[2,128,256]{2,1,0:T(8,128)(2,1)} %get-tuple-element.112), channel_id=1, source_target_pairs={{0,12},{4,8},{8,4},{12,0},{1,13},{5,9},{9,5},{13,1},{2,14},{6,10},... | collective-permute-start | bytes 393224 | tf_op jit(solution)/shard_map/ppermute | solution.py:428
  102.7 0.8 place.4.refs_3_
  103.5 0.8 place.5.refs_3_
  104.3 5.6 %collective-permute-done.19.refs_1_ = bf16[2,128,256]{2,1,0:T(8,128)(2,1)S(1)} collective-permute-done((bf16[2,128,256]{2,1,0:T(8,128)(2,1)S(1)}, bf16[2,128,256]{2,1,0:T(8,128)(2,1)S(1)}, u32[]{:S(2)}, u32[]{:S(2)}) %collective-permute-start.19) | collective-permute-done | bytes 131104 | tf_op jit(solution)/shard_map/ppermute | solution.py:428
  109.9 0.8 place.6.refs_3_
  110.7 3.9 %collective-permute-done.16.refs_1_ = bf16[2,128,256]{2,1,0:T(8,128)(2,1)S(1)} collective-permute-done((bf16[2,128,256]{2,1,0:T(8,128)(2,1)}, bf16[2,128,256]{2,1,0:T(8,128)(2,1)S(1)}, u32[]{:S(2)}, u32[]{:S(2)}) %collective-permute-start.16) | collective-permute-done | bytes 131104 | tf_op jit(solution)/shard_map/ppermute | solution.py:428
  114.6 0.8 place.7
  (38 shorter events, 0.1 us)
Async XLA Ops:
  3.0 15.2 %collective-permute-start = (bf16[4,128,256]{2,1,0:T(8,128)(2,1)}, bf16[4,128,256]{2,1,0:T(8,128)(2,1)S(1)}, u32[]{:S(2)}, u32[]{:S(2)}) collective-permute-start(bf16[4,128,256]{2,1,0:T(8,128)(2,1)} %get-tuple-element.70), channel_id=1, source_target_pairs={{0,1},{1,0},{2,3},{3,2},{4,5},{5,4},{6,7},{7,6},{8,9},{9,8},{10,11... | collective-permute-start | bytes 786440 | tf_op jit(solution)/shard_map/ppermute | solution.py:511
  3.5 14.7 %collective-permute-start.1 = (bf16[4,128,256]{2,1,0:T(8,128)(2,1)}, bf16[4,128,256]{2,1,0:T(8,128)(2,1)S(1)}, u32[]{:S(2)}, u32[]{:S(2)}) collective-permute-start(bf16[4,128,256]{2,1,0:T(8,128)(2,1)} %get-tuple-element.71), channel_id=1, source_target_pairs={{0,2},{1,3},{2,0},{3,1},{4,6},{5,7},{6,4},{7,5},{8,10},{9,11},{10,... | collective-permute-start | bytes 786440 | tf_op jit(solution)/shard_map/ppermute | solution.py:511
  6.1 12.5 %collective-permute-start.2 = (bf16[4,128,256]{2,1,0:T(8,128)(2,1)}, bf16[4,128,256]{2,1,0:T(8,128)(2,1)S(1)}, u32[]{:S(2)}, u32[]{:S(2)}) collective-permute-start(bf16[4,128,256]{2,1,0:T(8,128)(2,1)} %get-tuple-element.72), channel_id=1, source_target_pairs={{0,3},{1,2},{2,1},{3,0},{4,7},{5,6},{6,5},{7,4},{8,11},{9,10},{10,... | collective-permute-start | bytes 786440 | tf_op jit(solution)/shard_map/ppermute | solution.py:511
  15.5 3.0 %copy-start.3 = (bf16[256,256]{1,0:T(8,128)(2,1)S(1)}, bf16[256,256]{1,0:T(8,128)(2,1)}, u32[]{:S(2)}) copy-start(bf16[256,256]{1,0:T(8,128)(2,1)} %w_ref.7) | copy-start | bytes 393220
  15.5 3.0 %copy-start.11 = (s32[16]{0:T(128)S(1)}, s32[16]{0:T(128)}, u32[]{:S(2)}) copy-start(s32[16]{0:T(128)} %get-tuple-element.66.slots) | copy-start | bytes 196
  16.1 8.8 %collective-permute-start.3 = (bf16[4,128,256]{2,1,0:T(8,128)(2,1)}, bf16[4,128,256]{2,1,0:T(8,128)(2,1)S(1)}, u32[]{:S(2)}, u32[]{:S(2)}) collective-permute-start(bf16[4,128,256]{2,1,0:T(8,128)(2,1)} %get-tuple-element.83), channel_id=1, source_target_pairs={{0,1},{1,0},{2,3},{3,2},{4,5},{5,4},{6,7},{7,6},{8,9},{9,8},{10,11... | collective-permute-start | bytes 786440 | tf_op jit(solution)/shard_map/ppermute | solution.py:511
  16.3 15.0 %collective-permute-start.4 = (bf16[4,128,256]{2,1,0:T(8,128)(2,1)}, bf16[4,128,256]{2,1,0:T(8,128)(2,1)S(1)}, u32[]{:S(2)}, u32[]{:S(2)}) collective-permute-start(bf16[4,128,256]{2,1,0:T(8,128)(2,1)} %get-tuple-element.84), channel_id=1, source_target_pairs={{0,2},{1,3},{2,0},{3,1},{4,6},{5,7},{6,4},{7,5},{8,10},{9,11},{10,... | collective-permute-start | bytes 786440 | tf_op jit(solution)/shard_map/ppermute | solution.py:511
  18.2 13.1 %collective-permute-start.5 = (bf16[4,128,256]{2,1,0:T(8,128)(2,1)}, bf16[4,128,256]{2,1,0:T(8,128)(2,1)S(1)}, u32[]{:S(2)}, u32[]{:S(2)}) collective-permute-start(bf16[4,128,256]{2,1,0:T(8,128)(2,1)} %get-tuple-element.85), channel_id=1, source_target_pairs={{0,3},{1,2},{2,1},{3,0},{4,7},{5,6},{6,5},{7,4},{8,11},{9,10},{10,... | collective-permute-start | bytes 786440 | tf_op jit(solution)/shard_map/ppermute | solution.py:511
  18.6 6.4 %copy-start.4 = (bf16[256,256]{1,0:T(8,128)(2,1)S(1)}, bf16[256,256]{1,0:T(8,128)(2,1)}, u32[]{:S(2)}) copy-start(bf16[256,256]{1,0:T(8,128)(2,1)} %wq_ref.1) | copy-start | bytes 393220
  18.6 6.4 %copy-start.5 = (bf16[256,256]{1,0:T(8,128)(2,1)S(1)}, bf16[256,256]{1,0:T(8,128)(2,1)}, u32[]{:S(2)}) copy-start(bf16[256,256]{1,0:T(8,128)(2,1)} %wk_ref.1) | copy-start | bytes 393220
  18.6 6.4 %copy-start.6 = (bf16[256,256]{1,0:T(8,128)(2,1)S(1)}, bf16[256,256]{1,0:T(8,128)(2,1)}, u32[]{:S(2)}) copy-start(bf16[256,256]{1,0:T(8,128)(2,1)} %wv_ref.1) | copy-start | bytes 393220
  18.6 6.4 %copy-start.7 = (bf16[256,256]{1,0:T(8,128)(2,1)S(1)}, bf16[256,256]{1,0:T(8,128)(2,1)}, u32[]{:S(2)}) copy-start(bf16[256,256]{1,0:T(8,128)(2,1)} %wo_ref.1) | copy-start | bytes 393220
  18.6 6.4 %copy-start.10 = (bf16[8,256]{1,0:T(8,128)(2,1)S(1)}, bf16[8,256]{1,0:T(8,128)(2,1)}, u32[]{:S(2)}) copy-start(bf16[8,256]{1,0:T(8,128)(2,1)} %pos_ref.1) | copy-start | bytes 12292
  18.6 7.6 %copy-start = (bf16[2,2048,256]{2,1,0:T(8,128)(2,1)S(1)}, bf16[2,2048,256]{2,1,0:T(8,128)(2,1)}, u32[]{:S(2)}) copy-start(bf16[2,2048,256]{2,1,0:T(8,128)(2,1)} %param.12) | copy-start | bytes 6291460
  18.6 7.6 %copy-start.9 = (s32[2,64,4]{1,2,0:T(4,128)S(1)}, s32[2,64,4]{1,2,0:T(4,128)}, u32[]{:S(2)}) copy-start(s32[2,64,4]{1,2,0:T(4,128)} %param.14) | copy-start | bytes 6148
  20.6 13.5 %collective-permute-start.6 = (bf16[4,128,256]{2,1,0:T(8,128)(2,1)S(1)}, bf16[4,128,256]{2,1,0:T(8,128)(2,1)S(1)}, u32[]{:S(2)}, u32[]{:S(2)}) collective-permute-start(bf16[4,128,256]{2,1,0:T(8,128)(2,1)S(1)} %get-tuple-element.87), channel_id=1, source_target_pairs={{0,4},{4,0},{8,12},{12,8},{1,5},{5,1},{9,13},{13,9},{2,6},{6,2},{1... | collective-permute-start | bytes 786440 | tf_op jit(solution)/shard_map/ppermute | solution.py:428
  22.3 22.6 %collective-permute-start.9 = (bf16[4,128,256]{2,1,0:T(8,128)(2,1)S(1)}, bf16[4,128,256]{2,1,0:T(8,128)(2,1)S(1)}, u32[]{:S(2)}, u32[]{:S(2)}) collective-permute-start(bf16[4,128,256]{2,1,0:T(8,128)(2,1)S(1)} %get-tuple-element.96), channel_id=1, source_target_pairs={{0,8},{4,12},{8,0},{12,4},{1,9},{5,13},{9,1},{13,5},{2,10},{6,14},... | collective-permute-start | bytes 786440 | tf_op jit(solution)/shard_map/ppermute | solution.py:428
  24.9 22.5 %collective-permute-start.11 = (bf16[4,128,256]{2,1,0:T(8,128)(2,1)S(1)}, bf16[4,128,256]{2,1,0:T(8,128)(2,1)S(1)}, u32[]{:S(2)}, u32[]{:S(2)}) collective-permute-start(bf16[4,128,256]{2,1,0:T(8,128)(2,1)S(1)} %get-tuple-element.98), channel_id=1, source_target_pairs={{0,12},{4,8},{8,4},{12,0},{1,13},{5,9},{9,5},{13,1},{2,14},{6,10},... | collective-permute-start | bytes 786440 | tf_op jit(solution)/shard_map/ppermute | solution.py:428
  31.3 30.6 %copy-start.1 = (bf16[256,1024]{1,0:T(8,128)(2,1)S(1)}, bf16[256,1024]{1,0:T(8,128)(2,1)}, u32[]{:S(2)}) copy-start(bf16[256,1024]{1,0:T(8,128)(2,1)} %refs_11_.7) | copy-start | bytes 1572868
  31.3 30.6 %copy-start.2 = (bf16[1024,256]{1,0:T(8,128)(2,1)S(1)}, bf16[1024,256]{1,0:T(8,128)(2,1)}, u32[]{:S(2)}) copy-start(bf16[1024,256]{1,0:T(8,128)(2,1)} %refs_13_.7) | copy-start | bytes 1572868
  31.3 30.6 %copy-start.8 = (f32[1024]{0:T(1024)S(1)}, f32[1024]{0:T(1024)}, u32[]{:S(2)}) copy-start(f32[1024]{0:T(1024)} %param.22) | copy-start | bytes 12292
  34.6 9.6 %collective-permute-start.7 = (bf16[1,128,256]{2,1,0:T(8,128)(2,1)}, bf16[1,128,256]{2,1,0:T(8,128)(2,1)S(1)}, u32[]{:S(2)}, u32[]{:S(2)}) collective-permute-start(bf16[1,128,256]{2,1,0:T(8,128)(2,1)} %get-tuple-element.91), channel_id=1, source_target_pairs={{0,4},{4,0},{8,12},{12,8},{1,5},{5,1},{9,13},{13,9},{2,6},{6,2},{1... | collective-permute-start | bytes 196616 | tf_op jit(solution)/shard_map/ppermute | solution.py:428
  35.5 26.5 %collective-permute-start.13 = (bf16[1,128,256]{2,1,0:T(8,128)(2,1)}, bf16[1,128,256]{2,1,0:T(8,128)(2,1)S(1)}, u32[]{:S(2)}, u32[]{:S(2)}) collective-permute-start(bf16[1,128,256]{2,1,0:T(8,128)(2,1)} %get-tuple-element.104), channel_id=1, source_target_pairs={{0,8},{4,12},{8,0},{12,4},{1,9},{5,13},{9,1},{13,5},{2,10},{6,14},... | collective-permute-start | bytes 196616 | tf_op jit(solution)/shard_map/ppermute | solution.py:428
  38.9 23.0 %collective-permute-start.14 = (bf16[1,128,256]{2,1,0:T(8,128)(2,1)}, bf16[1,128,256]{2,1,0:T(8,128)(2,1)S(1)}, u32[]{:S(2)}, u32[]{:S(2)}) collective-permute-start(bf16[1,128,256]{2,1,0:T(8,128)(2,1)} %get-tuple-element.105), channel_id=1, source_target_pairs={{0,12},{4,8},{8,4},{12,0},{1,13},{5,9},{9,5},{13,1},{2,14},{6,10},... | collective-permute-start | bytes 196616 | tf_op jit(solution)/shard_map/ppermute | solution.py:428
  44.8 24.6 %collective-permute-start.8 = (bf16[3,128,256]{2,1,0:T(8,128)(2,1)}, bf16[3,128,256]{2,1,0:T(8,128)(2,1)S(1)}, u32[]{:S(2)}, u32[]{:S(2)}) collective-permute-start(bf16[3,128,256]{2,1,0:T(8,128)(2,1)} %get-tuple-element.95), channel_id=1, source_target_pairs={{0,4},{4,0},{8,12},{12,8},{1,5},{5,1},{9,13},{13,9},{2,6},{6,2},{1... | collective-permute-start | bytes 589832 | tf_op jit(solution)/shard_map/ppermute | solution.py:428
  44.9 25.9 %collective-permute-start.10 = (bf16[3,128,256]{2,1,0:T(8,128)(2,1)}, bf16[3,128,256]{2,1,0:T(8,128)(2,1)S(1)}, u32[]{:S(2)}, u32[]{:S(2)}) collective-permute-start(bf16[3,128,256]{2,1,0:T(8,128)(2,1)} %get-tuple-element.97), channel_id=1, source_target_pairs={{0,8},{4,12},{8,0},{12,4},{1,9},{5,13},{9,1},{13,5},{2,10},{6,14},... | collective-permute-start | bytes 589832 | tf_op jit(solution)/shard_map/ppermute | solution.py:428
  47.3 23.4 %collective-permute-start.12 = (bf16[3,128,256]{2,1,0:T(8,128)(2,1)}, bf16[3,128,256]{2,1,0:T(8,128)(2,1)S(1)}, u32[]{:S(2)}, u32[]{:S(2)}) collective-permute-start(bf16[3,128,256]{2,1,0:T(8,128)(2,1)} %get-tuple-element.99), channel_id=1, source_target_pairs={{0,12},{4,8},{8,4},{12,0},{1,13},{5,9},{9,5},{13,1},{2,14},{6,10},... | collective-permute-start | bytes 589832 | tf_op jit(solution)/shard_map/ppermute | solution.py:428
  66.2 20.1 %collective-permute-start.24 = (bf16[2,128,256]{2,1,0:T(8,128)(2,1)}, bf16[2,128,256]{2,1,0:T(8,128)(2,1)S(1)}, u32[]{:S(2)}, u32[]{:S(2)}) collective-permute-start(bf16[2,128,256]{2,1,0:T(8,128)(2,1)} %get-tuple-element.119), channel_id=1, source_target_pairs={{0,4},{4,0},{8,12},{12,8},{1,5},{5,1},{9,13},{13,9},{2,6},{6,2},{1... | collective-permute-start | bytes 393224 | tf_op jit(solution)/shard_map/ppermute | solution.py:428
  68.3 19.8 %collective-permute-start.25 = (bf16[2,128,256]{2,1,0:T(8,128)(2,1)}, bf16[2,128,256]{2,1,0:T(8,128)(2,1)S(1)}, u32[]{:S(2)}, u32[]{:S(2)}) collective-permute-start(bf16[2,128,256]{2,1,0:T(8,128)(2,1)} %get-tuple-element.120), channel_id=1, source_target_pairs={{0,8},{4,12},{8,0},{12,4},{1,9},{5,13},{9,1},{13,5},{2,10},{6,14},... | collective-permute-start | bytes 393224 | tf_op jit(solution)/shard_map/ppermute | solution.py:428
  69.4 23.0 %collective-permute-start.26 = (bf16[2,128,256]{2,1,0:T(8,128)(2,1)}, bf16[2,128,256]{2,1,0:T(8,128)(2,1)S(1)}, u32[]{:S(2)}, u32[]{:S(2)}) collective-permute-start(bf16[2,128,256]{2,1,0:T(8,128)(2,1)} %get-tuple-element.121), channel_id=1, source_target_pairs={{0,12},{4,8},{8,4},{12,0},{1,13},{5,9},{9,5},{13,1},{2,14},{6,10},... | collective-permute-start | bytes 393224 | tf_op jit(solution)/shard_map/ppermute | solution.py:428
  74.4 19.4 %collective-permute-start.21 = (bf16[2,128,256]{2,1,0:T(8,128)(2,1)}, bf16[2,128,256]{2,1,0:T(8,128)(2,1)S(1)}, u32[]{:S(2)}, u32[]{:S(2)}) collective-permute-start(bf16[2,128,256]{2,1,0:T(8,128)(2,1)} %get-tuple-element.116), channel_id=1, source_target_pairs={{0,4},{4,0},{8,12},{12,8},{1,5},{5,1},{9,13},{13,9},{2,6},{6,2},{1... | collective-permute-start | bytes 393224 | tf_op jit(solution)/shard_map/ppermute | solution.py:428
  80.6 15.3 %collective-permute-start.22 = (bf16[2,128,256]{2,1,0:T(8,128)(2,1)}, bf16[2,128,256]{2,1,0:T(8,128)(2,1)S(1)}, u32[]{:S(2)}, u32[]{:S(2)}) collective-permute-start(bf16[2,128,256]{2,1,0:T(8,128)(2,1)} %get-tuple-element.117), channel_id=1, source_target_pairs={{0,8},{4,12},{8,0},{12,4},{1,9},{5,13},{9,1},{13,5},{2,10},{6,14},... | collective-permute-start | bytes 393224 | tf_op jit(solution)/shard_map/ppermute | solution.py:428
  82.7 3.6 %copy-start.14 = (bf16[2,128,256]{2,1,0:T(8,128)(2,1)S(1)}, bf16[2,128,256]{2,1,0:T(8,128)(2,1)}, u32[]{:S(2)}) copy-start(bf16[2,128,256]{2,1,0:T(8,128)(2,1)} %get-tuple-element.118) | copy-start | bytes 393220
  86.4 10.4 %collective-permute-start.23 = (bf16[2,128,256]{2,1,0:T(8,128)(2,1)S(1)}, bf16[2,128,256]{2,1,0:T(8,128)(2,1)S(1)}, u32[]{:S(2)}, u32[]{:S(2)}) collective-permute-start(bf16[2,128,256]{2,1,0:T(8,128)(2,1)S(1)} %copy-done.14), channel_id=1, source_target_pairs={{0,12},{4,8},{8,4},{12,0},{1,13},{5,9},{9,5},{13,1},{2,14},{6,10},... | collective-permute-start | bytes 393224 | tf_op jit(solution)/shard_map/ppermute | solution.py:428
  88.1 12.3 %collective-permute-start.18 = (bf16[2,128,256]{2,1,0:T(8,128)(2,1)}, bf16[2,128,256]{2,1,0:T(8,128)(2,1)S(1)}, u32[]{:S(2)}, u32[]{:S(2)}) collective-permute-start(bf16[2,128,256]{2,1,0:T(8,128)(2,1)} %get-tuple-element.113), channel_id=1, source_target_pairs={{0,4},{4,0},{8,12},{12,8},{1,5},{5,1},{9,13},{13,9},{2,6},{6,2},{1... | collective-permute-start | bytes 393224 | tf_op jit(solution)/shard_map/ppermute | solution.py:428
  88.7 5.1 %copy-start.13 = (bf16[2,128,256]{2,1,0:T(8,128)(2,1)S(1)}, bf16[2,128,256]{2,1,0:T(8,128)(2,1)}, u32[]{:S(2)}) copy-start(bf16[2,128,256]{2,1,0:T(8,128)(2,1)} %get-tuple-element.114) | copy-start | bytes 393220
  88.7 7.1 %copy-start.12 = (bf16[2,128,256]{2,1,0:T(8,128)(2,1)S(1)}, bf16[2,128,256]{2,1,0:T(8,128)(2,1)}, u32[]{:S(2)}) copy-start(bf16[2,128,256]{2,1,0:T(8,128)(2,1)} %get-tuple-element.115) | copy-start | bytes 393220
  92.3 18.3 %collective-permute-start.15 = (bf16[2,128,256]{2,1,0:T(8,128)(2,1)}, bf16[2,128,256]{2,1,0:T(8,128)(2,1)S(1)}, u32[]{:S(2)}, u32[]{:S(2)}) collective-permute-start(bf16[2,128,256]{2,1,0:T(8,128)(2,1)} %get-tuple-element.110), channel_id=1, source_target_pairs={{0,4},{4,0},{8,12},{12,8},{1,5},{5,1},{9,13},{13,9},{2,6},{6,2},{1... | collective-permute-start | bytes 393224 | tf_op jit(solution)/shard_map/ppermute | solution.py:428
  93.8 16.0 %collective-permute-start.19 = (bf16[2,128,256]{2,1,0:T(8,128)(2,1)S(1)}, bf16[2,128,256]{2,1,0:T(8,128)(2,1)S(1)}, u32[]{:S(2)}, u32[]{:S(2)}) collective-permute-start(bf16[2,128,256]{2,1,0:T(8,128)(2,1)S(1)} %copy-done.13), channel_id=1, source_target_pairs={{0,8},{4,12},{8,0},{12,4},{1,9},{5,13},{9,1},{13,5},{2,10},{6,14},... | collective-permute-start | bytes 393224 | tf_op jit(solution)/shard_map/ppermute | solution.py:428
  95.8 14.0 %collective-permute-start.20 = (bf16[2,128,256]{2,1,0:T(8,128)(2,1)S(1)}, bf16[2,128,256]{2,1,0:T(8,128)(2,1)S(1)}, u32[]{:S(2)}, u32[]{:S(2)}) collective-permute-start(bf16[2,128,256]{2,1,0:T(8,128)(2,1)S(1)} %copy-done.12), channel_id=1, source_target_pairs={{0,12},{4,8},{8,4},{12,0},{1,13},{5,9},{9,5},{13,1},{2,14},{6,10},... | collective-permute-start | bytes 393224 | tf_op jit(solution)/shard_map/ppermute | solution.py:428
  96.8 17.8 %collective-permute-start.16 = (bf16[2,128,256]{2,1,0:T(8,128)(2,1)}, bf16[2,128,256]{2,1,0:T(8,128)(2,1)S(1)}, u32[]{:S(2)}, u32[]{:S(2)}) collective-permute-start(bf16[2,128,256]{2,1,0:T(8,128)(2,1)} %get-tuple-element.111), channel_id=1, source_target_pairs={{0,8},{4,12},{8,0},{12,4},{1,9},{5,13},{9,1},{13,5},{2,10},{6,14},... | collective-permute-start | bytes 393224 | tf_op jit(solution)/shard_map/ppermute | solution.py:428
  100.4 14.2 %collective-permute-start.17 = (bf16[2,128,256]{2,1,0:T(8,128)(2,1)}, bf16[2,128,256]{2,1,0:T(8,128)(2,1)S(1)}, u32[]{:S(2)}, u32[]{:S(2)}) collective-permute-start(bf16[2,128,256]{2,1,0:T(8,128)(2,1)} %get-tuple-element.112), channel_id=1, source_target_pairs={{0,12},{4,8},{8,4},{12,0},{1,13},{5,9},{9,5},{13,1},{2,14},{6,10},... | collective-permute-start | bytes 393224 | tf_op jit(solution)/shard_map/ppermute | solution.py:428
